TPU v7x, 512 devices: a whole 4x8x8 slice. The times are simulated.
512 devices in a mesh: gx: 8 (over y), gy: 64 (over z, x, core).
Axes of the slice: x: 4, y: 8, z: 8, core: 2. Of those that a mesh axis runs over, the one named last changes fastest.
Arguments:
- source: float32 [256, 16384], P('gx', 'gy'), may hold values from -6 to 6
- potential: float32 [256, 16384], P('gx', 'gy'), may hold values from -1.5 to 1.5
- mobility_along: float32 [256, 16384], P('gx', 'gy'), may hold values from 0.3 to 3
- mobility_across: float32 [256, 16384], P('gx', 'gy'), may hold values from 0.3 to 3
- recombination: float32 [256, 16384], P('gx', 'gy'), may hold values from 0.002 to 0.05
- counts: int32 [8, 64], P('gx', 'gy'), may hold values from 8 to 32, as said below
- basis: float32 [256, 1179648], P('gx', 'gy'), may hold values from -1 to 1
- coarse_inverse: float32 [16384, 16384], P(('gx', 'gy')), may hold values from -8 to 8
Outputs:
- solution: float32 [256, 16384], P('gx', 'gy')
- residual: float32 [256, 16384], P('gx', 'gy')
Inputs may be any that keep to these rules, and one draw needn't show every extreme that they name: `counts`: the number of a subdomain's rows of basis that are in use.
All inputs are finite; a program needn't handle non-finite values.
Results may differ from a plain program's by a relative error of at most 0.003.
Values sent between devices are 32-bit elements; how exact they have to be, the bound alone decides.
No kernel may reach another device: no remote copies, remote signals or barrier semaphores. Data moves between devices by JAX's collectives and lax.ppermute only.
A program may use at most 64 MiB of HBM per device.

v0:
```python
import jax
import jax.numpy as jnp
from jax import lax
from jax.sharding import PartitionSpec as P

OV = 16
SWEEPS = 8


OMEGA = 0.8
EPSILON = 1e-06
HIGHEST_PRECISION = lax.Precision.HIGHEST


def padded(cells, sides, width):
    for axis, dim in sides:
        count = lax.axis_size(axis)
        ends = count - 1
        head = lax.slice_in_dim(cells, 0, width, axis=dim)
        tail = lax.slice_in_dim(cells, cells.shape[dim] - width, cells.shape[dim], axis=dim)
        cells = jnp.concatenate(
            [
                lax.ppermute(tail, axis, [(i, (i + 1) % count) for i in range(ends)]),
                cells,
                lax.ppermute(head, axis, [((i + 1) % count, i) for i in range(ends)]),
            ],
            axis=dim,
        )
    return cells


def face_weights(potential, mobility_along, mobility_across):
    along_first = jnp.sqrt(mobility_along[:-1, :] * mobility_along[1:, :])
    along_second = jnp.sqrt(mobility_across[:, :-1] * mobility_across[:, 1:])
    rise_first = potential[1:, :] - potential[:-1, :]
    rise_second = potential[:, 1:] - potential[:, :-1]
    downward = along_first * jnp.exp(0.5 * rise_first)
    upward = along_first * jnp.exp(-0.5 * rise_first)
    eastward = along_second * jnp.exp(0.5 * rise_second)
    westward = along_second * jnp.exp(-0.5 * rise_second)
    return (downward, upward, eastward, westward)


def build(potential, mobility_along, mobility_across, recombination):
    downward, upward, eastward, westward = face_weights(potential, mobility_along, mobility_across)
    diagonal = (
        recombination + jnp.pad(upward, ((0, 1), (0, 0))) + jnp.pad(downward, ((1, 0), (0, 0)))
    )
    diagonal = diagonal + jnp.pad(westward, ((0, 0), (0, 1))) + jnp.pad(eastward, ((0, 0), (1, 0)))
    return (diagonal, (downward, upward, eastward, westward))


def coupled(field, faces):
    downward, upward, eastward, westward = faces
    total = jnp.pad(downward * field[1:, :], ((0, 1), (0, 0)))
    total = total + jnp.pad(upward * field[:-1, :], ((1, 0), (0, 0)))
    total = total + jnp.pad(eastward * field[:, 1:], ((0, 0), (0, 1)))
    total = total + jnp.pad(westward * field[:, :-1], ((0, 0), (1, 0)))
    return total


def smooth(vector_patch, diagonal, faces):
    field = jnp.zeros_like(vector_patch)
    for sweep in range(SWEEPS):
        field = (
            field + OMEGA * (vector_patch - (diagonal * field - coupled(field, faces))) / diagonal
        )
    return field


def least_squares(
    source_norm, first_first, second_first, first_second, second_second, third_second
):
    radius = jnp.sqrt(first_first * first_first + second_first * second_first)
    cosine = first_first / radius
    sine = second_first / radius
    upper_right = cosine * first_second + sine * second_second
    lower_right = cosine * second_second - sine * first_second
    radius_two = jnp.sqrt(lower_right * lower_right + third_second * third_second)
    weight_two = lower_right / radius_two * (-sine * source_norm) / radius_two
    weight_one = (cosine * source_norm - upper_right * weight_two) / radius
    remainder_one = source_norm - first_first * weight_one - first_second * weight_two
    remainder_two = -second_first * weight_one - second_second * weight_two
    remainder_three = -third_second * weight_two
    return (weight_one, weight_two, remainder_one, remainder_two, remainder_three)


def extend(stacked):
    return padded(stacked, (("gx", 1), ("gy", 2)), OV)


def totals(values):
    return lax.psum(values, ("gx", "gy"))


def fold(part):
    edges = jnp.concatenate([part[:OV], part[-OV:]], axis=0)
    arrived = padded(edges, (("gx", 0),), OV)
    middle = part[OV:-OV]
    middle = middle.at[:OV].add(arrived[:OV])
    middle = middle.at[-OV:].add(arrived[-OV:])
    sides = jnp.concatenate([middle[:, :OV], middle[:, -OV:]], axis=1)
    arrived = padded(sides, (("gy", 1),), OV)
    inner = middle[:, OV:-OV]
    inner = inner.at[:, :OV].add(arrived[:, :OV])
    inner = inner.at[:, -OV:].add(arrived[:, -OV:])
    return inner


def on_device(
    source, potential, mobility_along, mobility_across, recombination, counts, basis, coarse_inverse
):
    height, breadth = source.shape
    vectors = basis.shape[0]
    grown = extend(jnp.stack([source, potential, mobility_along, mobility_across, recombination]))
    source_patch = grown[0]
    diagonal, faces = build(grown[1], grown[2], grown[3], grown[4])
    row_place = (
        lax.axis_index("gx") * height - OV + lax.broadcasted_iota(jnp.int32, source_patch.shape, 0)
    )
    column_place = (
        lax.axis_index("gy") * breadth - OV + lax.broadcasted_iota(jnp.int32, source_patch.shape, 1)
    )
    inside = (
        (row_place >= 0)
        & (row_place < height * lax.axis_size("gx"))
        & (column_place >= 0)
        & (column_place < breadth * lax.axis_size("gy"))
    ).astype(jnp.float32)
    smooth_diagonal = diagonal + (1.0 - inside)
    window = grown[1:, OV - 1 : OV + height + 1, OV - 1 : OV + breadth + 1]
    window_diagonal, window_faces = build(window[0], window[1], window[2], window[3])
    count = counts[0, 0]
    live = (lax.broadcasted_iota(jnp.int32, (vectors,), 0) < count).astype(jnp.float32)

    def apply(window_vector):
        return (window_diagonal * window_vector - coupled(window_vector, window_faces))[1:-1, 1:-1]

    def operator_input(vector):
        return extend(vector[None])[0][OV - 1 : OV + height + 1, OV - 1 : OV + breadth + 1]

    def accumulate(piece):
        return jnp.dot(coarse_inverse, piece, precision=HIGHEST_PRECISION)

    def precondition(vector_patch):
        solved = smooth(vector_patch, smooth_diagonal, faces)[OV : OV + height, OV : OV + breadth]
        flattened = vector_patch.reshape(-1)
        restricted = jnp.dot(basis, flattened, precision=HIGHEST_PRECISION) * live
        coarse = accumulate(lax.all_gather(restricted, ("gx", "gy"), axis=0, tiled=True)) * live
        spread = jnp.dot(coarse, basis, precision=HIGHEST_PRECISION)
        return solved + fold(spread.reshape(vector_patch.shape))

    source_norm = jnp.sqrt(totals(jnp.stack([jnp.sum(source * source)]))[0] + EPSILON)
    first = source / source_norm
    first_dir = precondition(source_patch / source_norm)
    image = apply(operator_input(first_dir))
    first_first = totals(jnp.stack([jnp.sum(first * image)]))[0]
    image = image - first_first * first
    second_first = jnp.sqrt(totals(jnp.stack([jnp.sum(image * image)]))[0] + EPSILON)
    second = image / second_first
    second_dir = precondition(extend(second[None])[0])
    image = apply(operator_input(second_dir))
    sums = totals(jnp.stack([jnp.sum(first * image), jnp.sum(second * image)]))
    first_second = sums[0]
    second_second = sums[1]
    image = image - first_second * first - second_second * second
    third_second = jnp.sqrt(totals(jnp.stack([jnp.sum(image * image)]))[0] + EPSILON)
    third = image / third_second
    weight_one, weight_two, remainder_one, remainder_two, remainder_three = least_squares(
        source_norm, first_first, second_first, first_second, second_second, third_second
    )
    solution = weight_one * first_dir + weight_two * second_dir
    residual = remainder_one * first + remainder_two * second + remainder_three * third
    return (solution, residual)


def solution(mesh):
    placed = (
        P("gx", "gy"),
        P("gx", "gy"),
        P("gx", "gy"),
        P("gx", "gy"),
        P("gx", "gy"),
        P("gx", "gy"),
        P("gx", "gy"),
        P(("gx", "gy"), None),
    )
    return jax.shard_map(
        on_device,
        mesh=mesh,
        in_specs=placed,
        out_specs=(P("gx", "gy"), P("gx", "gy")),
        check_vma=False,
    )
```

profile of v0, /device:TPU:1, one launch (start us, length us, event | category | flops | bytes accessed | tf_op | source)
XLA Modules:
  0.0 1194.1 jit_solution(2397084876444644998)
XLA Ops:
  11.2 4.0 collective-permute-start
  15.2 1.3 collective-permute-start.1
  16.5 1.4 multiply_reduce_fusion.5
  17.9 2.5 collective-permute-done.1
  20.6 5.1 collective-permute-start.2
  25.7 3.4 collective-permute-start.3
  29.1 103.7 %psum.35 = f32[1]{0:T(128)} all-reduce(f32[1]{0:T(128)} %bitcast), channel_id=1, replica_groups=mesh['gx'=8,'gy'=64] {'gx','gy'}, use_global_device_ids=true, to_apply=%region_1.2 | all-reduce | flops 1 | bytes 8 | tf_op jit(solution)/shard_map/psum | solution.py:93
  138.9 2.8 fusion.5
  142.3 1.4 dynamic-update-slice.24
  146.3 253.9 %all-reduce.81.cloned.1.call-done = f32[16384]{0:T(1024)} async-done(((f32[16384]{0:T(1024)}), f32[16384]{0:T(1024)}) %all-reduce.81.cloned.1.call-update) | async-done | bytes 65552
  400.3 3.4 fusion.4
  403.7 1.9 fusion.52
  405.5 1.4 fusion.42
  407.0 1.4 slice.692
  408.4 3.6 collective-permute-start.4
  412.7 1.4 slice.828
  414.1 1.4 reshape.306
  415.5 1.5 slice.689
  417.0 1.4 slice.695
  419.7 1.4 add_dynamic-update-slice_fusion.1
  421.1 2.1 collective-permute-done.5
  423.2 1.3 fusion.32
  424.5 1.3 fusion.47
  425.9 3.8 collective-permute-start.6
  429.7 1.6 pad_add_fusion.1
  431.4 1.5 slice.833
  432.8 1.9 collective-permute-start.7
  434.8 1.3 add_select_fusion.1
  436.1 1.4 scatter-add.30
  439.0 1.4 scatter-add.31
  441.4 1.6 collective-permute-start.8
  443.0 1.3 collective-permute-start.9
  444.3 3.2 collective-permute-done.9
  447.6 4.3 collective-permute-start.10
  451.9 1.9 collective-permute-start.11
  454.0 3.2 collective-permute-done.11
  458.6 99.3 %psum.36 = f32[]{:T(128)} all-reduce(f32[]{:T(128)} %get-tuple-element.103), channel_id=1, replica_groups=mesh['gx'=8,'gy'=64] {'gx','gy'}, use_global_device_ids=true, to_apply=%region_4.5 | all-reduce | flops 1 | bytes 8 | tf_op jit(solution)/shard_map/psum | solution.py:93
  557.9 1.3 multiply_reduce_fusion.3
  559.2 95.2 %psum.37 = f32[1]{0:T(128)} all-reduce(f32[1]{0:T(128)} %bitcast.26), channel_id=1, replica_groups=mesh['gx'=8,'gy'=64] {'gx','gy'}, use_global_device_ids=true, to_apply=%region_6.7 | all-reduce | flops 1 | bytes 8 | tf_op jit(solution)/shard_map/psum | solution.py:93
  655.8 2.6 collective-permute-start.12
  658.4 1.3 collective-permute-start.13
  659.7 3.3 collective-permute-done.13
  663.1 5.5 collective-permute-start.14
  668.6 2.1 collective-permute-start.15
  670.7 3.1 collective-permute-done.15
  677.9 1.9 fusion.2
  682.5 257.4 %all-reduce.83.cloned.1.call-done = f32[16384]{0:T(1024)} async-done(((f32[16384]{0:T(1024)}), f32[16384]{0:T(1024)}) %all-reduce.83.cloned.1.call-update) | async-done | bytes 65552
  939.8 3.4 fusion.1
  945.2 3.6 collective-permute-start.16
  949.8 1.3 collective-permute-start.17
  951.8 2.5 collective-permute-done.17
  954.4 3.8 collective-permute-start.18
  959.4 1.9 collective-permute-start.19
  962.2 2.2 collective-permute-done.19
  964.9 1.6 collective-permute-start.20
  966.5 1.3 collective-permute-start.21
  967.8 3.2 collective-permute-done.21
  971.1 3.3 collective-permute-start.22
  974.5 1.9 collective-permute-start.23
  980.1 1.4 multiply_reduce_fusion.2
  982.8 98.7 %psum.38 = f32[2]{0:T(128)S(1)} all-reduce(f32[2]{0:T(128)S(1)} %pad_maximum_fusion.6), channel_id=1, replica_groups=mesh['gx'=8,'gy'=64] {'gx','gy'}, use_global_device_ids=true, to_apply=%region_9.10 | all-reduce | flops 2 | bytes 16 | tf_op jit(solution)/shard_map/psum | solution.py:93
  1084.3 2.4 multiply_reduce_fusion
  1086.7 94.8 %psum.39 = f32[1]{0:T(128)} all-reduce(f32[1]{0:T(128)} %bitcast.41), channel_id=1, replica_groups=mesh['gx'=8,'gy'=64] {'gx','gy'}, use_global_device_ids=true, to_apply=%region_11.12 | all-reduce | flops 1 | bytes 8 | tf_op jit(solution)/shard_map/psum | solution.py:93
  1184.8 2.4 multiply_add_fusion
  (159 shorter events, 35.7 us)
Async XLA Ops:
  7.2 131.7 %copy-start = (f32[32,18432]{1,0:T(8,128)S(1)}, f32[32,18432]{1,0:T(8,128)}, u32[]{:S(2)}) copy-start(f32[32,18432]{1,0:T(8,128)} %param.30) | copy-start | bytes 7077892
  7.2 393.1 %all-reduce.81.cloned.1.call-start = ((), (), s32[]{:S(2)}) async-start(), calls=%async_computation | async-start | bytes 131072
  11.2 6.7 collective-permute-start
  15.2 5.2 collective-permute-start.1
  20.6 114.2 %collective-permute-start.2 = (f32[5,64,16]{2,1,0:T(8,128)S(1)}, f32[5,64,16]{2,1,0:T(8,128)S(1)}, u32[]{:S(2)}, u32[]{:S(2)}) collective-permute-start(f32[5,64,16]{2,1,0:T(8,128)S(1)} %get-tuple-element.133), channel_id=1, source_target_pairs={{0,1},{1,2},{2,3},{3,4},{4,5},{5,6},{6,7},{7,8},{8,9},{9,10},{10,1... | collective-permute-start | bytes 61448 | tf_op jit(solution)/shard_map/ppermute | solution.py:23
  25.7 109.1 %collective-permute-start.3 = (f32[5,64,16]{2,1,0:T(8,128)S(1)}, f32[5,64,16]{2,1,0:T(8,128)S(1)}, u32[]{:S(2)}, u32[]{:S(2)}) collective-permute-start(f32[5,64,16]{2,1,0:T(8,128)S(1)} %get-tuple-element.134), channel_id=1, source_target_pairs={{1,0},{2,1},{3,2},{4,3},{5,4},{6,5},{7,6},{8,7},{9,8},{10,9},{11,1... | collective-permute-start | bytes 61448 | tf_op jit(solution)/shard_map/ppermute | solution.py:25
  135.4 1.2 copy-start.5
  143.8 796.1 %all-reduce.83.cloned.1.call-start = ((), (), s32[]{:S(2)}) async-start(), calls=%async_computation.1 | async-start | bytes 131072
  145.0 0.6 copy-start.1
  400.3 11.7 copy-start.2
  408.4 11.3 collective-permute-start.4
  418.4 4.8 collective-permute-start.5
  425.9 8.9 collective-permute-start.6
  432.8 5.4 collective-permute-start.7
  440.4 17.4 %copy-start.3 = (f32[32,256]{1,0:T(8,128)S(1)}, f32[32,256]{1,0:T(8,128)}, u32[]{:S(2)}) copy-start(f32[32,256]{1,0:T(8,128)} %param.24) | copy-start | bytes 98308
  441.4 17.2 %copy-start.6 = (f32[32,256]{1,0:T(8,128)}, f32[32,256]{1,0:T(8,128)S(1)}, u32[]{:S(2)}) copy-start(f32[32,256]{1,0:T(8,128)S(1)} %fusion.29) | copy-start | bytes 98308
  441.4 116.5 %copy-start.4 = (f32[32,256]{1,0:T(8,128)S(1)}, f32[32,256]{1,0:T(8,128)}, u32[]{:S(2)}) copy-start(f32[32,256]{1,0:T(8,128)} %param.24) | copy-start | bytes 98308
  441.4 2.9 collective-permute-start.8
  443.0 4.5 collective-permute-start.9
  447.6 6.4 collective-permute-start.10
  451.9 5.2 collective-permute-start.11
  457.4 1.1 copy-start.8
  457.7 0.9 copy-start.10
  457.7 0.9 copy-start.12
  457.8 0.8 copy-start.14
  655.8 3.9 collective-permute-start.12
  658.4 4.6 collective-permute-start.13
  663.1 7.6 collective-permute-start.14
  668.6 5.2 collective-permute-start.15
  680.1 0.6 copy-start.16
  943.2 36.6 %copy-start.9 = (f32[33,258]{1,0:T(8,128)S(1)}, f32[33,258]{1,0:T(8,128)}, u32[]{:S(2)}) copy-start(f32[33,258]{1,0:T(8,128)} %copy-done.8) | copy-start | bytes 102172
  943.2 36.7 %copy-start.11 = (f32[34,257]{1,0:T(8,128)S(1)}, f32[34,257]{1,0:T(8,128)}, u32[]{:S(2)}) copy-start(f32[34,257]{1,0:T(8,128)} %copy-done.10) | copy-start | bytes 104860
  943.2 36.7 %copy-start.13 = (f32[34,257]{1,0:T(8,128)S(1)}, f32[34,257]{1,0:T(8,128)}, u32[]{:S(2)}) copy-start(f32[34,257]{1,0:T(8,128)} %copy-done.12) | copy-start | bytes 104860
  944.5 35.7 %copy-start.15 = (f32[34,258]{1,0:T(8,128)S(1)}, f32[34,258]{1,0:T(8,128)}, u32[]{:S(2)}) copy-start(f32[34,258]{1,0:T(8,128)} %copy-done.14) | copy-start | bytes 105268
  944.5 239.7 %copy-start.7 = (f32[32,256]{1,0:T(8,128)S(1)}, f32[32,256]{1,0:T(8,128)}, u32[]{:S(2)}) copy-start(f32[32,256]{1,0:T(8,128)} %copy-done.6) | copy-start | bytes 98308
  945.2 5.9 collective-permute-start.16
  949.8 4.6 collective-permute-start.17
  954.4 6.9 collective-permute-start.18
  959.4 5.1 collective-permute-start.19
  964.9 2.9 collective-permute-start.20
  966.5 4.5 collective-permute-start.21
  971.1 7.4 collective-permute-start.22
  974.5 5.2 collective-permute-start.23
Sparse Core Ops, SparseCore 0:
  143.9 256.3 all-reduce.80
  680.8 258.9 all-reduce.82
where the time goes:
time: 1200 us; the launch traced here: 1190 us
  waiting for transfers between devices  539 us (45%)
  blocking collectives  492 us (41%)
  starting transfers between devices  64 us (5%)
  other arithmetic  35.7 us (3%)
  local copies, waits for them, and re-layouts  25.6 us (2%)
  between operations  23.9 us (2%)
  matrix products  14.6 us (1%)
    unnamed x4, waiting for transfers between devices  511 us
    psum x5, blocking collectives, totals(): return lax.psum(values, ('gx', 'gy'))  492 us
    ppermute x12, starting transfers between devices, padded(): lax.ppermute(tail, axis, [(i, (i + 1) % count) for i in range(ends)])  43.1 us
    ppermute x12, waiting for transfers between devices, padded(): lax.ppermute(head, axis, [((i + 1) % count, i) for i in range(ends)])  27.2 us
  transfers between devices with their start and end apart: 26, of which 13 were waited for; matrix products, arithmetic and copies ran while one was open for 2% of the time, Pallas kernels for 0%

commit v1 on v0

v1 whole, which is shorter than its diff:
```python
import jax
import jax.numpy as jnp
from jax import lax
from jax.experimental import pallas as pl
from jax.experimental.pallas import tpu as pltpu
from jax.sharding import PartitionSpec as P

OV = 16
SWEEPS = 8
OMEGA = 0.8
EPSILON = 1e-06
CX = 32
CY = 256
K = 32
PX = CX + 2 * OV
PY = CY + 2 * OV
LW = 384
GROUPS = PX // 4
STRIP = 24
SCALARS = 96
f32 = jnp.float32
AXES = ("gx", "gy")


def lanes_of(shape):
    return lax.broadcasted_iota(jnp.int32, shape, len(shape) - 1)


def rows_of(shape):
    return lax.broadcasted_iota(jnp.int32, shape, len(shape) - 2)


def left(x):
    return pltpu.roll(x, LW - 1, 1)


def right(x):
    return pltpu.roll(x, 1, 1)


def up(x):
    return pltpu.roll(x, x.shape[0] - 1, 0)


def down(x):
    return pltpu.roll(x, 1, 0)


def own_mask(shape, first):
    rows, lanes = rows_of(shape) + first, lanes_of(shape)
    return (rows >= OV) & (rows < OV + CX) & (lanes >= OV) & (lanes < OV + CY)


def total(x):
    return jnp.sum(jnp.sum(x, axis=0, keepdims=True), axis=1, keepdims=True)


def to_row(column):
    shape = (K, 128)
    spread = jnp.broadcast_to(column, shape)
    return jnp.sum(jnp.where(rows_of(shape) == lanes_of(shape), spread, 0.0), axis=0, keepdims=True)


def restrict(basis, patch, tiles, flat):
    for t in range(3):
        tiles[t] = patch[:, t * 128 : (t + 1) * 128]
    parts = [None] * 9
    for m in range(4):
        rows = jnp.concatenate(
            [tiles[t, pl.ds(m, GROUPS, stride=4), :] for t in range(3)], axis=1
        )
        if m:
            rows = pltpu.roll(rows, 32 * m, 1)
        for t in range(3):
            piece = rows[:, t * 128 : (t + 1) * 128]
            at = 2 * m + t
            parts[at] = piece if parts[at] is None else parts[at] + piece
    for t in range(9):
        flat[t] = parts[t]
    sums = [jnp.zeros((K, 128), f32) for _ in range(3)]
    for g in range(GROUPS):
        for t in range(9):
            block = (g * 9 + t) * 128
            row = jnp.broadcast_to(flat[t, pl.ds(g, 1), :], (K, 128))
            sums[t % 3] = sums[t % 3] + basis[:, block : block + 128] * row
    return jnp.sum(sums[0] + sums[1] + sums[2], axis=1, keepdims=True)


def prolong(basis, weights, tiles, flat):
    wide = jnp.broadcast_to(weights, (K, 128))
    for g in range(GROUPS):
        for t in range(9):
            block = (g * 9 + t) * 128
            flat[t, pl.ds(g, 1), :] = jnp.sum(
                basis[:, block : block + 128] * wide, axis=0, keepdims=True
            )
    for m in range(4):
        rows = jnp.concatenate([flat[2 * m + t] for t in range(3)], axis=1)
        if m:
            rows = pltpu.roll(rows, LW - 32 * m, 1)
        rows = jnp.where(lanes_of(rows.shape) < PY, rows, 0.0)
        for t in range(3):
            tiles[t, pl.ds(m, GROUPS, stride=4), :] = rows[:, t * 128 : (t + 1) * 128]
    return jnp.concatenate([tiles[t] for t in range(3)], axis=1)


def gathered(rows, coarse, suby):
    count = rows.shape[0] // 4
    shift = suby // 4
    taken = [rows[pl.ds(q, count, stride=4), :] for q in range(4)]
    zero = jnp.zeros((shift, 128), f32)
    lanes = lanes_of((count, 128))
    result = None
    for s in range(4):
        own = taken[s]
        later = jnp.concatenate([zero, taken[(s + 1) % 4][: count - shift]], axis=0)
        earlier = jnp.concatenate([taken[(s + 2) % 4][shift:], zero], axis=0)
        piece = jnp.where(
            lanes < 32, own, jnp.where(lanes < 64, later, jnp.where(lanes < 96, earlier, 0.0))
        )
        if s:
            piece = pltpu.roll(piece, 32 * s, 1)
        result = piece if result is None else result + piece
    coarse[...] = result
    return jnp.sum(taken[0] + taken[1] + (taken[2] + taken[3]), axis=0, keepdims=True)


def pick(row, lane):
    return jnp.sum(jnp.where(lanes_of(row.shape) == lane, row, 0.0), axis=1, keepdims=True)


def coarse_solve(inverse, coarse):
    sums = [jnp.zeros((K, 128), f32) for _ in range(4)]
    for b in range(coarse.shape[0]):
        row = jnp.broadcast_to(coarse[pl.ds(b, 1), :], (K, 128))
        sums[b % 4] = sums[b % 4] + inverse[:, b * 128 : (b + 1) * 128] * row
    return jnp.sum((sums[0] + sums[1]) + (sums[2] + sums[3]), axis=1, keepdims=True)


def live_of(counts):
    return (rows_of((K, 1)) < counts[0, 0]).astype(f32)


def relax(vector, diagonal, faces):
    inverse = OMEGA / jnp.where(diagonal > 0.0, diagonal, 1.0)
    below, above, east, west = [inverse * face for face in faces]
    start = inverse * vector
    field = start
    for _ in range(SWEEPS - 1):
        moved = below * up(field) + above * down(field)
        moved = moved + (east * left(field) + west * right(field))
        field = (start + (1.0 - OMEGA) * field) + moved
    return field


def operate(field, diagonal, faces):
    below, above, east, west = faces
    moved = below * up(field) + above * down(field)
    moved = moved + (east * left(field) + west * right(field))
    return diagonal * field - moved


def pack_rows(counts, source, potential, along, across, recombination, head, tail, ahead, behind):
    live = live_of(counts)
    fields = (source, potential, along, across, recombination)
    for f, field in enumerate(fields):
        for t in range(2):
            at = (2 * f + t) * OV
            cols = slice(t * 128, (t + 1) * 128)
            ahead[at : at + OV, :] = field[CX - OV :, cols]
            behind[at : at + OV, :] = field[:OV, cols]
    for t in range(3):
        at = 160 + t * K
        cols = slice(t * 128, (t + 1) * 128)
        ahead[at : at + K, :] = tail[:, cols] * live
        behind[at : at + K, :] = head[:, cols] * live


def pack_columns(
    source, potential, along, across, recombination, before, after, rows, rightward, leftward
):
    fields = (source, potential, along, across, recombination)
    lanes = lanes_of((PX, 128))
    to_right = to_left = None
    for f, field in enumerate(fields):
        tiles = []
        for t in range(2):
            at = (2 * f + t) * OV
            cols = slice(t * 128, (t + 1) * 128)
            tile = jnp.concatenate(
                [before[at : at + OV, :], field[:, cols], after[at : at + OV, :]], axis=0
            )
            rows[f, :, cols] = tile
            tiles.append(tile)
        last = pltpu.roll(jnp.where(lanes >= 111, tiles[1], 0.0), 17 + STRIP * f, 1)
        first = jnp.where(lanes < 17, tiles[0], 0.0)
        if f:
            first = pltpu.roll(first, STRIP * f, 1)
        to_right = last if f == 0 else to_right + last
        to_left = first if f == 0 else to_left + first
    rightward[...] = to_right
    leftward[...] = to_left


def prepare(suby, counts, rows, from_left, from_right, basis, patch, coefs, solved, gather, tiles, flat):
    zero = jnp.zeros((PX, LW - CY), f32)
    lanes = lanes_of((PX, 128))
    fields = []
    for f in range(5):
        middle = pltpu.roll(jnp.concatenate([rows[f], zero], axis=1), OV, 1)
        band = (lanes >= STRIP * f) & (lanes < STRIP * f + 17)
        wide = jnp.zeros((PX, LW - 128), f32)
        one = jnp.concatenate([jnp.where(band, from_left[...], 0.0), wide], axis=1)
        two = jnp.concatenate([jnp.where(band, from_right[...], 0.0), wide], axis=1)
        one = pltpu.roll(one, LW - 1 - STRIP * f, 1)
        two = pltpu.roll(two, OV + CY - STRIP * f, 1)
        fields.append(middle + one + two)
    source, potential, along, across, recombination = fields
    weight = jnp.sqrt(along * up(along))
    rise = 0.5 * (up(potential) - potential)
    below = weight * jnp.exp(rise)
    above = weight * jnp.exp(-rise)
    diagonal = recombination + above + down(below)
    weight = jnp.sqrt(across * left(across))
    rise = 0.5 * (left(potential) - potential)
    east = weight * jnp.exp(rise)
    west = weight * jnp.exp(-rise)
    diagonal = diagonal + west + right(east)
    faces = (below, down(above), east, right(west))
    coefs[0] = diagonal
    for f in range(4):
        coefs[1 + f] = faces[f]
    source = jnp.where(lanes_of((PX, LW)) < PY, source, 0.0)
    patch[...] = source
    own = own_mask((PX, LW), 0)
    square = total(jnp.where(own, source * source, 0.0))
    local = relax(source[8:56], diagonal[8:56], [face[8:56] for face in faces])
    solved[...] = jnp.where(own_mask((48, LW), 8), local, 0.0)
    residual = restrict(basis, source, tiles, flat) * live_of(counts)
    row = to_row(residual)
    row = jnp.where(lanes_of((1, 128)) == SCALARS, square, row)
    gather[...] = jnp.broadcast_to(row, gather.shape)


def put(scalars, at, value):
    scalars[pl.ds(at, 1), :] = jnp.broadcast_to(value, (1, 128))


def got(scalars, at):
    return scalars[pl.ds(at, 1), :][:, 0:1]


def spread_first(
    suby, counts, rows, inverse, basis, solved, part, weights, scalars, coarse, tiles, flat
):
    sums = gathered(rows, coarse, suby)
    square = pick(sums, SCALARS)
    norm = jnp.sqrt(square + EPSILON)
    scale = 1.0 / norm
    solution = coarse_solve(inverse, coarse) * live_of(counts) * scale
    weights[...] = jnp.broadcast_to(solution, (K, 128))
    put(scalars, 0, norm)
    put(scalars, 1, square / (square + EPSILON))
    part[...] = prolong(basis, solution, tiles, flat)
    part[8:56, :] = part[8:56, :] + solved[...] * scale


def fold_rows(part, before, after, folded, rightward, leftward):
    height = folded.shape[0]
    first = (PX - height) // 2
    half = height // 2
    whole = part[first : first + height, :] + jnp.concatenate(
        [before[PX // 2 - half :, :] if before.shape[0] > half else before[...],
         after[:half, :] if after.shape[0] > half else after[...]],
        axis=0,
    )
    folded[...] = whole
    lanes = lanes_of((height, 128))
    moved = pltpu.roll(whole, LW - 255, 1)
    rightward[...] = jnp.where(lanes < 33, moved[:, :128], 0.0)
    leftward[...] = jnp.where(lanes < 33, whole[:, :128], 0.0)


def folded_columns(folded, from_left, from_right):
    height = folded.shape[0]
    zero = jnp.zeros((height, 256), f32)
    one = pltpu.roll(jnp.concatenate([from_left[...], zero], axis=1), LW - 1, 1)
    two = jnp.concatenate([zero, from_right[...]], axis=1)
    return folded[...] + one + two


def apply_first(
    suby, counts, folded, from_left, from_right, coefs, patch, scalars, basis, before, after,
    direction, image, solved, gather, tiles, flat,
):
    field = folded_columns(folded, from_left, from_right)
    direction[...] = field[OV : OV + CX]
    diagonal = coefs[0]
    faces = [coefs[1 + f] for f in range(4)]
    shape = (PX, LW)
    rows, lanes = rows_of(shape), lanes_of(shape)
    inner = (rows >= 1) & (rows < PX - 1) & (lanes < PY)
    vector = jnp.where(inner, operate(field, diagonal, faces), 0.0)
    image[...] = vector[OV : OV + CX]
    own = own_mask((CX, LW), OV)
    mine = jnp.where(own, vector[OV : OV + CX], 0.0)
    first = patch[OV : OV + CX] * (1.0 / got(scalars, 0))
    cross = total(mine * first)
    square = total(mine * mine)
    local = relax(vector[8:56], diagonal[8:56], [face[8:56] for face in faces])
    solved[...] = jnp.where(own_mask((48, LW), 8), local, 0.0)
    residual = restrict(basis, vector, tiles, flat) * live_of(counts)
    fourth = vector[32:40]
    third = pltpu.roll(vector[24:32], 96, 1)
    for_next = for_before = jnp.zeros((K, 128), f32)
    for t in range(3):
        cols = slice(t * 128, (t + 1) * 128)
        at = 160 + t * K
        for_next = for_next + after[at : at + K, :] * fourth[0:1, cols]
        for_before = for_before + before[at : at + K, :] * third[7:8, cols]
    row = to_row(residual)
    row = row + pltpu.roll(to_row(jnp.sum(for_next, axis=1, keepdims=True)), 32, 1)
    row = row + pltpu.roll(to_row(jnp.sum(for_before, axis=1, keepdims=True)), 64, 1)
    lanes = lanes_of((1, 128))
    row = jnp.where(lanes == SCALARS, cross, jnp.where(lanes == SCALARS + 1, square, row))
    gather[...] = jnp.broadcast_to(row, gather.shape)


def spread_second(
    suby, counts, rows, inverse, basis, solved_first, solved, weights, scalars_in,
    part, scalars, coarse, tiles, flat,
):
    sums = gathered(rows, coarse, suby)
    cross = pick(sums, SCALARS)
    square = pick(sums, SCALARS + 1)
    norm = got(scalars_in, 0)
    unit = got(scalars_in, 1)
    rest = square - 2.0 * cross * cross + cross * cross * unit
    second = jnp.sqrt(jnp.maximum(rest, 0.0) + EPSILON)
    scale = 1.0 / second
    solution = coarse_solve(inverse, coarse) * live_of(counts)
    solution = (solution - cross * weights[:, 0:1]) * scale
    put(scalars, 0, norm)
    put(scalars, 1, unit)
    put(scalars, 2, cross)
    put(scalars, 3, second)
    part[...] = prolong(basis, solution, tiles, flat)
    local = (solved[...] - (cross / norm) * solved_first[...]) * scale
    part[8:56, :] = part[8:56, :] + local


def apply_second(
    folded, from_left, from_right, coefs, patch, image, scalars, direction, third, gather
):
    field = folded_columns(folded, from_left, from_right)
    vector = operate(field, coefs[0, 8:56, :], [coefs[1 + f, 8:56, :] for f in range(4)])
    own = own_mask((CX, LW), OV)
    direction[...] = field[8 : 8 + CX]
    vector = jnp.where(own, vector[8 : 8 + CX], 0.0)
    third[...] = vector
    first = jnp.where(own, patch[OV : OV + CX] * (1.0 / got(scalars, 0)), 0.0)
    second = (image[...] - got(scalars, 2) * first) * (1.0 / got(scalars, 3))
    second = jnp.where(own, second, 0.0)
    lanes = lanes_of((1, 128))
    row = jnp.zeros((1, 128), f32)
    for lane, value in enumerate(
        (first * vector, second * vector, vector * vector, first * second, second * second)
    ):
        row = jnp.where(lanes == lane, total(value), row)
    gather[...] = jnp.broadcast_to(row, gather.shape)


def finish(rows, patch, image, third_image, direction_one, direction_two, scalars, solution, residual):
    sums = jnp.sum(rows[...], axis=0, keepdims=True)
    first_second = pick(sums, 0)
    second_second = pick(sums, 1)
    square = pick(sums, 2)
    cross = pick(sums, 3)
    unit_two = pick(sums, 4)
    source_norm = got(scalars, 0)
    unit = got(scalars, 1)
    first_first = got(scalars, 2)
    second_first = got(scalars, 3)
    rest = square - first_second * first_second * (2.0 - unit)
    rest = rest - second_second * second_second * (2.0 - unit_two)
    rest = rest + 2.0 * first_second * second_second * cross
    third_second = jnp.sqrt(jnp.maximum(rest, 0.0) + EPSILON)
    radius = jnp.sqrt(first_first * first_first + second_first * second_first)
    cosine = first_first / radius
    sine = second_first / radius
    upper_right = cosine * first_second + sine * second_second
    lower_right = cosine * second_second - sine * first_second
    radius_two = jnp.sqrt(lower_right * lower_right + third_second * third_second)
    weight_two = lower_right / radius_two * (-sine * source_norm) / radius_two
    weight_one = (cosine * source_norm - upper_right * weight_two) / radius
    remainder_one = source_norm - first_first * weight_one - first_second * weight_two
    remainder_two = -second_first * weight_one - second_second * weight_two
    remainder_three = -third_second * weight_two
    first = patch[OV : OV + CX] * (1.0 / source_norm)
    second = (image[...] - first_first * first) * (1.0 / second_first)
    third = (third_image[...] - first_second * first - second_second * second) * (1.0 / third_second)
    found = weight_one * direction_one[...] + weight_two * direction_two[...]
    left_over = remainder_one * first + remainder_two * second + remainder_three * third
    solution[...] = pltpu.roll(found, LW - OV, 1)[:, :CY]
    residual[...] = pltpu.roll(left_over, LW - OV, 1)[:, :CY]


def shape_of(*dims):
    return jax.ShapeDtypeStruct(dims, f32)


VMEM = pl.BlockSpec(memory_space=pltpu.VMEM)
SMEM = pl.BlockSpec(memory_space=pltpu.SMEM)
PARAMS = pltpu.CompilerParams(vmem_limit_bytes=24 * 1024 * 1024)


def kernel(body, outs, scratch=(), first_smem=False):
    def call(*args):
        specs = [VMEM] * len(args)
        if first_smem:
            specs[0] = SMEM
        return pl.pallas_call(
            body,
            out_shape=outs,
            in_specs=specs,
            out_specs=[VMEM] * len(outs),
            scratch_shapes=list(scratch),
            compiler_params=PARAMS,
        )(*args)

    return call


def swap(axis, forward, backward):
    count = lax.axis_size(axis)
    before = lax.ppermute(forward, axis, [(i, i + 1) for i in range(count - 1)])
    after = lax.ppermute(backward, axis, [(i + 1, i) for i in range(count - 1)])
    return before, after


def everywhere(rows):
    count = rows.shape[0]
    return lax.all_to_all(rows.reshape(count, 1, 128), AXES, 0, 0).reshape(count, 128)


def on_device(
    source, potential, mobility_along, mobility_across, recombination, counts, basis, coarse_inverse
):
    suby = lax.axis_size("gy")
    devices = lax.axis_size("gx") * suby
    rows = shape_of(devices, 128)
    patch_shape, own_shape = shape_of(PX, LW), shape_of(CX, LW)
    tiles = pltpu.VMEM((3, PX, 128), f32)
    flat = pltpu.VMEM((9, GROUPS, 128), f32)
    coarse = pltpu.VMEM((devices // 4, 128), f32)
    fields = (source, potential, mobility_along, mobility_across, recombination)

    def bind(body):
        def run(*refs):
            return body(suby, *refs)

        return run

    whole = lambda shape: pl.BlockSpec(shape, lambda i: (0,) * len(shape))
    edge = 3 * 128
    last = basis.shape[1] // edge - 1
    ahead, behind = pl.pallas_call(
        pack_rows,
        grid=(1,),
        out_shape=[shape_of(256, 128)] * 2,
        in_specs=[SMEM]
        + [whole((CX, CY))] * 5
        + [pl.BlockSpec((K, edge), lambda i: (0, 0)), pl.BlockSpec((K, edge), lambda i: (0, last))],
        out_specs=[whole((256, 128))] * 2,
        compiler_params=PARAMS,
    )(counts, *fields, basis, basis)
    before, after = swap("gx", ahead, behind)
    strip = shape_of(PX, 128)
    grown, rightward, leftward = kernel(pack_columns, [shape_of(5, PX, CY), strip, strip])(
        *fields, before, after
    )
    from_left, from_right = swap("gy", rightward, leftward)
    patch, coefs, solved_one, row = kernel(
        bind(prepare),
        [patch_shape, shape_of(5, PX, LW), shape_of(48, LW), rows],
        [tiles, flat],
        True,
    )(counts, grown, from_left, from_right, basis)
    part, weights, scalars_one = kernel(
        bind(spread_first),
        [patch_shape, shape_of(K, 128), shape_of(8, 128)],
        [coarse, tiles, flat],
        True,
    )(counts, everywhere(row), coarse_inverse, basis, solved_one)
    over, under = swap("gx", part[PX // 2 :], part[: PX // 2])
    folded, rightward, leftward = kernel(fold_rows, [patch_shape, strip, strip])(part, over, under)
    from_left, from_right = swap("gy", rightward, leftward)
    direction_one, image_one, solved_two, row = kernel(
        bind(apply_first),
        [own_shape, own_shape, shape_of(48, LW), rows],
        [tiles, flat],
        True,
    )(
        counts, folded, from_left, from_right, coefs, patch, scalars_one, basis, before, after
    )
    part, scalars_two = kernel(
        bind(spread_second),
        [patch_shape, shape_of(8, 128)],
        [coarse, tiles, flat],
        True,
    )(
        counts, everywhere(row), coarse_inverse, basis, solved_one, solved_two, weights, scalars_one
    )
    over, under = swap("gx", part[40:], part[:24])
    strip = shape_of(48, 128)
    folded, rightward, leftward = kernel(fold_rows, [shape_of(48, LW), strip, strip])(
        part, over, under
    )
    from_left, from_right = swap("gy", rightward, leftward)
    direction_two, image_two, row = kernel(apply_second, [own_shape, own_shape, rows])(
        folded, from_left, from_right, coefs, patch, image_one, scalars_two
    )
    out = shape_of(CX, CY)
    answer, residual = kernel(finish, [out, out])(
        everywhere(row), patch, image_one, image_two, direction_one, direction_two, scalars_two
    )
    return answer, residual


def solution(mesh):
    grid = P("gx", "gy")
    return jax.shard_map(
        on_device,
        mesh=mesh,
        in_specs=(grid,) * 7 + (P(("gx", "gy"), None),),
        out_specs=(grid, grid),
        check_vma=False,
    )
```

time: 1200 us -> 171 us (0.14)
  waiting for transfers between devices: 539 us -> 15 us
  blocking collectives: 492 us -> 108 us
  other arithmetic: 35.7 us -> 0 us
  starting transfers between devices: 64 us -> 34.6 us
  between operations: 23.9 us -> 1.5 us
  local copies, waits for them, and re-layouts: 25.6 us -> 5.47 us
  matrix products: 14.6 us -> 0 us
    unnamed x4 -> x0, waiting for transfers between devices: 511 us -> none
    psum x5 -> x0, blocking collectives: 492 us -> none  [totals(): return lax.psum(values, ('gx', 'gy'))]
    all_to_all x0 -> x3, blocking collectives: none -> 108 us  [everywhere(): lax.all_to_all(rows.reshape(count, 1, 128), AXES, 0, 0).reshape(count, 128)]
    ppermute x24 -> x12, starting transfers between devices: 64 us -> 34.6 us  [the longest x6 23.5 us: swap(): before = lax.ppermute(forward, axis, [(i, i + 1) for i in range(count - 1)])]
    dot_general x6 -> x0, matrix products: 14.6 us -> none  [the longest x2 6.74 us: accumulate(): return jnp.dot(coarse_inverse, piece, precision=HIGHEST_PRECISION)]
    ppermute x24 -> x12, waiting for transfers between devices: 27.2 us -> 15 us  [the longest x6 12.2 us: swap(): after = lax.ppermute(backward, axis, [(i + 1, i) for i in range(count - 1)])]
    slice x25 -> x2, local copies, waits for them, and re-layouts: 12 us -> 0.02 us  [the longest x1 0.01 us: on_device(): over, under = swap('gx', part[PX // 2:], part[:PX // 2])]
  transfers between devices with their start and end apart: 26 -> 12, of which waited for: 13 -> 8; matrix products, arithmetic and copies ran while one was open for 2% -> 0% of each run, Pallas kernels for 0% -> 0%
where the time goes in v1:
time: 171 us; the launch traced here: 170 us
  blocking collectives  108 us (63%)
  starting transfers between devices  34.6 us (20%)
  waiting for transfers between devices  15 us (9%)
  local copies, waits for them, and re-layouts  5.47 us (3%)
  Pallas kernels  5.4 us (3%)
    all_to_all x3, blocking collectives, everywhere(): lax.all_to_all(rows.reshape(count, 1, 128), AXES, 0, 0).reshape(count, 128)  108 us
    ppermute x6, starting transfers between devices, swap(): before = lax.ppermute(forward, axis, [(i, i + 1) for i in range(count - 1)])  23.5 us
    ppermute x6, waiting for transfers between devices, swap(): after = lax.ppermute(backward, axis, [(i + 1, i) for i in range(count - 1)])  12.2 us
    ppermute x6, starting transfers between devices, swap(): after = lax.ppermute(backward, axis, [(i + 1, i) for i in range(count - 1)])  11.1 us
    unnamed x16, local copies, waits for them, and re-layouts  5.46 us
    pallas_call x9, Pallas kernels, call(): pl.pallas_call(body, out_shape=outs, in_specs=specs, out_specs=[VMEM] * l...  5.39 us
  transfers between devices with their start and end apart: 12, of which 8 were waited for; matrix products, arithmetic and copies ran while one was open for 0% of the time, Pallas kernels for 0%

profile of v1, /device:TPU:1, one launch (start us, length us, event | category | flops | bytes accessed | tf_op | source)
XLA Modules:
  0.0 170.0 jit_solution(15999549794539595325)
XLA Ops:
  1.3 0.0 copy-start
  1.3 1.7 copy-done
  2.9 0.0 copy-start.3
  2.9 0.8 copy-done.3
  3.7 0.0 copy-start.4
  3.7 0.8 copy-done.4
  4.5 0.0 copy-start.5
  4.5 0.8 copy-done.5
  5.2 0.0 copy-start.6
  5.2 0.8 copy-done.6
  6.0 0.0 copy-start.7
  6.0 0.8 copy-done.7
  6.7 0.0 copy-start.1
  6.8 0.0 copy-start.2
  6.8 4.3 %collective-permute-start = (f32[256,128]{1,0:T(8,128)S(1)}, f32[256,128]{1,0:T(8,128)S(1)}, u32[]{:S(2)}, u32[]{:S(2)}) collective-permute-start(f32[256,128]{1,0:T(8,128)S(1)} %get-tuple-element.29), channel_id=1, source_target_pairs={{0,64},{64,128},{128,192},{192,256},{256,320},{320,384},{384,448},... | collective-permute-start | bytes 393224 | tf_op jit(solution)/shard_map/ppermute | solution.py:436
  11.1 1.3 collective-permute-start.1
  12.4 0.6 collective-permute-done.before.refs_8_
  13.0 3.8 %collective-permute-done.1.after.refs_9_ = f32[256,128]{1,0:T(8,128)S(1)} collective-permute-done((f32[256,128]{1,0:T(8,128)S(1)}, f32[256,128]{1,0:T(8,128)S(1)}, u32[]{:S(2)}, u32[]{:S(2)}) %collective-permute-start.1) | collective-permute-done | bytes 131104 | tf_op jit(solution)/shard_map/ppermute | solution.py:437
  16.8 0.1 shard_map.96
  17.0 5.1 %collective-permute-start.2 = (f32[64,128]{1,0:T(8,128)S(1)}, f32[64,128]{1,0:T(8,128)S(1)}, u32[]{:S(2)}, u32[]{:S(2)}) collective-permute-start(f32[64,128]{1,0:T(8,128)S(1)} %get-tuple-element.32), channel_id=1, source_target_pairs={{0,1},{1,2},{2,3},{3,4},{4,5},{5,6},{6,7},{7,8},{8,9},{9,10},{10,1... | collective-permute-start | bytes 98312 | tf_op jit(solution)/shard_map/ppermute | solution.py:436
  22.1 3.4 %collective-permute-start.3 = (f32[64,128]{1,0:T(8,128)S(1)}, f32[64,128]{1,0:T(8,128)S(1)}, u32[]{:S(2)}, u32[]{:S(2)}) collective-permute-start(f32[64,128]{1,0:T(8,128)S(1)} %get-tuple-element.33), channel_id=1, source_target_pairs={{1,0},{2,1},{3,2},{4,3},{5,4},{6,5},{7,6},{8,7},{9,8},{10,9},{11,1... | collective-permute-start | bytes 98312 | tf_op jit(solution)/shard_map/ppermute | solution.py:437
  25.5 0.0 collective-permute-done.2.refs_2_
  25.5 1.8 %collective-permute-done.3.refs_3_ = f32[64,128]{1,0:T(8,128)S(1)} collective-permute-done((f32[64,128]{1,0:T(8,128)S(1)}, f32[64,128]{1,0:T(8,128)S(1)}, u32[]{:S(2)}, u32[]{:S(2)}) %collective-permute-start.3) | collective-permute-done | bytes 32800 | tf_op jit(solution)/shard_map/ppermute | solution.py:437
  27.3 0.0 copy-done.1
  27.3 1.3 shard_map.97
  28.6 40.2 %all_to_all.15 = f32[512,1,128]{2,1,0:T(1,128)S(1)} all-to-all(f32[512,1,128]{2,1,0:T(1,128)S(1)} %bitcast.16), channel_id=1, replica_groups=mesh['gx'=8,'gy'=64] {'gx','gy'}, dimensions={0} | all-to-all | bytes 524288 | tf_op jit(solution)/shard_map/all_to_all | solution.py:443
  68.9 0.0 copy-done.2
  68.9 0.6 shard_map.98
  69.5 1.3 collective-permute-start.5
  70.8 4.0 %collective-permute-start.4 = (f32[32,384]{1,0:T(8,128)S(1)}, f32[32,384]{1,0:T(8,128)S(1)}, u32[]{:S(2)}, u32[]{:S(2)}) collective-permute-start(f32[32,384]{1,0:T(8,128)S(1)} %get-tuple-element.59), channel_id=1, source_target_pairs={{0,64},{64,128},{128,192},{192,256},{256,320},{320,384},{384,448},... | collective-permute-start | bytes 147464 | tf_op jit(solution)/shard_map/ppermute | solution.py:436
  74.8 0.1 collective-permute-done.5.after
  74.9 1.0 collective-permute-done.4.before
  76.0 0.1 shard_map.99
  76.1 3.0 %collective-permute-start.6 = (f32[64,128]{1,0:T(8,128)S(1)}, f32[64,128]{1,0:T(8,128)S(1)}, u32[]{:S(2)}, u32[]{:S(2)}) collective-permute-start(f32[64,128]{1,0:T(8,128)S(1)} %get-tuple-element.38), channel_id=1, source_target_pairs={{0,1},{1,2},{2,3},{3,4},{4,5},{5,6},{6,7},{7,8},{8,9},{9,10},{10,1... | collective-permute-start | bytes 98312 | tf_op jit(solution)/shard_map/ppermute | solution.py:436
  79.1 1.9 %collective-permute-start.7 = (f32[64,128]{1,0:T(8,128)S(1)}, f32[64,128]{1,0:T(8,128)S(1)}, u32[]{:S(2)}, u32[]{:S(2)}) collective-permute-start(f32[64,128]{1,0:T(8,128)S(1)} %get-tuple-element.39), channel_id=1, source_target_pairs={{1,0},{2,1},{3,2},{4,3},{5,4},{6,5},{7,6},{8,7},{9,8},{10,9},{11,1... | collective-permute-start | bytes 98312 | tf_op jit(solution)/shard_map/ppermute | solution.py:437
  81.0 0.0 collective-permute-done.6.refs_2_
  81.0 3.3 %collective-permute-done.7.refs_3_ = f32[64,128]{1,0:T(8,128)S(1)} collective-permute-done((f32[64,128]{1,0:T(8,128)S(1)}, f32[64,128]{1,0:T(8,128)S(1)}, u32[]{:S(2)}, u32[]{:S(2)}) %collective-permute-start.7) | collective-permute-done | bytes 32800 | tf_op jit(solution)/shard_map/ppermute | solution.py:437
  84.3 1.2 shard_map.100
  85.5 34.0 %all_to_all.16 = f32[512,1,128]{2,1,0:T(1,128)S(1)} all-to-all(f32[512,1,128]{2,1,0:T(1,128)S(1)} %bitcast.15), channel_id=1, replica_groups=mesh['gx'=8,'gy'=64] {'gx','gy'}, dimensions={0} | all-to-all | bytes 524288 | tf_op jit(solution)/shard_map/all_to_all | solution.py:443
  119.5 0.7 shard_map.101
  120.2 1.3 collective-permute-start.9
  121.5 4.0 %collective-permute-start.8 = (f32[24,384]{1,0:T(8,128)S(1)}, f32[24,384]{1,0:T(8,128)S(1)}, u32[]{:S(2)}, u32[]{:S(2)}) collective-permute-start(f32[24,384]{1,0:T(8,128)S(1)} %get-tuple-element.57), channel_id=1, source_target_pairs={{0,64},{64,128},{128,192},{192,256},{256,320},{320,384},{384,448},... | collective-permute-start | bytes 110600 | tf_op jit(solution)/shard_map/ppermute | solution.py:436
  125.5 0.0 collective-permute-done.9.after
  125.5 1.0 collective-permute-done.8.before
  126.6 0.1 shard_map.102
  126.7 3.0 %collective-permute-start.10 = (f32[48,128]{1,0:T(8,128)S(1)}, f32[48,128]{1,0:T(8,128)S(1)}, u32[]{:S(2)}, u32[]{:S(2)}) collective-permute-start(f32[48,128]{1,0:T(8,128)S(1)} %get-tuple-element.48), channel_id=1, source_target_pairs={{0,1},{1,2},{2,3},{3,4},{4,5},{5,6},{6,7},{7,8},{8,9},{9,10},{10,1... | collective-permute-start | bytes 73736 | tf_op jit(solution)/shard_map/ppermute | solution.py:436
  129.7 1.9 %collective-permute-start.11 = (f32[48,128]{1,0:T(8,128)S(1)}, f32[48,128]{1,0:T(8,128)S(1)}, u32[]{:S(2)}, u32[]{:S(2)}) collective-permute-start(f32[48,128]{1,0:T(8,128)S(1)} %get-tuple-element.49), channel_id=1, source_target_pairs={{1,0},{2,1},{3,2},{4,3},{5,4},{6,5},{7,6},{8,7},{9,8},{10,9},{11,1... | collective-permute-start | bytes 73736 | tf_op jit(solution)/shard_map/ppermute | solution.py:437
  131.6 0.0 collective-permute-done.10.from_left
  131.6 3.2 %collective-permute-done.11.from_right = f32[48,128]{1,0:T(8,128)S(1)} collective-permute-done((f32[48,128]{1,0:T(8,128)S(1)}, f32[48,128]{1,0:T(8,128)S(1)}, u32[]{:S(2)}, u32[]{:S(2)}) %collective-permute-start.11) | collective-permute-done | bytes 24608 | tf_op jit(solution)/shard_map/ppermute | solution.py:437
  134.8 0.3 shard_map.103
  135.1 34.0 %all_to_all.17 = f32[512,1,128]{2,1,0:T(1,128)S(1)} all-to-all(f32[512,1,128]{2,1,0:T(1,128)S(1)} %bitcast.17), channel_id=1, replica_groups=mesh['gx'=8,'gy'=64] {'gx','gy'}, dimensions={0} | all-to-all | bytes 524288 | tf_op jit(solution)/shard_map/all_to_all | solution.py:443
  169.1 0.9 shard_map.104
  (3 shorter events, 0.0 us)
Async XLA Ops:
  1.3 1.7 copy-start
  2.9 0.8 copy-start.3
  3.7 0.8 copy-start.4
  4.5 0.8 copy-start.5
  5.2 0.8 copy-start.6
  6.0 0.8 copy-start.7
  6.7 20.6 %copy-start.1 = (f32[32,18432]{1,0:T(8,128)S(1)}, f32[32,18432]{1,0:T(8,128)}, u32[]{:S(2)}) copy-start(f32[32,18432]{1,0:T(8,128)} %refs_3_.3) | copy-start | bytes 7077892
  6.8 62.1 %copy-start.2 = (f32[32,16384]{1,0:T(8,128)S(1)}, f32[32,16384]{1,0:T(8,128)}, u32[]{:S(2)}) copy-start(f32[32,16384]{1,0:T(8,128)} %refs_2_.3) | copy-start | bytes 6291460
  6.8 6.2 %collective-permute-start = (f32[256,128]{1,0:T(8,128)S(1)}, f32[256,128]{1,0:T(8,128)S(1)}, u32[]{:S(2)}, u32[]{:S(2)}) collective-permute-start(f32[256,128]{1,0:T(8,128)S(1)} %get-tuple-element.29), channel_id=1, source_target_pairs={{0,64},{64,128},{128,192},{192,256},{256,320},{320,384},{384,448},... | collective-permute-start | bytes 393224 | tf_op jit(solution)/shard_map/ppermute | solution.py:436
  11.1 5.7 %collective-permute-start.1 = (f32[256,128]{1,0:T(8,128)S(1)}, f32[256,128]{1,0:T(8,128)S(1)}, u32[]{:S(2)}, u32[]{:S(2)}) collective-permute-start(f32[256,128]{1,0:T(8,128)S(1)} %get-tuple-element.30), channel_id=1, source_target_pairs={{64,0},{128,64},{192,128},{256,192},{320,256},{384,320},{448,384},... | collective-permute-start | bytes 393224 | tf_op jit(solution)/shard_map/ppermute | solution.py:437
  17.0 8.5 %collective-permute-start.2 = (f32[64,128]{1,0:T(8,128)S(1)}, f32[64,128]{1,0:T(8,128)S(1)}, u32[]{:S(2)}, u32[]{:S(2)}) collective-permute-start(f32[64,128]{1,0:T(8,128)S(1)} %get-tuple-element.32), channel_id=1, source_target_pairs={{0,1},{1,2},{2,3},{3,4},{4,5},{5,6},{6,7},{7,8},{8,9},{9,10},{10,1... | collective-permute-start | bytes 98312 | tf_op jit(solution)/shard_map/ppermute | solution.py:436
  22.1 5.2 %collective-permute-start.3 = (f32[64,128]{1,0:T(8,128)S(1)}, f32[64,128]{1,0:T(8,128)S(1)}, u32[]{:S(2)}, u32[]{:S(2)}) collective-permute-start(f32[64,128]{1,0:T(8,128)S(1)} %get-tuple-element.33), channel_id=1, source_target_pairs={{1,0},{2,1},{3,2},{4,3},{5,4},{6,5},{7,6},{8,7},{9,8},{10,9},{11,1... | collective-permute-start | bytes 98312 | tf_op jit(solution)/shard_map/ppermute | solution.py:437
  69.5 5.4 %collective-permute-start.5 = (f32[32,384]{1,0:T(8,128)S(1)}, f32[32,384]{1,0:T(8,128)S(1)}, u32[]{:S(2)}, u32[]{:S(2)}) collective-permute-start(f32[32,384]{1,0:T(8,128)S(1)} %get-tuple-element.58), channel_id=1, source_target_pairs={{64,0},{128,64},{192,128},{256,192},{320,256},{384,320},{448,384},... | collective-permute-start | bytes 147464 | tf_op jit(solution)/shard_map/ppermute | solution.py:437
  70.8 5.2 %collective-permute-start.4 = (f32[32,384]{1,0:T(8,128)S(1)}, f32[32,384]{1,0:T(8,128)S(1)}, u32[]{:S(2)}, u32[]{:S(2)}) collective-permute-start(f32[32,384]{1,0:T(8,128)S(1)} %get-tuple-element.59), channel_id=1, source_target_pairs={{0,64},{64,128},{128,192},{192,256},{256,320},{320,384},{384,448},... | collective-permute-start | bytes 147464 | tf_op jit(solution)/shard_map/ppermute | solution.py:436
  76.1 5.0 %collective-permute-start.6 = (f32[64,128]{1,0:T(8,128)S(1)}, f32[64,128]{1,0:T(8,128)S(1)}, u32[]{:S(2)}, u32[]{:S(2)}) collective-permute-start(f32[64,128]{1,0:T(8,128)S(1)} %get-tuple-element.38), channel_id=1, source_target_pairs={{0,1},{1,2},{2,3},{3,4},{4,5},{5,6},{6,7},{7,8},{8,9},{9,10},{10,1... | collective-permute-start | bytes 98312 | tf_op jit(solution)/shard_map/ppermute | solution.py:436
  79.1 5.2 %collective-permute-start.7 = (f32[64,128]{1,0:T(8,128)S(1)}, f32[64,128]{1,0:T(8,128)S(1)}, u32[]{:S(2)}, u32[]{:S(2)}) collective-permute-start(f32[64,128]{1,0:T(8,128)S(1)} %get-tuple-element.39), channel_id=1, source_target_pairs={{1,0},{2,1},{3,2},{4,3},{5,4},{6,5},{7,6},{8,7},{9,8},{10,9},{11,1... | collective-permute-start | bytes 98312 | tf_op jit(solution)/shard_map/ppermute | solution.py:437
  120.2 5.3 %collective-permute-start.9 = (f32[24,384]{1,0:T(8,128)S(1)}, f32[24,384]{1,0:T(8,128)S(1)}, u32[]{:S(2)}, u32[]{:S(2)}) collective-permute-start(f32[24,384]{1,0:T(8,128)S(1)} %get-tuple-element.56), channel_id=1, source_target_pairs={{64,0},{128,64},{192,128},{256,192},{320,256},{384,320},{448,384},... | collective-permute-start | bytes 110600 | tf_op jit(solution)/shard_map/ppermute | solution.py:437
  121.5 5.0 %collective-permute-start.8 = (f32[24,384]{1,0:T(8,128)S(1)}, f32[24,384]{1,0:T(8,128)S(1)}, u32[]{:S(2)}, u32[]{:S(2)}) collective-permute-start(f32[24,384]{1,0:T(8,128)S(1)} %get-tuple-element.57), channel_id=1, source_target_pairs={{0,64},{64,128},{128,192},{192,256},{256,320},{320,384},{384,448},... | collective-permute-start | bytes 110600 | tf_op jit(solution)/shard_map/ppermute | solution.py:436
  126.7 5.0 %collective-permute-start.10 = (f32[48,128]{1,0:T(8,128)S(1)}, f32[48,128]{1,0:T(8,128)S(1)}, u32[]{:S(2)}, u32[]{:S(2)}) collective-permute-start(f32[48,128]{1,0:T(8,128)S(1)} %get-tuple-element.48), channel_id=1, source_target_pairs={{0,1},{1,2},{2,3},{3,4},{4,5},{5,6},{6,7},{7,8},{8,9},{9,10},{10,1... | collective-permute-start | bytes 73736 | tf_op jit(solution)/shard_map/ppermute | solution.py:436
  129.7 5.1 %collective-permute-start.11 = (f32[48,128]{1,0:T(8,128)S(1)}, f32[48,128]{1,0:T(8,128)S(1)}, u32[]{:S(2)}, u32[]{:S(2)}) collective-permute-start(f32[48,128]{1,0:T(8,128)S(1)} %get-tuple-element.49), channel_id=1, source_target_pairs={{1,0},{2,1},{3,2},{4,3},{5,4},{6,5},{7,6},{8,7},{9,8},{10,9},{11,1... | collective-permute-start | bytes 73736 | tf_op jit(solution)/shard_map/ppermute | solution.py:437

commit v2 on v1

--- a/solution.py
+++ b/solution.py
@@ -160,15 +160,30 @@
     return diagonal * field - moved
 
 
-def pack_rows(counts, source, potential, along, across, recombination, head, tail, ahead, behind):
+def pack_rows(
+    counts, source, potential, along, across, recombination, basis, held, ahead, behind,
+    head, tail, sems,
+):
+    edge = head.shape[1]
+    copies = [
+        pltpu.make_async_copy(field, held.at[f], sems.at[f])
+        for f, field in enumerate((source, potential, along, across, recombination))
+    ]
+    copies.append(pltpu.make_async_copy(basis.at[:, :edge], head, sems.at[5]))
+    copies.append(
+        pltpu.make_async_copy(basis.at[:, basis.shape[1] - edge :], tail, sems.at[6])
+    )
+    for copy in copies:
+        copy.start()
     live = live_of(counts)
-    fields = (source, potential, along, across, recombination)
-    for f, field in enumerate(fields):
+    for copy in copies:
+        copy.wait()
+    for f in range(5):
         for t in range(2):
             at = (2 * f + t) * OV
             cols = slice(t * 128, (t + 1) * 128)
-            ahead[at : at + OV, :] = field[CX - OV :, cols]
-            behind[at : at + OV, :] = field[:OV, cols]
+            ahead[at : at + OV, :] = held[f, CX - OV :, cols]
+            behind[at : at + OV, :] = held[f, :OV, cols]
     for t in range(3):
         at = 160 + t * K
         cols = slice(t * 128, (t + 1) * 128)
@@ -176,19 +191,16 @@
         behind[at : at + K, :] = head[:, cols] * live
 
 
-def pack_columns(
-    source, potential, along, across, recombination, before, after, rows, rightward, leftward
-):
-    fields = (source, potential, along, across, recombination)
+def pack_columns(held, before, after, rows, rightward, leftward):
     lanes = lanes_of((PX, 128))
     to_right = to_left = None
-    for f, field in enumerate(fields):
+    for f in range(5):
         tiles = []
         for t in range(2):
             at = (2 * f + t) * OV
             cols = slice(t * 128, (t + 1) * 128)
             tile = jnp.concatenate(
-                [before[at : at + OV, :], field[:, cols], after[at : at + OV, :]], axis=0
+                [before[at : at + OV, :], held[f, :, cols], after[at : at + OV, :]], axis=0
             )
             rows[f, :, cols] = tile
             tiles.append(tile)
@@ -370,6 +382,11 @@
     gather[...] = jnp.broadcast_to(row, gather.shape)
 
 
+def add_rows(rows, gather):
+    row = jnp.sum(rows[...], axis=0, keepdims=True)
+    gather[...] = jnp.broadcast_to(row, gather.shape)
+
+
 def finish(rows, patch, image, third_image, direction_one, direction_two, scalars, solution, residual):
     sums = jnp.sum(rows[...], axis=0, keepdims=True)
     first_second = pick(sums, 0)
@@ -438,9 +455,9 @@
     return before, after
 
 
-def everywhere(rows):
+def everywhere(rows, axes=AXES):
     count = rows.shape[0]
-    return lax.all_to_all(rows.reshape(count, 1, 128), AXES, 0, 0).reshape(count, 128)
+    return lax.all_to_all(rows.reshape(count, 1, 128), axes, 0, 0).reshape(count, 128)
 
 
 def on_device(
@@ -461,23 +478,19 @@
 
         return run
 
-    whole = lambda shape: pl.BlockSpec(shape, lambda i: (0,) * len(shape))
-    edge = 3 * 128
-    last = basis.shape[1] // edge - 1
-    ahead, behind = pl.pallas_call(
+    edge = pltpu.VMEM((K, 3 * 128), f32)
+    held, ahead, behind = pl.pallas_call(
         pack_rows,
-        grid=(1,),
-        out_shape=[shape_of(256, 128)] * 2,
-        in_specs=[SMEM]
-        + [whole((CX, CY))] * 5
-        + [pl.BlockSpec((K, edge), lambda i: (0, 0)), pl.BlockSpec((K, edge), lambda i: (0, last))],
-        out_specs=[whole((256, 128))] * 2,
+        out_shape=[shape_of(5, CX, CY), shape_of(256, 128), shape_of(256, 128)],
+        in_specs=[SMEM] + [pl.BlockSpec(memory_space=pltpu.HBM)] * 6,
+        out_specs=[VMEM] * 3,
+        scratch_shapes=[edge, edge, pltpu.SemaphoreType.DMA((7,))],
         compiler_params=PARAMS,
-    )(counts, *fields, basis, basis)
+    )(counts, *[pltpu.with_memory_space_constraint(x, pltpu.HBM) for x in (*fields, basis)])
     before, after = swap("gx", ahead, behind)
     strip = shape_of(PX, 128)
     grown, rightward, leftward = kernel(pack_columns, [shape_of(5, PX, CY), strip, strip])(
-        *fields, before, after
+        held, before, after
     )
     from_left, from_right = swap("gy", rightward, leftward)
     patch, coefs, solved_one, row = kernel(
@@ -517,12 +530,15 @@
         part, over, under
     )
     from_left, from_right = swap("gy", rightward, leftward)
-    direction_two, image_two, row = kernel(apply_second, [own_shape, own_shape, rows])(
+    direction_two, image_two, row = kernel(
+        apply_second, [own_shape, own_shape, shape_of(devices // suby, 128)]
+    )(
         folded, from_left, from_right, coefs, patch, image_one, scalars_two
     )
+    (row,) = kernel(add_rows, [shape_of(suby, 128)])(everywhere(row, "gx"))
     out = shape_of(CX, CY)
     answer, residual = kernel(finish, [out, out])(
-        everywhere(row), patch, image_one, image_two, direction_one, direction_two, scalars_two
+        everywhere(row, "gy"), patch, image_one, image_two, direction_one, direction_two, scalars_two
     )
     return answer, residual
 

time: 171 us -> 164 us (0.959)
  local copies, waits for them, and re-layouts: 5.47 us -> 0.03 us
  blocking collectives: 108 us -> 106 us
    unnamed x16 -> x4, local copies, waits for them, and re-layouts: 5.46 us -> 0.01 us
    all_to_all x3 -> x4, blocking collectives: 108 us -> 106 us  [everywhere(): lax.all_to_all(rows.reshape(count, 1, 128), axes, 0, 0).reshape(count, 128)]
    pallas_call x9 -> x10, Pallas kernels: 5.39 us -> 5.31 us  [call(): pl.pallas_call(body, out_shape=outs, in_specs=specs, out_specs=[VMEM] * l...]
where the time goes in v2:
time: 164 us; the launch traced here: 163 us
  blocking collectives  106 us (65%)
  starting transfers between devices  34.4 us (21%)
  waiting for transfers between devices  14.9 us (9%)
  Pallas kernels  6.3 us (4%)
    all_to_all x4, blocking collectives, everywhere(): lax.all_to_all(rows.reshape(count, 1, 128), axes, 0, 0).reshape(count, 128)  106 us
    ppermute x6, starting transfers between devices, swap(): before = lax.ppermute(forward, axis, [(i, i + 1) for i in range(count - 1)])  23.3 us
    ppermute x6, waiting for transfers between devices, swap(): after = lax.ppermute(backward, axis, [(i + 1, i) for i in range(count - 1)])  12.2 us
    ppermute x6, starting transfers between devices, swap(): after = lax.ppermute(backward, axis, [(i + 1, i) for i in range(count - 1)])  11.1 us
    pallas_call x10, Pallas kernels, call(): pl.pallas_call(body, out_shape=outs, in_specs=specs, out_specs=[VMEM] * l...  5.31 us
  transfers between devices with their start and end apart: 12, of which 8 were waited for; matrix products, arithmetic and copies ran while one was open for 0% of the time, Pallas kernels for 0%

profile of v2, /device:TPU:1, one launch (start us, length us, event | category | flops | bytes accessed | tf_op | source)
XLA Modules:
  0.0 163.2 jit_solution(16111014680684364680)
XLA Ops:
  0.6 0.0 copy-start
  1.4 1.0 shard_map.95
  2.4 0.0 copy-start.1
  2.4 4.2 %collective-permute-start = (f32[256,128]{1,0:T(8,128)S(1)}, f32[256,128]{1,0:T(8,128)S(1)}, u32[]{:S(2)}, u32[]{:S(2)}) collective-permute-start(f32[256,128]{1,0:T(8,128)S(1)} %get-tuple-element.31), channel_id=1, source_target_pairs={{0,64},{64,128},{128,192},{192,256},{256,320},{320,384},{384,448},... | collective-permute-start | bytes 393224 | tf_op jit(solution)/shard_map/ppermute | solution.py:453
  6.6 1.3 collective-permute-start.1
  7.9 0.6 collective-permute-done.before.refs_8_
  8.5 3.8 %collective-permute-done.1.after.refs_9_ = f32[256,128]{1,0:T(8,128)S(1)} collective-permute-done((f32[256,128]{1,0:T(8,128)S(1)}, f32[256,128]{1,0:T(8,128)S(1)}, u32[]{:S(2)}, u32[]{:S(2)}) %collective-permute-start.1) | collective-permute-done | bytes 131104 | tf_op jit(solution)/shard_map/ppermute | solution.py:454
  12.3 0.1 shard_map.96
  12.5 5.1 %collective-permute-start.2 = (f32[64,128]{1,0:T(8,128)S(1)}, f32[64,128]{1,0:T(8,128)S(1)}, u32[]{:S(2)}, u32[]{:S(2)}) collective-permute-start(f32[64,128]{1,0:T(8,128)S(1)} %get-tuple-element.34), channel_id=1, source_target_pairs={{0,1},{1,2},{2,3},{3,4},{4,5},{5,6},{6,7},{7,8},{8,9},{9,10},{10,1... | collective-permute-start | bytes 98312 | tf_op jit(solution)/shard_map/ppermute | solution.py:453
  17.6 3.4 %collective-permute-start.3 = (f32[64,128]{1,0:T(8,128)S(1)}, f32[64,128]{1,0:T(8,128)S(1)}, u32[]{:S(2)}, u32[]{:S(2)}) collective-permute-start(f32[64,128]{1,0:T(8,128)S(1)} %get-tuple-element.35), channel_id=1, source_target_pairs={{1,0},{2,1},{3,2},{4,3},{5,4},{6,5},{7,6},{8,7},{9,8},{10,9},{11,1... | collective-permute-start | bytes 98312 | tf_op jit(solution)/shard_map/ppermute | solution.py:454
  21.0 0.0 collective-permute-done.2.refs_2_
  21.0 1.8 %collective-permute-done.3.refs_3_ = f32[64,128]{1,0:T(8,128)S(1)} collective-permute-done((f32[64,128]{1,0:T(8,128)S(1)}, f32[64,128]{1,0:T(8,128)S(1)}, u32[]{:S(2)}, u32[]{:S(2)}) %collective-permute-start.3) | collective-permute-done | bytes 32800 | tf_op jit(solution)/shard_map/ppermute | solution.py:454
  22.8 0.0 copy-done
  22.8 1.3 shard_map.97
  24.2 40.2 %all_to_all.20 = f32[512,1,128]{2,1,0:T(1,128)S(1)} all-to-all(f32[512,1,128]{2,1,0:T(1,128)S(1)} %bitcast.19), channel_id=1, replica_groups=mesh['gx'=8,'gy'=64] {'gx','gy'}, dimensions={0} | all-to-all | bytes 524288 | tf_op jit(solution)/shard_map/all_to_all | solution.py:460
  64.4 0.0 copy-done.1
  64.4 0.6 shard_map.98
  65.0 1.3 collective-permute-start.5
  66.3 4.0 %collective-permute-start.4 = (f32[32,384]{1,0:T(8,128)S(1)}, f32[32,384]{1,0:T(8,128)S(1)}, u32[]{:S(2)}, u32[]{:S(2)}) collective-permute-start(f32[32,384]{1,0:T(8,128)S(1)} %get-tuple-element.61), channel_id=1, source_target_pairs={{0,64},{64,128},{128,192},{192,256},{256,320},{320,384},{384,448},... | collective-permute-start | bytes 147464 | tf_op jit(solution)/shard_map/ppermute | solution.py:453
  70.3 0.1 collective-permute-done.5.after
  70.5 1.0 collective-permute-done.4.before
  71.5 0.1 shard_map.99
  71.6 3.0 %collective-permute-start.6 = (f32[64,128]{1,0:T(8,128)S(1)}, f32[64,128]{1,0:T(8,128)S(1)}, u32[]{:S(2)}, u32[]{:S(2)}) collective-permute-start(f32[64,128]{1,0:T(8,128)S(1)} %get-tuple-element.40), channel_id=1, source_target_pairs={{0,1},{1,2},{2,3},{3,4},{4,5},{5,6},{6,7},{7,8},{8,9},{9,10},{10,1... | collective-permute-start | bytes 98312 | tf_op jit(solution)/shard_map/ppermute | solution.py:453
  74.6 1.9 %collective-permute-start.7 = (f32[64,128]{1,0:T(8,128)S(1)}, f32[64,128]{1,0:T(8,128)S(1)}, u32[]{:S(2)}, u32[]{:S(2)}) collective-permute-start(f32[64,128]{1,0:T(8,128)S(1)} %get-tuple-element.41), channel_id=1, source_target_pairs={{1,0},{2,1},{3,2},{4,3},{5,4},{6,5},{7,6},{8,7},{9,8},{10,9},{11,1... | collective-permute-start | bytes 98312 | tf_op jit(solution)/shard_map/ppermute | solution.py:454
  76.6 0.0 collective-permute-done.6.refs_2_
  76.6 3.3 %collective-permute-done.7.refs_3_ = f32[64,128]{1,0:T(8,128)S(1)} collective-permute-done((f32[64,128]{1,0:T(8,128)S(1)}, f32[64,128]{1,0:T(8,128)S(1)}, u32[]{:S(2)}, u32[]{:S(2)}) %collective-permute-start.7) | collective-permute-done | bytes 32800 | tf_op jit(solution)/shard_map/ppermute | solution.py:454
  79.9 1.2 shard_map.100
  81.1 34.0 %all_to_all.21 = f32[512,1,128]{2,1,0:T(1,128)S(1)} all-to-all(f32[512,1,128]{2,1,0:T(1,128)S(1)} %bitcast.18), channel_id=1, replica_groups=mesh['gx'=8,'gy'=64] {'gx','gy'}, dimensions={0} | all-to-all | bytes 524288 | tf_op jit(solution)/shard_map/all_to_all | solution.py:460
  115.0 0.7 shard_map.101
  115.8 1.3 collective-permute-start.9
  117.1 4.0 %collective-permute-start.8 = (f32[24,384]{1,0:T(8,128)S(1)}, f32[24,384]{1,0:T(8,128)S(1)}, u32[]{:S(2)}, u32[]{:S(2)}) collective-permute-start(f32[24,384]{1,0:T(8,128)S(1)} %get-tuple-element.59), channel_id=1, source_target_pairs={{0,64},{64,128},{128,192},{192,256},{256,320},{320,384},{384,448},... | collective-permute-start | bytes 110600 | tf_op jit(solution)/shard_map/ppermute | solution.py:453
  121.1 0.0 collective-permute-done.9.after
  121.1 1.0 collective-permute-done.8.before
  122.1 0.1 shard_map.102
  122.2 3.0 %collective-permute-start.10 = (f32[48,128]{1,0:T(8,128)S(1)}, f32[48,128]{1,0:T(8,128)S(1)}, u32[]{:S(2)}, u32[]{:S(2)}) collective-permute-start(f32[48,128]{1,0:T(8,128)S(1)} %get-tuple-element.50), channel_id=1, source_target_pairs={{0,1},{1,2},{2,3},{3,4},{4,5},{5,6},{6,7},{7,8},{8,9},{9,10},{10,1... | collective-permute-start | bytes 73736 | tf_op jit(solution)/shard_map/ppermute | solution.py:453
  125.2 1.9 %collective-permute-start.11 = (f32[48,128]{1,0:T(8,128)S(1)}, f32[48,128]{1,0:T(8,128)S(1)}, u32[]{:S(2)}, u32[]{:S(2)}) collective-permute-start(f32[48,128]{1,0:T(8,128)S(1)} %get-tuple-element.51), channel_id=1, source_target_pairs={{1,0},{2,1},{3,2},{4,3},{5,4},{6,5},{7,6},{8,7},{9,8},{10,9},{11,1... | collective-permute-start | bytes 73736 | tf_op jit(solution)/shard_map/ppermute | solution.py:454
  127.2 0.0 collective-permute-done.10.from_left
  127.2 3.2 %collective-permute-done.11.from_right = f32[48,128]{1,0:T(8,128)S(1)} collective-permute-done((f32[48,128]{1,0:T(8,128)S(1)}, f32[48,128]{1,0:T(8,128)S(1)}, u32[]{:S(2)}, u32[]{:S(2)}) %collective-permute-start.11) | collective-permute-done | bytes 24608 | tf_op jit(solution)/shard_map/ppermute | solution.py:454
  130.4 0.3 shard_map.103
  130.7 13.0 %all_to_all.22 = f32[8,1,128]{2,1,0:T(1,128)S(1)} all-to-all(f32[8,1,128]{2,1,0:T(1,128)S(1)} %bitcast.23), channel_id=1, replica_groups=mesh['gx'=8,'gy'=64] {'gx'}, dimensions={0} | all-to-all | bytes 8192 | tf_op jit(solution)/shard_map/all_to_all | solution.py:460
  143.6 18.7 %all_to_all.23 = f32[64,1,128]{2,1,0:T(1,128)S(1)} all-to-all(f32[64,1,128]{2,1,0:T(1,128)S(1)} %bitcast.20), channel_id=1, replica_groups=mesh['gx'=8,'gy'=64] {'gy'}, dimensions={0} | all-to-all | bytes 65536 | tf_op jit(solution)/shard_map/all_to_all | solution.py:460
  162.4 0.9 shard_map.105
  (3 shorter events, 0.0 us)
Async XLA Ops:
  0.6 22.2 %copy-start = (f32[32,18432]{1,0:T(8,128)S(1)}, f32[32,18432]{1,0:T(8,128)}, u32[]{:S(2)}) copy-start(f32[32,18432]{1,0:T(8,128)} %refs_3_.3) | copy-start | bytes 7077892
  2.4 62.0 %copy-start.1 = (f32[32,16384]{1,0:T(8,128)S(1)}, f32[32,16384]{1,0:T(8,128)}, u32[]{:S(2)}) copy-start(f32[32,16384]{1,0:T(8,128)} %refs_2_.3) | copy-start | bytes 6291460
  2.4 6.1 %collective-permute-start = (f32[256,128]{1,0:T(8,128)S(1)}, f32[256,128]{1,0:T(8,128)S(1)}, u32[]{:S(2)}, u32[]{:S(2)}) collective-permute-start(f32[256,128]{1,0:T(8,128)S(1)} %get-tuple-element.31), channel_id=1, source_target_pairs={{0,64},{64,128},{128,192},{192,256},{256,320},{320,384},{384,448},... | collective-permute-start | bytes 393224 | tf_op jit(solution)/shard_map/ppermute | solution.py:453
  6.6 5.7 %collective-permute-start.1 = (f32[256,128]{1,0:T(8,128)S(1)}, f32[256,128]{1,0:T(8,128)S(1)}, u32[]{:S(2)}, u32[]{:S(2)}) collective-permute-start(f32[256,128]{1,0:T(8,128)S(1)} %get-tuple-element.32), channel_id=1, source_target_pairs={{64,0},{128,64},{192,128},{256,192},{320,256},{384,320},{448,384},... | collective-permute-start | bytes 393224 | tf_op jit(solution)/shard_map/ppermute | solution.py:454
  12.5 8.5 %collective-permute-start.2 = (f32[64,128]{1,0:T(8,128)S(1)}, f32[64,128]{1,0:T(8,128)S(1)}, u32[]{:S(2)}, u32[]{:S(2)}) collective-permute-start(f32[64,128]{1,0:T(8,128)S(1)} %get-tuple-element.34), channel_id=1, source_target_pairs={{0,1},{1,2},{2,3},{3,4},{4,5},{5,6},{6,7},{7,8},{8,9},{9,10},{10,1... | collective-permute-start | bytes 98312 | tf_op jit(solution)/shard_map/ppermute | solution.py:453
  17.6 5.2 %collective-permute-start.3 = (f32[64,128]{1,0:T(8,128)S(1)}, f32[64,128]{1,0:T(8,128)S(1)}, u32[]{:S(2)}, u32[]{:S(2)}) collective-permute-start(f32[64,128]{1,0:T(8,128)S(1)} %get-tuple-element.35), channel_id=1, source_target_pairs={{1,0},{2,1},{3,2},{4,3},{5,4},{6,5},{7,6},{8,7},{9,8},{10,9},{11,1... | collective-permute-start | bytes 98312 | tf_op jit(solution)/shard_map/ppermute | solution.py:454
  65.0 5.4 %collective-permute-start.5 = (f32[32,384]{1,0:T(8,128)S(1)}, f32[32,384]{1,0:T(8,128)S(1)}, u32[]{:S(2)}, u32[]{:S(2)}) collective-permute-start(f32[32,384]{1,0:T(8,128)S(1)} %get-tuple-element.60), channel_id=1, source_target_pairs={{64,0},{128,64},{192,128},{256,192},{320,256},{384,320},{448,384},... | collective-permute-start | bytes 147464 | tf_op jit(solution)/shard_map/ppermute | solution.py:454
  66.3 5.2 %collective-permute-start.4 = (f32[32,384]{1,0:T(8,128)S(1)}, f32[32,384]{1,0:T(8,128)S(1)}, u32[]{:S(2)}, u32[]{:S(2)}) collective-permute-start(f32[32,384]{1,0:T(8,128)S(1)} %get-tuple-element.61), channel_id=1, source_target_pairs={{0,64},{64,128},{128,192},{192,256},{256,320},{320,384},{384,448},... | collective-permute-start | bytes 147464 | tf_op jit(solution)/shard_map/ppermute | solution.py:453
  71.6 5.0 %collective-permute-start.6 = (f32[64,128]{1,0:T(8,128)S(1)}, f32[64,128]{1,0:T(8,128)S(1)}, u32[]{:S(2)}, u32[]{:S(2)}) collective-permute-start(f32[64,128]{1,0:T(8,128)S(1)} %get-tuple-element.40), channel_id=1, source_target_pairs={{0,1},{1,2},{2,3},{3,4},{4,5},{5,6},{6,7},{7,8},{8,9},{9,10},{10,1... | collective-permute-start | bytes 98312 | tf_op jit(solution)/shard_map/ppermute | solution.py:453
  74.6 5.2 %collective-permute-start.7 = (f32[64,128]{1,0:T(8,128)S(1)}, f32[64,128]{1,0:T(8,128)S(1)}, u32[]{:S(2)}, u32[]{:S(2)}) collective-permute-start(f32[64,128]{1,0:T(8,128)S(1)} %get-tuple-element.41), channel_id=1, source_target_pairs={{1,0},{2,1},{3,2},{4,3},{5,4},{6,5},{7,6},{8,7},{9,8},{10,9},{11,1... | collective-permute-start | bytes 98312 | tf_op jit(solution)/shard_map/ppermute | solution.py:454
  115.8 5.3 %collective-permute-start.9 = (f32[24,384]{1,0:T(8,128)S(1)}, f32[24,384]{1,0:T(8,128)S(1)}, u32[]{:S(2)}, u32[]{:S(2)}) collective-permute-start(f32[24,384]{1,0:T(8,128)S(1)} %get-tuple-element.58), channel_id=1, source_target_pairs={{64,0},{128,64},{192,128},{256,192},{320,256},{384,320},{448,384},... | collective-permute-start | bytes 110600 | tf_op jit(solution)/shard_map/ppermute | solution.py:454
  117.1 5.0 %collective-permute-start.8 = (f32[24,384]{1,0:T(8,128)S(1)}, f32[24,384]{1,0:T(8,128)S(1)}, u32[]{:S(2)}, u32[]{:S(2)}) collective-permute-start(f32[24,384]{1,0:T(8,128)S(1)} %get-tuple-element.59), channel_id=1, source_target_pairs={{0,64},{64,128},{128,192},{192,256},{256,320},{320,384},{384,448},... | collective-permute-start | bytes 110600 | tf_op jit(solution)/shard_map/ppermute | solution.py:453
  122.2 5.0 %collective-permute-start.10 = (f32[48,128]{1,0:T(8,128)S(1)}, f32[48,128]{1,0:T(8,128)S(1)}, u32[]{:S(2)}, u32[]{:S(2)}) collective-permute-start(f32[48,128]{1,0:T(8,128)S(1)} %get-tuple-element.50), channel_id=1, source_target_pairs={{0,1},{1,2},{2,3},{3,4},{4,5},{5,6},{6,7},{7,8},{8,9},{9,10},{10,1... | collective-permute-start | bytes 73736 | tf_op jit(solution)/shard_map/ppermute | solution.py:453
  125.2 5.1 %collective-permute-start.11 = (f32[48,128]{1,0:T(8,128)S(1)}, f32[48,128]{1,0:T(8,128)S(1)}, u32[]{:S(2)}, u32[]{:S(2)}) collective-permute-start(f32[48,128]{1,0:T(8,128)S(1)} %get-tuple-element.51), channel_id=1, source_target_pairs={{1,0},{2,1},{3,2},{4,3},{5,4},{6,5},{7,6},{8,7},{9,8},{10,9},{11,1... | collective-permute-start | bytes 73736 | tf_op jit(solution)/shard_map/ppermute | solution.py:454

commit v3 on v2

--- a/solution.py
+++ b/solution.py
@@ -49,6 +49,20 @@
 def own_mask(shape, first):
     rows, lanes = rows_of(shape) + first, lanes_of(shape)
     return (rows >= OV) & (rows < OV + CX) & (lanes >= OV) & (lanes < OV + CY)
+
+
+def is_even():
+    return lax.rem(lax.axis_index("gy"), 2) == 0
+
+
+def to_pairs(rightward, leftward):
+    even = is_even()
+    return jnp.where(even, leftward, rightward), jnp.where(even, rightward, leftward)
+
+
+def from_pairs(odd, even_pairs):
+    even = is_even()
+    return jnp.where(even, odd, even_pairs), jnp.where(even, even_pairs, odd)
 
 
 def total(x):
@@ -191,7 +205,7 @@
         behind[at : at + K, :] = head[:, cols] * live
 
 
-def pack_columns(held, before, after, rows, rightward, leftward):
+def pack_columns(held, before, after, rows, odd, even):
     lanes = lanes_of((PX, 128))
     to_right = to_left = None
     for f in range(5):
@@ -210,20 +224,20 @@
             first = pltpu.roll(first, STRIP * f, 1)
         to_right = last if f == 0 else to_right + last
         to_left = first if f == 0 else to_left + first
-    rightward[...] = to_right
-    leftward[...] = to_left
-
-
-def prepare(suby, counts, rows, from_left, from_right, basis, patch, coefs, solved, gather, tiles, flat):
+    odd[...], even[...] = to_pairs(to_right, to_left)
+
+
+def prepare(suby, counts, rows, odd, even, basis, patch, coefs, solved, gather, tiles, flat):
     zero = jnp.zeros((PX, LW - CY), f32)
     lanes = lanes_of((PX, 128))
+    from_left, from_right = from_pairs(odd[...], even[...])
     fields = []
     for f in range(5):
         middle = pltpu.roll(jnp.concatenate([rows[f], zero], axis=1), OV, 1)
         band = (lanes >= STRIP * f) & (lanes < STRIP * f + 17)
         wide = jnp.zeros((PX, LW - 128), f32)
-        one = jnp.concatenate([jnp.where(band, from_left[...], 0.0), wide], axis=1)
-        two = jnp.concatenate([jnp.where(band, from_right[...], 0.0), wide], axis=1)
+        one = jnp.concatenate([jnp.where(band, from_left, 0.0), wide], axis=1)
+        two = jnp.concatenate([jnp.where(band, from_right, 0.0), wide], axis=1)
         one = pltpu.roll(one, LW - 1 - STRIP * f, 1)
         two = pltpu.roll(two, OV + CY - STRIP * f, 1)
         fields.append(middle + one + two)
@@ -277,7 +291,7 @@
     part[8:56, :] = part[8:56, :] + solved[...] * scale
 
 
-def fold_rows(part, before, after, folded, rightward, leftward):
+def fold_rows(part, before, after, folded, odd, even):
     height = folded.shape[0]
     first = (PX - height) // 2
     half = height // 2
@@ -289,23 +303,25 @@
     folded[...] = whole
     lanes = lanes_of((height, 128))
     moved = pltpu.roll(whole, LW - 255, 1)
-    rightward[...] = jnp.where(lanes < 33, moved[:, :128], 0.0)
-    leftward[...] = jnp.where(lanes < 33, whole[:, :128], 0.0)
-
-
-def folded_columns(folded, from_left, from_right):
+    odd[...], even[...] = to_pairs(
+        jnp.where(lanes < 33, moved[:, :128], 0.0), jnp.where(lanes < 33, whole[:, :128], 0.0)
+    )
+
+
+def folded_columns(folded, odd, even):
     height = folded.shape[0]
     zero = jnp.zeros((height, 256), f32)
-    one = pltpu.roll(jnp.concatenate([from_left[...], zero], axis=1), LW - 1, 1)
-    two = jnp.concatenate([zero, from_right[...]], axis=1)
+    from_left, from_right = from_pairs(odd[...], even[...])
+    one = pltpu.roll(jnp.concatenate([from_left, zero], axis=1), LW - 1, 1)
+    two = jnp.concatenate([zero, from_right], axis=1)
     return folded[...] + one + two
 
 
 def apply_first(
-    suby, counts, folded, from_left, from_right, coefs, patch, scalars, basis, before, after,
+    suby, counts, folded, odd, even, coefs, patch, scalars, basis, before, after,
     direction, image, solved, gather, tiles, flat,
 ):
-    field = folded_columns(folded, from_left, from_right)
+    field = folded_columns(folded, odd, even)
     direction[...] = field[OV : OV + CX]
     diagonal = coefs[0]
     faces = [coefs[1 + f] for f in range(4)]
@@ -362,9 +378,9 @@
 
 
 def apply_second(
-    folded, from_left, from_right, coefs, patch, image, scalars, direction, third, gather
+    folded, odd, even, coefs, patch, image, scalars, direction, third, gather
 ):
-    field = folded_columns(folded, from_left, from_right)
+    field = folded_columns(folded, odd, even)
     vector = operate(field, coefs[0, 8:56, :], [coefs[1 + f, 8:56, :] for f in range(4)])
     own = own_mask((CX, LW), OV)
     direction[...] = field[8 : 8 + CX]
@@ -455,6 +471,15 @@
     return before, after
 
 
+def swap_columns(odd, even):
+    count = lax.axis_size("gy")
+    inside = [(i, i ^ 1) for i in range(count)]
+    across = [(i, i + 1 if i % 2 else i - 1) for i in range(1, count - 1)]
+    even = lax.ppermute(even, "gy", inside)
+    odd = lax.ppermute(odd, "gy", across)
+    return odd, even
+
+
 def everywhere(rows, axes=AXES):
     count = rows.shape[0]
     return lax.all_to_all(rows.reshape(count, 1, 128), axes, 0, 0).reshape(count, 128)
@@ -489,16 +514,16 @@
     )(counts, *[pltpu.with_memory_space_constraint(x, pltpu.HBM) for x in (*fields, basis)])
     before, after = swap("gx", ahead, behind)
     strip = shape_of(PX, 128)
-    grown, rightward, leftward = kernel(pack_columns, [shape_of(5, PX, CY), strip, strip])(
+    grown, odd, even = kernel(pack_columns, [shape_of(5, PX, CY), strip, strip])(
         held, before, after
     )
-    from_left, from_right = swap("gy", rightward, leftward)
+    odd, even = swap_columns(odd, even)
     patch, coefs, solved_one, row = kernel(
         bind(prepare),
         [patch_shape, shape_of(5, PX, LW), shape_of(48, LW), rows],
         [tiles, flat],
         True,
-    )(counts, grown, from_left, from_right, basis)
+    )(counts, grown, odd, even, basis)
     part, weights, scalars_one = kernel(
         bind(spread_first),
         [patch_shape, shape_of(K, 128), shape_of(8, 128)],
@@ -506,15 +531,15 @@
         True,
     )(counts, everywhere(row), coarse_inverse, basis, solved_one)
     over, under = swap("gx", part[PX // 2 :], part[: PX // 2])
-    folded, rightward, leftward = kernel(fold_rows, [patch_shape, strip, strip])(part, over, under)
-    from_left, from_right = swap("gy", rightward, leftward)
+    folded, odd, even = kernel(fold_rows, [patch_shape, strip, strip])(part, over, under)
+    odd, even = swap_columns(odd, even)
     direction_one, image_one, solved_two, row = kernel(
         bind(apply_first),
         [own_shape, own_shape, shape_of(48, LW), rows],
         [tiles, flat],
         True,
     )(
-        counts, folded, from_left, from_right, coefs, patch, scalars_one, basis, before, after
+        counts, folded, odd, even, coefs, patch, scalars_one, basis, before, after
     )
     part, scalars_two = kernel(
         bind(spread_second),
@@ -526,14 +551,14 @@
     )
     over, under = swap("gx", part[40:], part[:24])
     strip = shape_of(48, 128)
-    folded, rightward, leftward = kernel(fold_rows, [shape_of(48, LW), strip, strip])(
+    folded, odd, even = kernel(fold_rows, [shape_of(48, LW), strip, strip])(
         part, over, under
     )
-    from_left, from_right = swap("gy", rightward, leftward)
+    odd, even = swap_columns(odd, even)
     direction_two, image_two, row = kernel(
         apply_second, [own_shape, own_shape, shape_of(devices // suby, 128)]
     )(
-        folded, from_left, from_right, coefs, patch, image_one, scalars_two
+        folded, odd, even, coefs, patch, image_one, scalars_two
     )
     (row,) = kernel(add_rows, [shape_of(suby, 128)])(everywhere(row, "gx"))
     out = shape_of(CX, CY)

time: 164 us -> 152 us (0.927)
  blocking collectives: 106 us -> 100 us
  waiting for transfers between devices: 14.9 us -> 9.77 us
    ppermute x0 -> x6, starting transfers between devices: none -> 17.8 us  [the longest x3 11.2 us: swap_columns(): odd = lax.ppermute(odd, 'gy', across)]
    ppermute x6 -> x3, starting transfers between devices: 23.3 us -> 12.1 us  [swap(): before = lax.ppermute(forward, axis, [(i, i + 1) for i in range(count - 1)])]
    ppermute x6 -> x3, waiting for transfers between devices: 12.2 us -> 3.9 us  [swap(): after = lax.ppermute(backward, axis, [(i + 1, i) for i in range(count - 1)])]
    ppermute x6 -> x3, starting transfers between devices: 11.1 us -> 3.88 us  [swap(): after = lax.ppermute(backward, axis, [(i + 1, i) for i in range(count - 1)])]
    all_to_all x4, blocking collectives: 106 us -> 100 us  [everywhere(): lax.all_to_all(rows.reshape(count, 1, 128), axes, 0, 0).reshape(count, 128)]
    ppermute x0 -> x6, waiting for transfers between devices: none -> 3.16 us  [the longest x3 2.73 us: swap_columns(): even = lax.ppermute(even, 'gy', inside)]
  transfers between devices with their start and end apart: 12 -> 12, of which waited for: 8 -> 10; matrix products, arithmetic and copies ran while one was open for 0% -> 0% of each run, Pallas kernels for 0% -> 0%
where the time goes in v3:
time: 152 us
  blocking collectives  100 us (66%)
  starting transfers between devices  33.8 us (22%)
  waiting for transfers between devices  9.77 us (6%)
  Pallas kernels  6.29 us (4%)
  between operations  1.62 us (1%)
    all_to_all x4, blocking collectives, everywhere(): lax.all_to_all(rows.reshape(count, 1, 128), axes, 0, 0).reshape(count, 128)  100 us
    ppermute x3, starting transfers between devices, swap(): before = lax.ppermute(forward, axis, [(i, i + 1) for i in range(count - 1)])  12.1 us
    ppermute x3, starting transfers between devices, swap_columns(): odd = lax.ppermute(odd, 'gy', across)  11.2 us
    ppermute x3, starting transfers between devices, swap_columns(): even = lax.ppermute(even, 'gy', inside)  6.59 us
    pallas_call x10, Pallas kernels, call(): pl.pallas_call(body, out_shape=outs, in_specs=specs, out_specs=[VMEM] * l...  5.3 us
    ppermute x3, waiting for transfers between devices, swap(): after = lax.ppermute(backward, axis, [(i + 1, i) for i in range(count - 1)])  3.9 us
    ppermute x3, starting transfers between devices, swap(): after = lax.ppermute(backward, axis, [(i + 1, i) for i in range(count - 1)])  3.88 us
  transfers between devices with their start and end apart: 12, of which 10 were waited for; matrix products, arithmetic and copies ran while one was open for 0% of the time, Pallas kernels for 0%

profile of v3, /device:TPU:1, one launch (start us, length us, event | category | flops | bytes accessed | tf_op | source)
XLA Modules:
  0.0 151.7 jit_solution(10852056022725459879)
XLA Ops:
  0.6 0.0 copy-start
  1.4 1.0 shard_map.95
  2.4 0.0 copy-start.1
  2.4 4.2 %collective-permute-start = (f32[256,128]{1,0:T(8,128)S(1)}, f32[256,128]{1,0:T(8,128)S(1)}, u32[]{:S(2)}, u32[]{:S(2)}) collective-permute-start(f32[256,128]{1,0:T(8,128)S(1)} %get-tuple-element.31), channel_id=1, source_target_pairs={{0,64},{64,128},{128,192},{192,256},{256,320},{320,384},{384,448},... | collective-permute-start | bytes 393224 | tf_op jit(solution)/shard_map/ppermute | solution.py:469
  6.6 1.3 collective-permute-start.1
  7.9 0.6 collective-permute-done.before.refs_8_
  8.5 3.8 %collective-permute-done.1.after.refs_9_ = f32[256,128]{1,0:T(8,128)S(1)} collective-permute-done((f32[256,128]{1,0:T(8,128)S(1)}, f32[256,128]{1,0:T(8,128)S(1)}, u32[]{:S(2)}, u32[]{:S(2)}) %collective-permute-start.1) | collective-permute-done | bytes 131104 | tf_op jit(solution)/shard_map/ppermute | solution.py:470
  12.3 0.1 shard_map.96
  12.5 5.1 %collective-permute-start.2 = (f32[64,128]{1,0:T(8,128)S(1)}, f32[64,128]{1,0:T(8,128)S(1)}, u32[]{:S(2)}, u32[]{:S(2)}) collective-permute-start(f32[64,128]{1,0:T(8,128)S(1)} %get-tuple-element.34), channel_id=1, source_target_pairs={{1,2},{2,1},{3,4},{4,3},{5,6},{6,5},{7,8},{8,7},{9,10},{10,9},{11,... | collective-permute-start | bytes 98312 | tf_op jit(solution)/shard_map/ppermute | solution.py:479
  17.6 2.8 %collective-permute-start.3 = (f32[64,128]{1,0:T(8,128)S(1)}, f32[64,128]{1,0:T(8,128)S(1)}, u32[]{:S(2)}, u32[]{:S(2)}) collective-permute-start(f32[64,128]{1,0:T(8,128)S(1)} %get-tuple-element.35), channel_id=1, source_target_pairs={{0,1},{1,0},{2,3},{3,2},{4,5},{5,4},{6,7},{7,6},{8,9},{9,8},{10,11... | collective-permute-start | bytes 98312 | tf_op jit(solution)/shard_map/ppermute | solution.py:478
  20.4 0.0 collective-permute-done.2.refs_2_
  20.4 0.8 collective-permute-done.3.refs_3_
  21.2 0.0 copy-done
  21.2 1.3 shard_map.97
  22.5 37.5 %all_to_all.20 = f32[512,1,128]{2,1,0:T(1,128)S(1)} all-to-all(f32[512,1,128]{2,1,0:T(1,128)S(1)} %bitcast.19), channel_id=1, replica_groups=mesh['gx'=8,'gy'=64] {'gx','gy'}, dimensions={0} | all-to-all | bytes 524288 | tf_op jit(solution)/shard_map/all_to_all | solution.py:485
  60.1 0.0 copy-done.1
  60.1 0.6 shard_map.98
  60.7 1.3 collective-permute-start.5
  62.0 4.0 %collective-permute-start.4 = (f32[32,384]{1,0:T(8,128)S(1)}, f32[32,384]{1,0:T(8,128)S(1)}, u32[]{:S(2)}, u32[]{:S(2)}) collective-permute-start(f32[32,384]{1,0:T(8,128)S(1)} %get-tuple-element.61), channel_id=1, source_target_pairs={{0,64},{64,128},{128,192},{192,256},{256,320},{320,384},{384,448},... | collective-permute-start | bytes 147464 | tf_op jit(solution)/shard_map/ppermute | solution.py:469
  66.0 0.1 collective-permute-done.5.after
  66.1 1.0 collective-permute-done.4.before
  67.2 0.1 shard_map.99
  67.3 3.0 %collective-permute-start.6 = (f32[64,128]{1,0:T(8,128)S(1)}, f32[64,128]{1,0:T(8,128)S(1)}, u32[]{:S(2)}, u32[]{:S(2)}) collective-permute-start(f32[64,128]{1,0:T(8,128)S(1)} %get-tuple-element.40), channel_id=1, source_target_pairs={{1,2},{2,1},{3,4},{4,3},{5,6},{6,5},{7,8},{8,7},{9,10},{10,9},{11,... | collective-permute-start | bytes 98312 | tf_op jit(solution)/shard_map/ppermute | solution.py:479
  70.3 1.9 %collective-permute-start.7 = (f32[64,128]{1,0:T(8,128)S(1)}, f32[64,128]{1,0:T(8,128)S(1)}, u32[]{:S(2)}, u32[]{:S(2)}) collective-permute-start(f32[64,128]{1,0:T(8,128)S(1)} %get-tuple-element.41), channel_id=1, source_target_pairs={{0,1},{1,0},{2,3},{3,2},{4,5},{5,4},{6,7},{7,6},{8,9},{9,8},{10,11... | collective-permute-start | bytes 98312 | tf_op jit(solution)/shard_map/ppermute | solution.py:478
  72.3 0.3 collective-permute-done.6.refs_2_
  72.5 0.9 collective-permute-done.7.refs_3_
  73.4 1.2 shard_map.100
  74.6 31.8 %all_to_all.21 = f32[512,1,128]{2,1,0:T(1,128)S(1)} all-to-all(f32[512,1,128]{2,1,0:T(1,128)S(1)} %bitcast.18), channel_id=1, replica_groups=mesh['gx'=8,'gy'=64] {'gx','gy'}, dimensions={0} | all-to-all | bytes 524288 | tf_op jit(solution)/shard_map/all_to_all | solution.py:485
  106.4 0.7 shard_map.101
  107.1 1.3 collective-permute-start.9
  108.4 4.0 %collective-permute-start.8 = (f32[24,384]{1,0:T(8,128)S(1)}, f32[24,384]{1,0:T(8,128)S(1)}, u32[]{:S(2)}, u32[]{:S(2)}) collective-permute-start(f32[24,384]{1,0:T(8,128)S(1)} %get-tuple-element.59), channel_id=1, source_target_pairs={{0,64},{64,128},{128,192},{192,256},{256,320},{320,384},{384,448},... | collective-permute-start | bytes 110600 | tf_op jit(solution)/shard_map/ppermute | solution.py:469
  112.4 0.0 collective-permute-done.9.after
  112.5 1.0 collective-permute-done.8.before
  113.5 0.1 shard_map.102
  113.6 3.0 %collective-permute-start.10 = (f32[48,128]{1,0:T(8,128)S(1)}, f32[48,128]{1,0:T(8,128)S(1)}, u32[]{:S(2)}, u32[]{:S(2)}) collective-permute-start(f32[48,128]{1,0:T(8,128)S(1)} %get-tuple-element.50), channel_id=1, source_target_pairs={{1,2},{2,1},{3,4},{4,3},{5,6},{6,5},{7,8},{8,7},{9,10},{10,9},{11,... | collective-permute-start | bytes 73736 | tf_op jit(solution)/shard_map/ppermute | solution.py:479
  116.6 1.9 %collective-permute-start.11 = (f32[48,128]{1,0:T(8,128)S(1)}, f32[48,128]{1,0:T(8,128)S(1)}, u32[]{:S(2)}, u32[]{:S(2)}) collective-permute-start(f32[48,128]{1,0:T(8,128)S(1)} %get-tuple-element.51), channel_id=1, source_target_pairs={{0,1},{1,0},{2,3},{3,2},{4,5},{5,4},{6,7},{7,6},{8,9},{9,8},{10,11... | collective-permute-start | bytes 73736 | tf_op jit(solution)/shard_map/ppermute | solution.py:478
  118.5 0.2 collective-permute-done.10.odd
  118.7 1.0 collective-permute-done.11.even
  119.7 0.3 shard_map.103
  120.0 13.0 %all_to_all.22 = f32[8,1,128]{2,1,0:T(1,128)S(1)} all-to-all(f32[8,1,128]{2,1,0:T(1,128)S(1)} %bitcast.23), channel_id=1, replica_groups=mesh['gx'=8,'gy'=64] {'gx'}, dimensions={0} | all-to-all | bytes 8192 | tf_op jit(solution)/shard_map/all_to_all | solution.py:485
  133.0 17.9 %all_to_all.23 = f32[64,1,128]{2,1,0:T(1,128)S(1)} all-to-all(f32[64,1,128]{2,1,0:T(1,128)S(1)} %bitcast.20), channel_id=1, replica_groups=mesh['gx'=8,'gy'=64] {'gy'}, dimensions={0} | all-to-all | bytes 65536 | tf_op jit(solution)/shard_map/all_to_all | solution.py:485
  150.9 0.9 shard_map.105
  (3 shorter events, 0.0 us)
Async XLA Ops:
  0.6 20.6 %copy-start = (f32[32,18432]{1,0:T(8,128)S(1)}, f32[32,18432]{1,0:T(8,128)}, u32[]{:S(2)}) copy-start(f32[32,18432]{1,0:T(8,128)} %refs_3_.3) | copy-start | bytes 7077892
  2.4 57.6 %copy-start.1 = (f32[32,16384]{1,0:T(8,128)S(1)}, f32[32,16384]{1,0:T(8,128)}, u32[]{:S(2)}) copy-start(f32[32,16384]{1,0:T(8,128)} %refs_2_.3) | copy-start | bytes 6291460
  2.4 6.1 %collective-permute-start = (f32[256,128]{1,0:T(8,128)S(1)}, f32[256,128]{1,0:T(8,128)S(1)}, u32[]{:S(2)}, u32[]{:S(2)}) collective-permute-start(f32[256,128]{1,0:T(8,128)S(1)} %get-tuple-element.31), channel_id=1, source_target_pairs={{0,64},{64,128},{128,192},{192,256},{256,320},{320,384},{384,448},... | collective-permute-start | bytes 393224 | tf_op jit(solution)/shard_map/ppermute | solution.py:469
  6.6 5.7 %collective-permute-start.1 = (f32[256,128]{1,0:T(8,128)S(1)}, f32[256,128]{1,0:T(8,128)S(1)}, u32[]{:S(2)}, u32[]{:S(2)}) collective-permute-start(f32[256,128]{1,0:T(8,128)S(1)} %get-tuple-element.32), channel_id=1, source_target_pairs={{64,0},{128,64},{192,128},{256,192},{320,256},{384,320},{448,384},... | collective-permute-start | bytes 393224 | tf_op jit(solution)/shard_map/ppermute | solution.py:470
  12.5 7.9 %collective-permute-start.2 = (f32[64,128]{1,0:T(8,128)S(1)}, f32[64,128]{1,0:T(8,128)S(1)}, u32[]{:S(2)}, u32[]{:S(2)}) collective-permute-start(f32[64,128]{1,0:T(8,128)S(1)} %get-tuple-element.34), channel_id=1, source_target_pairs={{1,2},{2,1},{3,4},{4,3},{5,6},{6,5},{7,8},{8,7},{9,10},{10,9},{11,... | collective-permute-start | bytes 98312 | tf_op jit(solution)/shard_map/ppermute | solution.py:479
  17.6 3.6 %collective-permute-start.3 = (f32[64,128]{1,0:T(8,128)S(1)}, f32[64,128]{1,0:T(8,128)S(1)}, u32[]{:S(2)}, u32[]{:S(2)}) collective-permute-start(f32[64,128]{1,0:T(8,128)S(1)} %get-tuple-element.35), channel_id=1, source_target_pairs={{0,1},{1,0},{2,3},{3,2},{4,5},{5,4},{6,7},{7,6},{8,9},{9,8},{10,11... | collective-permute-start | bytes 98312 | tf_op jit(solution)/shard_map/ppermute | solution.py:478
  60.7 5.4 %collective-permute-start.5 = (f32[32,384]{1,0:T(8,128)S(1)}, f32[32,384]{1,0:T(8,128)S(1)}, u32[]{:S(2)}, u32[]{:S(2)}) collective-permute-start(f32[32,384]{1,0:T(8,128)S(1)} %get-tuple-element.60), channel_id=1, source_target_pairs={{64,0},{128,64},{192,128},{256,192},{320,256},{384,320},{448,384},... | collective-permute-start | bytes 147464 | tf_op jit(solution)/shard_map/ppermute | solution.py:470
  62.0 5.2 %collective-permute-start.4 = (f32[32,384]{1,0:T(8,128)S(1)}, f32[32,384]{1,0:T(8,128)S(1)}, u32[]{:S(2)}, u32[]{:S(2)}) collective-permute-start(f32[32,384]{1,0:T(8,128)S(1)} %get-tuple-element.61), channel_id=1, source_target_pairs={{0,64},{64,128},{128,192},{192,256},{256,320},{320,384},{384,448},... | collective-permute-start | bytes 147464 | tf_op jit(solution)/shard_map/ppermute | solution.py:469
  67.3 5.2 %collective-permute-start.6 = (f32[64,128]{1,0:T(8,128)S(1)}, f32[64,128]{1,0:T(8,128)S(1)}, u32[]{:S(2)}, u32[]{:S(2)}) collective-permute-start(f32[64,128]{1,0:T(8,128)S(1)} %get-tuple-element.40), channel_id=1, source_target_pairs={{1,2},{2,1},{3,4},{4,3},{5,6},{6,5},{7,8},{8,7},{9,10},{10,9},{11,... | collective-permute-start | bytes 98312 | tf_op jit(solution)/shard_map/ppermute | solution.py:479
  70.3 3.1 %collective-permute-start.7 = (f32[64,128]{1,0:T(8,128)S(1)}, f32[64,128]{1,0:T(8,128)S(1)}, u32[]{:S(2)}, u32[]{:S(2)}) collective-permute-start(f32[64,128]{1,0:T(8,128)S(1)} %get-tuple-element.41), channel_id=1, source_target_pairs={{0,1},{1,0},{2,3},{3,2},{4,5},{5,4},{6,7},{7,6},{8,9},{9,8},{10,11... | collective-permute-start | bytes 98312 | tf_op jit(solution)/shard_map/ppermute | solution.py:478
  107.1 5.3 %collective-permute-start.9 = (f32[24,384]{1,0:T(8,128)S(1)}, f32[24,384]{1,0:T(8,128)S(1)}, u32[]{:S(2)}, u32[]{:S(2)}) collective-permute-start(f32[24,384]{1,0:T(8,128)S(1)} %get-tuple-element.58), channel_id=1, source_target_pairs={{64,0},{128,64},{192,128},{256,192},{320,256},{384,320},{448,384},... | collective-permute-start | bytes 110600 | tf_op jit(solution)/shard_map/ppermute | solution.py:470
  108.4 5.0 %collective-permute-start.8 = (f32[24,384]{1,0:T(8,128)S(1)}, f32[24,384]{1,0:T(8,128)S(1)}, u32[]{:S(2)}, u32[]{:S(2)}) collective-permute-start(f32[24,384]{1,0:T(8,128)S(1)} %get-tuple-element.59), channel_id=1, source_target_pairs={{0,64},{64,128},{128,192},{192,256},{256,320},{320,384},{384,448},... | collective-permute-start | bytes 110600 | tf_op jit(solution)/shard_map/ppermute | solution.py:469
  113.6 5.1 %collective-permute-start.10 = (f32[48,128]{1,0:T(8,128)S(1)}, f32[48,128]{1,0:T(8,128)S(1)}, u32[]{:S(2)}, u32[]{:S(2)}) collective-permute-start(f32[48,128]{1,0:T(8,128)S(1)} %get-tuple-element.50), channel_id=1, source_target_pairs={{1,2},{2,1},{3,4},{4,3},{5,6},{6,5},{7,8},{8,7},{9,10},{10,9},{11,... | collective-permute-start | bytes 73736 | tf_op jit(solution)/shard_map/ppermute | solution.py:479
  116.6 3.1 %collective-permute-start.11 = (f32[48,128]{1,0:T(8,128)S(1)}, f32[48,128]{1,0:T(8,128)S(1)}, u32[]{:S(2)}, u32[]{:S(2)}) collective-permute-start(f32[48,128]{1,0:T(8,128)S(1)} %get-tuple-element.51), channel_id=1, source_target_pairs={{0,1},{1,0},{2,3},{3,2},{4,5},{5,4},{6,7},{7,6},{8,9},{9,8},{10,11... | collective-permute-start | bytes 73736 | tf_op jit(solution)/shard_map/ppermute | solution.py:478

commit v4 on v3

--- a/solution.py
+++ b/solution.py
@@ -139,6 +139,38 @@
     return jnp.sum(taken[0] + taken[1] + (taken[2] + taken[3]), axis=0, keepdims=True)
 
 
+def compact(rows, gather):
+    count = rows.shape[0] // 4
+    slot = slot_rows(rows.shape[0])
+    taken = [rows[pl.ds(q, count, stride=4), :] for q in range(4)]
+    lanes = lanes_of((count, 128))
+    result = None
+    for q in range(4):
+        piece = jnp.where(lanes < 32, taken[q], 0.0)
+        if q:
+            piece = pltpu.roll(piece, 32 * q, 1)
+        result = piece if result is None else result + piece
+    sums = jnp.sum(taken[0] + taken[1] + (taken[2] + taken[3]), axis=0, keepdims=True)
+    tail = jnp.broadcast_to(sums, (slot - count, 128))
+    block = jnp.concatenate([result, tail], axis=0)
+    for at in range(0, gather.shape[0], slot):
+        gather[at : at + slot, :] = block
+
+
+def slot_rows(suby):
+    return suby // 4 + 8
+
+
+def unpacked(rows, coarse, suby):
+    count, slot = suby // 4, slot_rows(suby)
+    sums = None
+    for i in range(rows.shape[0] // slot):
+        coarse[i * count : (i + 1) * count, :] = rows[i * slot : i * slot + count, :]
+        row = rows[i * slot + count : i * slot + count + 1, :]
+        sums = row if sums is None else sums + row
+    return sums
+
+
 def pick(row, lane):
     return jnp.sum(jnp.where(lanes_of(row.shape) == lane, row, 0.0), axis=1, keepdims=True)
 
@@ -149,10 +181,6 @@
         row = jnp.broadcast_to(coarse[pl.ds(b, 1), :], (K, 128))
         sums[b % 4] = sums[b % 4] + inverse[:, b * 128 : (b + 1) * 128] * row
     return jnp.sum((sums[0] + sums[1]) + (sums[2] + sums[3]), axis=1, keepdims=True)
-
-
-def live_of(counts):
-    return (rows_of((K, 1)) < counts[0, 0]).astype(f32)
 
 
 def relax(vector, diagonal, faces):
@@ -175,7 +203,7 @@
 
 
 def pack_rows(
-    counts, source, potential, along, across, recombination, basis, held, ahead, behind,
+    counts, source, potential, along, across, recombination, basis, held, ahead, behind, live_out,
     head, tail, sems,
 ):
     edge = head.shape[1]
@@ -189,9 +217,10 @@
     )
     for copy in copies:
         copy.start()
-    live = live_of(counts)
     for copy in copies:
         copy.wait()
+    live = (rows_of((K, 128)) < counts[0, 0]).astype(f32)
+    live_out[...] = live
     for f in range(5):
         for t in range(2):
             at = (2 * f + t) * OV
@@ -227,7 +256,7 @@
     odd[...], even[...] = to_pairs(to_right, to_left)
 
 
-def prepare(suby, counts, rows, odd, even, basis, patch, coefs, solved, gather, tiles, flat):
+def prepare(suby, live, rows, odd, even, basis, patch, coefs, solved, gather, tiles, flat):
     zero = jnp.zeros((PX, LW - CY), f32)
     lanes = lanes_of((PX, 128))
     from_left, from_right = from_pairs(odd[...], even[...])
@@ -262,7 +291,7 @@
     square = total(jnp.where(own, source * source, 0.0))
     local = relax(source[8:56], diagonal[8:56], [face[8:56] for face in faces])
     solved[...] = jnp.where(own_mask((48, LW), 8), local, 0.0)
-    residual = restrict(basis, source, tiles, flat) * live_of(counts)
+    residual = restrict(basis, source, tiles, flat) * live[:, 0:1]
     row = to_row(residual)
     row = jnp.where(lanes_of((1, 128)) == SCALARS, square, row)
     gather[...] = jnp.broadcast_to(row, gather.shape)
@@ -277,13 +306,13 @@
 
 
 def spread_first(
-    suby, counts, rows, inverse, basis, solved, part, weights, scalars, coarse, tiles, flat
+    suby, live, rows, inverse, basis, solved, part, weights, scalars, coarse, tiles, flat
 ):
-    sums = gathered(rows, coarse, suby)
+    sums = unpacked(rows, coarse, suby)
     square = pick(sums, SCALARS)
     norm = jnp.sqrt(square + EPSILON)
     scale = 1.0 / norm
-    solution = coarse_solve(inverse, coarse) * live_of(counts) * scale
+    solution = coarse_solve(inverse, coarse) * live[:, 0:1] * scale
     weights[...] = jnp.broadcast_to(solution, (K, 128))
     put(scalars, 0, norm)
     put(scalars, 1, square / (square + EPSILON))
@@ -318,7 +347,7 @@
 
 
 def apply_first(
-    suby, counts, folded, odd, even, coefs, patch, scalars, basis, before, after,
+    suby, live, folded, odd, even, coefs, patch, scalars, basis, before, after,
     direction, image, solved, gather, tiles, flat,
 ):
     field = folded_columns(folded, odd, even)
@@ -337,7 +366,7 @@
     square = total(mine * mine)
     local = relax(vector[8:56], diagonal[8:56], [face[8:56] for face in faces])
     solved[...] = jnp.where(own_mask((48, LW), 8), local, 0.0)
-    residual = restrict(basis, vector, tiles, flat) * live_of(counts)
+    residual = restrict(basis, vector, tiles, flat) * live[:, 0:1]
     fourth = vector[32:40]
     third = pltpu.roll(vector[24:32], 96, 1)
     for_next = for_before = jnp.zeros((K, 128), f32)
@@ -355,7 +384,7 @@
 
 
 def spread_second(
-    suby, counts, rows, inverse, basis, solved_first, solved, weights, scalars_in,
+    suby, live, rows, inverse, basis, solved_first, solved, weights, scalars_in,
     part, scalars, coarse, tiles, flat,
 ):
     sums = gathered(rows, coarse, suby)
@@ -366,7 +395,7 @@
     rest = square - 2.0 * cross * cross + cross * cross * unit
     second = jnp.sqrt(jnp.maximum(rest, 0.0) + EPSILON)
     scale = 1.0 / second
-    solution = coarse_solve(inverse, coarse) * live_of(counts)
+    solution = coarse_solve(inverse, coarse) * live[:, 0:1]
     solution = (solution - cross * weights[:, 0:1]) * scale
     put(scalars, 0, norm)
     put(scalars, 1, unit)
@@ -443,19 +472,15 @@
 
 
 VMEM = pl.BlockSpec(memory_space=pltpu.VMEM)
-SMEM = pl.BlockSpec(memory_space=pltpu.SMEM)
 PARAMS = pltpu.CompilerParams(vmem_limit_bytes=24 * 1024 * 1024)
 
 
-def kernel(body, outs, scratch=(), first_smem=False):
+def kernel(body, outs, scratch=()):
     def call(*args):
-        specs = [VMEM] * len(args)
-        if first_smem:
-            specs[0] = SMEM
         return pl.pallas_call(
             body,
             out_shape=outs,
-            in_specs=specs,
+            in_specs=[VMEM] * len(args),
             out_specs=[VMEM] * len(outs),
             scratch_shapes=list(scratch),
             compiler_params=PARAMS,
@@ -481,8 +506,9 @@
 
 
 def everywhere(rows, axes=AXES):
-    count = rows.shape[0]
-    return lax.all_to_all(rows.reshape(count, 1, 128), axes, 0, 0).reshape(count, 128)
+    count = lax.axis_size(axes)
+    slots = rows.reshape(count, rows.shape[0] // count, 128)
+    return lax.all_to_all(slots, axes, 0, 0).reshape(rows.shape)
 
 
 def on_device(
@@ -504,12 +530,17 @@
         return run
 
     edge = pltpu.VMEM((K, 3 * 128), f32)
-    held, ahead, behind = pl.pallas_call(
+    held, ahead, behind, live = pl.pallas_call(
         pack_rows,
-        out_shape=[shape_of(5, CX, CY), shape_of(256, 128), shape_of(256, 128)],
-        in_specs=[SMEM] + [pl.BlockSpec(memory_space=pltpu.HBM)] * 6,
-        out_specs=[VMEM] * 3,
-        scratch_shapes=[edge, edge, pltpu.SemaphoreType.DMA((7,))],
+        out_shape=[
+            shape_of(5, CX, CY), shape_of(256, 128), shape_of(256, 128), shape_of(K, 128)
+        ],
+        in_specs=[pl.BlockSpec(memory_space=pltpu.SMEM)]
+        + [pl.BlockSpec(memory_space=pltpu.HBM)] * 6,
+        out_specs=[VMEM] * 4,
+        scratch_shapes=[
+            edge, edge, pltpu.SemaphoreType.DMA((7,))
+        ],
         compiler_params=PARAMS,
     )(counts, *[pltpu.with_memory_space_constraint(x, pltpu.HBM) for x in (*fields, basis)])
     before, after = swap("gx", ahead, behind)
@@ -520,16 +551,17 @@
     odd, even = swap_columns(odd, even)
     patch, coefs, solved_one, row = kernel(
         bind(prepare),
-        [patch_shape, shape_of(5, PX, LW), shape_of(48, LW), rows],
+        [patch_shape, shape_of(5, PX, LW), shape_of(48, LW), shape_of(suby, 128)],
         [tiles, flat],
-        True,
-    )(counts, grown, odd, even, basis)
+    )(live, grown, odd, even, basis)
+    (row,) = kernel(compact, [shape_of(devices // suby * slot_rows(suby), 128)])(
+        everywhere(row, "gy")
+    )
     part, weights, scalars_one = kernel(
         bind(spread_first),
         [patch_shape, shape_of(K, 128), shape_of(8, 128)],
         [coarse, tiles, flat],
-        True,
-    )(counts, everywhere(row), coarse_inverse, basis, solved_one)
+    )(live, everywhere(row, "gx"), coarse_inverse, basis, solved_one)
     over, under = swap("gx", part[PX // 2 :], part[: PX // 2])
     folded, odd, even = kernel(fold_rows, [patch_shape, strip, strip])(part, over, under)
     odd, even = swap_columns(odd, even)
@@ -537,17 +569,15 @@
         bind(apply_first),
         [own_shape, own_shape, shape_of(48, LW), rows],
         [tiles, flat],
-        True,
     )(
-        counts, folded, odd, even, coefs, patch, scalars_one, basis, before, after
+        live, folded, odd, even, coefs, patch, scalars_one, basis, before, after
     )
     part, scalars_two = kernel(
         bind(spread_second),
         [patch_shape, shape_of(8, 128)],
         [coarse, tiles, flat],
-        True,
     )(
-        counts, everywhere(row), coarse_inverse, basis, solved_one, solved_two, weights, scalars_one
+        live, everywhere(row), coarse_inverse, basis, solved_one, solved_two, weights, scalars_one
     )
     over, under = swap("gx", part[40:], part[:24])
     strip = shape_of(48, 128)

time: 152 us -> 151 us (level)
  blocking collectives: 100 us -> 96.6 us
  starting transfers between devices: 33.8 us -> 36 us
    all_to_all x4 -> x5, blocking collectives: 100 us -> 96.6 us  [everywhere(): return lax.all_to_all(slots, axes, 0, 0).reshape(rows.shape)]
    ppermute x3, starting transfers between devices: 11.2 us -> 13.4 us  [swap_columns(): odd = lax.ppermute(odd, 'gy', across)]
    pallas_call x10 -> x11, Pallas kernels: 5.3 us -> 5.51 us  [call(): pl.pallas_call(body, out_shape=outs, in_specs=[VMEM] * len(args), out_spe...]
  transfers between devices with their start and end apart: 12 -> 12, of which waited for: 10 -> 8; matrix products, arithmetic and copies ran while one was open for 0% -> 0% of each run, Pallas kernels for 0% -> 0%
where the time goes in v4:
time: 151 us
  blocking collectives  96.6 us (64%)
  starting transfers between devices  36 us (24%)
  waiting for transfers between devices  9.75 us (6%)
  Pallas kernels  6.5 us (4%)
  between operations  1.64 us (1%)
    all_to_all x5, blocking collectives, everywhere(): return lax.all_to_all(slots, axes, 0, 0).reshape(rows.shape)  96.6 us
    ppermute x3, starting transfers between devices, swap_columns(): odd = lax.ppermute(odd, 'gy', across)  13.4 us
    ppermute x3, starting transfers between devices, swap(): before = lax.ppermute(forward, axis, [(i, i + 1) for i in range(count - 1)])  12.1 us
    ppermute x3, starting transfers between devices, swap_columns(): even = lax.ppermute(even, 'gy', inside)  6.59 us
    pallas_call x11, Pallas kernels, call(): pl.pallas_call(body, out_shape=outs, in_specs=[VMEM] * len(args), out_spe...  5.51 us
    ppermute x3, starting transfers between devices, swap(): after = lax.ppermute(backward, axis, [(i + 1, i) for i in range(count - 1)])  3.88 us
    ppermute x3, waiting for transfers between devices, swap(): after = lax.ppermute(backward, axis, [(i + 1, i) for i in range(count - 1)])  3.79 us
  transfers between devices with their start and end apart: 12, of which 8 were waited for; matrix products, arithmetic and copies ran while one was open for 0% of the time, Pallas kernels for 0%

profile of v4, /device:TPU:1, one launch (start us, length us, event | category | flops | bytes accessed | tf_op | source)
XLA Modules:
  0.0 150.6 jit_solution(6603974155907344736)
XLA Ops:
  0.6 0.0 copy-start
  1.4 1.0 shard_map.95
  2.4 0.0 copy-start.1
  2.4 4.2 %collective-permute-start = (f32[256,128]{1,0:T(8,128)S(1)}, f32[256,128]{1,0:T(8,128)S(1)}, u32[]{:S(2)}, u32[]{:S(2)}) collective-permute-start(f32[256,128]{1,0:T(8,128)S(1)} %get-tuple-element.33), channel_id=1, source_target_pairs={{0,64},{64,128},{128,192},{192,256},{256,320},{320,384},{384,448},... | collective-permute-start | bytes 393224 | tf_op jit(solution)/shard_map/ppermute | solution.py:494
  6.6 1.3 collective-permute-start.1
  7.9 0.6 collective-permute-done.before.refs_8_
  8.5 3.8 %collective-permute-done.1.after.refs_9_ = f32[256,128]{1,0:T(8,128)S(1)} collective-permute-done((f32[256,128]{1,0:T(8,128)S(1)}, f32[256,128]{1,0:T(8,128)S(1)}, u32[]{:S(2)}, u32[]{:S(2)}) %collective-permute-start.1) | collective-permute-done | bytes 131104 | tf_op jit(solution)/shard_map/ppermute | solution.py:495
  12.3 0.1 shard_map.96
  12.5 5.1 %collective-permute-start.2 = (f32[64,128]{1,0:T(8,128)S(1)}, f32[64,128]{1,0:T(8,128)S(1)}, u32[]{:S(2)}, u32[]{:S(2)}) collective-permute-start(f32[64,128]{1,0:T(8,128)S(1)} %get-tuple-element.36), channel_id=1, source_target_pairs={{1,2},{2,1},{3,4},{4,3},{5,6},{6,5},{7,8},{8,7},{9,10},{10,9},{11,... | collective-permute-start | bytes 98312 | tf_op jit(solution)/shard_map/ppermute | solution.py:504
  17.6 2.8 %collective-permute-start.3 = (f32[64,128]{1,0:T(8,128)S(1)}, f32[64,128]{1,0:T(8,128)S(1)}, u32[]{:S(2)}, u32[]{:S(2)}) collective-permute-start(f32[64,128]{1,0:T(8,128)S(1)} %get-tuple-element.37), channel_id=1, source_target_pairs={{0,1},{1,0},{2,3},{3,2},{4,5},{5,4},{6,7},{7,6},{8,9},{9,8},{10,11... | collective-permute-start | bytes 98312 | tf_op jit(solution)/shard_map/ppermute | solution.py:503
  20.4 0.0 collective-permute-done.2.refs_2_
  20.4 0.8 collective-permute-done.3.refs_3_
  21.2 0.0 copy-done
  21.2 1.4 shard_map.97
  22.6 22.0 %all_to_all.25 = f32[64,1,128]{2,1,0:T(1,128)S(1)} all-to-all(f32[64,1,128]{2,1,0:T(1,128)S(1)} %bitcast.25), channel_id=1, replica_groups=mesh['gx'=8,'gy'=64] {'gy'}, dimensions={0} | all-to-all | bytes 65536 | tf_op jit(solution)/shard_map/all_to_all | solution.py:511
  44.6 0.1 shard_map.98
  44.7 14.4 %all_to_all.26 = f32[8,24,128]{2,1,0:T(8,128)S(1)} all-to-all(f32[8,24,128]{2,1,0:T(8,128)S(1)} %bitcast.19), channel_id=1, replica_groups=mesh['gx'=8,'gy'=64] {'gx'}, dimensions={0} | all-to-all | bytes 196608 | tf_op jit(solution)/shard_map/all_to_all | solution.py:511
  59.1 0.0 copy-done.1
  59.1 0.6 shard_map.99
  59.7 1.3 collective-permute-start.5
  61.0 4.0 %collective-permute-start.4 = (f32[32,384]{1,0:T(8,128)S(1)}, f32[32,384]{1,0:T(8,128)S(1)}, u32[]{:S(2)}, u32[]{:S(2)}) collective-permute-start(f32[32,384]{1,0:T(8,128)S(1)} %get-tuple-element.63), channel_id=1, source_target_pairs={{0,64},{64,128},{128,192},{192,256},{256,320},{320,384},{384,448},... | collective-permute-start | bytes 147464 | tf_op jit(solution)/shard_map/ppermute | solution.py:494
  65.0 0.0 collective-permute-done.5.after
  65.0 1.1 collective-permute-done.4.before
  66.2 0.1 shard_map.100
  66.3 5.3 %collective-permute-start.6 = (f32[64,128]{1,0:T(8,128)S(1)}, f32[64,128]{1,0:T(8,128)S(1)}, u32[]{:S(2)}, u32[]{:S(2)}) collective-permute-start(f32[64,128]{1,0:T(8,128)S(1)} %get-tuple-element.42), channel_id=1, source_target_pairs={{1,2},{2,1},{3,4},{4,3},{5,6},{6,5},{7,8},{8,7},{9,10},{10,9},{11,... | collective-permute-start | bytes 98312 | tf_op jit(solution)/shard_map/ppermute | solution.py:504
  71.6 1.9 %collective-permute-start.7 = (f32[64,128]{1,0:T(8,128)S(1)}, f32[64,128]{1,0:T(8,128)S(1)}, u32[]{:S(2)}, u32[]{:S(2)}) collective-permute-start(f32[64,128]{1,0:T(8,128)S(1)} %get-tuple-element.43), channel_id=1, source_target_pairs={{0,1},{1,0},{2,3},{3,2},{4,5},{5,4},{6,7},{7,6},{8,9},{9,8},{10,11... | collective-permute-start | bytes 98312 | tf_op jit(solution)/shard_map/ppermute | solution.py:503
  73.5 0.0 collective-permute-done.6.refs_2_
  73.5 1.2 collective-permute-done.7.refs_3_
  74.7 1.2 shard_map.101
  75.9 29.3 %all_to_all.27 = f32[512,1,128]{2,1,0:T(1,128)S(1)} all-to-all(f32[512,1,128]{2,1,0:T(1,128)S(1)} %bitcast.21), channel_id=1, replica_groups=mesh['gx'=8,'gy'=64] {'gx','gy'}, dimensions={0} | all-to-all | bytes 524288 | tf_op jit(solution)/shard_map/all_to_all | solution.py:511
  105.2 0.7 shard_map.102
  106.0 1.3 collective-permute-start.9
  107.3 4.0 %collective-permute-start.8 = (f32[24,384]{1,0:T(8,128)S(1)}, f32[24,384]{1,0:T(8,128)S(1)}, u32[]{:S(2)}, u32[]{:S(2)}) collective-permute-start(f32[24,384]{1,0:T(8,128)S(1)} %get-tuple-element.61), channel_id=1, source_target_pairs={{0,64},{64,128},{128,192},{192,256},{256,320},{320,384},{384,448},... | collective-permute-start | bytes 110600 | tf_op jit(solution)/shard_map/ppermute | solution.py:494
  111.3 0.0 collective-permute-done.9.after
  111.3 1.0 collective-permute-done.8.before
  112.3 0.1 shard_map.103
  112.4 3.0 %collective-permute-start.10 = (f32[48,128]{1,0:T(8,128)S(1)}, f32[48,128]{1,0:T(8,128)S(1)}, u32[]{:S(2)}, u32[]{:S(2)}) collective-permute-start(f32[48,128]{1,0:T(8,128)S(1)} %get-tuple-element.52), channel_id=1, source_target_pairs={{1,2},{2,1},{3,4},{4,3},{5,6},{6,5},{7,8},{8,7},{9,10},{10,9},{11,... | collective-permute-start | bytes 73736 | tf_op jit(solution)/shard_map/ppermute | solution.py:504
  115.5 1.9 %collective-permute-start.11 = (f32[48,128]{1,0:T(8,128)S(1)}, f32[48,128]{1,0:T(8,128)S(1)}, u32[]{:S(2)}, u32[]{:S(2)}) collective-permute-start(f32[48,128]{1,0:T(8,128)S(1)} %get-tuple-element.53), channel_id=1, source_target_pairs={{0,1},{1,0},{2,3},{3,2},{4,5},{5,4},{6,7},{7,6},{8,9},{9,8},{10,11... | collective-permute-start | bytes 73736 | tf_op jit(solution)/shard_map/ppermute | solution.py:503
  117.4 0.2 collective-permute-done.10.odd
  117.6 1.0 collective-permute-done.11.even
  118.5 0.3 shard_map.104
  118.8 13.0 %all_to_all.28 = f32[8,1,128]{2,1,0:T(1,128)S(1)} all-to-all(f32[8,1,128]{2,1,0:T(1,128)S(1)} %bitcast.27), channel_id=1, replica_groups=mesh['gx'=8,'gy'=64] {'gx'}, dimensions={0} | all-to-all | bytes 8192 | tf_op jit(solution)/shard_map/all_to_all | solution.py:511
  131.8 17.9 %all_to_all.29 = f32[64,1,128]{2,1,0:T(1,128)S(1)} all-to-all(f32[64,1,128]{2,1,0:T(1,128)S(1)} %bitcast.22), channel_id=1, replica_groups=mesh['gx'=8,'gy'=64] {'gy'}, dimensions={0} | all-to-all | bytes 65536 | tf_op jit(solution)/shard_map/all_to_all | solution.py:511
  149.7 0.9 shard_map.106
  (3 shorter events, 0.0 us)
Async XLA Ops:
  0.6 20.6 %copy-start = (f32[32,18432]{1,0:T(8,128)S(1)}, f32[32,18432]{1,0:T(8,128)}, u32[]{:S(2)}) copy-start(f32[32,18432]{1,0:T(8,128)} %refs_3_.3) | copy-start | bytes 7077892
  2.4 56.7 %copy-start.1 = (f32[32,16384]{1,0:T(8,128)S(1)}, f32[32,16384]{1,0:T(8,128)}, u32[]{:S(2)}) copy-start(f32[32,16384]{1,0:T(8,128)} %refs_2_.3) | copy-start | bytes 6291460
  2.4 6.1 %collective-permute-start = (f32[256,128]{1,0:T(8,128)S(1)}, f32[256,128]{1,0:T(8,128)S(1)}, u32[]{:S(2)}, u32[]{:S(2)}) collective-permute-start(f32[256,128]{1,0:T(8,128)S(1)} %get-tuple-element.33), channel_id=1, source_target_pairs={{0,64},{64,128},{128,192},{192,256},{256,320},{320,384},{384,448},... | collective-permute-start | bytes 393224 | tf_op jit(solution)/shard_map/ppermute | solution.py:494
  6.6 5.7 %collective-permute-start.1 = (f32[256,128]{1,0:T(8,128)S(1)}, f32[256,128]{1,0:T(8,128)S(1)}, u32[]{:S(2)}, u32[]{:S(2)}) collective-permute-start(f32[256,128]{1,0:T(8,128)S(1)} %get-tuple-element.34), channel_id=1, source_target_pairs={{64,0},{128,64},{192,128},{256,192},{320,256},{384,320},{448,384},... | collective-permute-start | bytes 393224 | tf_op jit(solution)/shard_map/ppermute | solution.py:495
  12.5 7.9 %collective-permute-start.2 = (f32[64,128]{1,0:T(8,128)S(1)}, f32[64,128]{1,0:T(8,128)S(1)}, u32[]{:S(2)}, u32[]{:S(2)}) collective-permute-start(f32[64,128]{1,0:T(8,128)S(1)} %get-tuple-element.36), channel_id=1, source_target_pairs={{1,2},{2,1},{3,4},{4,3},{5,6},{6,5},{7,8},{8,7},{9,10},{10,9},{11,... | collective-permute-start | bytes 98312 | tf_op jit(solution)/shard_map/ppermute | solution.py:504
  17.6 3.6 %collective-permute-start.3 = (f32[64,128]{1,0:T(8,128)S(1)}, f32[64,128]{1,0:T(8,128)S(1)}, u32[]{:S(2)}, u32[]{:S(2)}) collective-permute-start(f32[64,128]{1,0:T(8,128)S(1)} %get-tuple-element.37), channel_id=1, source_target_pairs={{0,1},{1,0},{2,3},{3,2},{4,5},{5,4},{6,7},{7,6},{8,9},{9,8},{10,11... | collective-permute-start | bytes 98312 | tf_op jit(solution)/shard_map/ppermute | solution.py:503
  59.7 5.3 %collective-permute-start.5 = (f32[32,384]{1,0:T(8,128)S(1)}, f32[32,384]{1,0:T(8,128)S(1)}, u32[]{:S(2)}, u32[]{:S(2)}) collective-permute-start(f32[32,384]{1,0:T(8,128)S(1)} %get-tuple-element.62), channel_id=1, source_target_pairs={{64,0},{128,64},{192,128},{256,192},{320,256},{384,320},{448,384},... | collective-permute-start | bytes 147464 | tf_op jit(solution)/shard_map/ppermute | solution.py:495
  61.0 5.2 %collective-permute-start.4 = (f32[32,384]{1,0:T(8,128)S(1)}, f32[32,384]{1,0:T(8,128)S(1)}, u32[]{:S(2)}, u32[]{:S(2)}) collective-permute-start(f32[32,384]{1,0:T(8,128)S(1)} %get-tuple-element.63), channel_id=1, source_target_pairs={{0,64},{64,128},{128,192},{192,256},{256,320},{320,384},{384,448},... | collective-permute-start | bytes 147464 | tf_op jit(solution)/shard_map/ppermute | solution.py:494
  66.3 7.2 %collective-permute-start.6 = (f32[64,128]{1,0:T(8,128)S(1)}, f32[64,128]{1,0:T(8,128)S(1)}, u32[]{:S(2)}, u32[]{:S(2)}) collective-permute-start(f32[64,128]{1,0:T(8,128)S(1)} %get-tuple-element.42), channel_id=1, source_target_pairs={{1,2},{2,1},{3,4},{4,3},{5,6},{6,5},{7,8},{8,7},{9,10},{10,9},{11,... | collective-permute-start | bytes 98312 | tf_op jit(solution)/shard_map/ppermute | solution.py:504
  71.6 3.1 %collective-permute-start.7 = (f32[64,128]{1,0:T(8,128)S(1)}, f32[64,128]{1,0:T(8,128)S(1)}, u32[]{:S(2)}, u32[]{:S(2)}) collective-permute-start(f32[64,128]{1,0:T(8,128)S(1)} %get-tuple-element.43), channel_id=1, source_target_pairs={{0,1},{1,0},{2,3},{3,2},{4,5},{5,4},{6,7},{7,6},{8,9},{9,8},{10,11... | collective-permute-start | bytes 98312 | tf_op jit(solution)/shard_map/ppermute | solution.py:503
  106.0 5.3 %collective-permute-start.9 = (f32[24,384]{1,0:T(8,128)S(1)}, f32[24,384]{1,0:T(8,128)S(1)}, u32[]{:S(2)}, u32[]{:S(2)}) collective-permute-start(f32[24,384]{1,0:T(8,128)S(1)} %get-tuple-element.60), channel_id=1, source_target_pairs={{64,0},{128,64},{192,128},{256,192},{320,256},{384,320},{448,384},... | collective-permute-start | bytes 110600 | tf_op jit(solution)/shard_map/ppermute | solution.py:495
  107.3 5.0 %collective-permute-start.8 = (f32[24,384]{1,0:T(8,128)S(1)}, f32[24,384]{1,0:T(8,128)S(1)}, u32[]{:S(2)}, u32[]{:S(2)}) collective-permute-start(f32[24,384]{1,0:T(8,128)S(1)} %get-tuple-element.61), channel_id=1, source_target_pairs={{0,64},{64,128},{128,192},{192,256},{256,320},{320,384},{384,448},... | collective-permute-start | bytes 110600 | tf_op jit(solution)/shard_map/ppermute | solution.py:494
  112.4 5.1 %collective-permute-start.10 = (f32[48,128]{1,0:T(8,128)S(1)}, f32[48,128]{1,0:T(8,128)S(1)}, u32[]{:S(2)}, u32[]{:S(2)}) collective-permute-start(f32[48,128]{1,0:T(8,128)S(1)} %get-tuple-element.52), channel_id=1, source_target_pairs={{1,2},{2,1},{3,4},{4,3},{5,6},{6,5},{7,8},{8,7},{9,10},{10,9},{11,... | collective-permute-start | bytes 73736 | tf_op jit(solution)/shard_map/ppermute | solution.py:504
  115.5 3.1 %collective-permute-start.11 = (f32[48,128]{1,0:T(8,128)S(1)}, f32[48,128]{1,0:T(8,128)S(1)}, u32[]{:S(2)}, u32[]{:S(2)}) collective-permute-start(f32[48,128]{1,0:T(8,128)S(1)} %get-tuple-element.53), channel_id=1, source_target_pairs={{0,1},{1,0},{2,3},{3,2},{4,5},{5,4},{6,7},{7,6},{8,9},{9,8},{10,11... | collective-permute-start | bytes 73736 | tf_op jit(solution)/shard_map/ppermute | solution.py:503

commit v5 on v4

--- a/solution.py
+++ b/solution.py
@@ -17,6 +17,7 @@
 LW = 384
 GROUPS = PX // 4
 STRIP = 24
+LIVE = PY
 SCALARS = 96
 f32 = jnp.float32
 AXES = ("gx", "gy")
@@ -51,17 +52,17 @@
     return (rows >= OV) & (rows < OV + CX) & (lanes >= OV) & (lanes < OV + CY)
 
 
-def is_even():
-    return lax.rem(lax.axis_index("gy"), 2) == 0
-
-
-def to_pairs(rightward, leftward):
-    even = is_even()
-    return jnp.where(even, leftward, rightward), jnp.where(even, rightward, leftward)
-
-
-def from_pairs(odd, even_pairs):
-    even = is_even()
+def is_even(axis):
+    return lax.rem(lax.axis_index(axis), 2) == 0
+
+
+def to_pairs(axis, ahead, back):
+    even = is_even(axis)
+    return jnp.where(even, back, ahead), jnp.where(even, ahead, back)
+
+
+def from_pairs(axis, odd, even_pairs):
+    even = is_even(axis)
     return jnp.where(even, odd, even_pairs), jnp.where(even, even_pairs, odd)
 
 
@@ -203,8 +204,7 @@
 
 
 def pack_rows(
-    counts, source, potential, along, across, recombination, basis, held, ahead, behind, live_out,
-    head, tail, sems,
+    source, potential, along, across, recombination, basis, held, odd, even, head, tail, sems
 ):
     edge = head.shape[1]
     copies = [
@@ -219,22 +219,21 @@
         copy.start()
     for copy in copies:
         copy.wait()
-    live = (rows_of((K, 128)) < counts[0, 0]).astype(f32)
-    live_out[...] = live
     for f in range(5):
         for t in range(2):
-            at = (2 * f + t) * OV
+            at = slice((2 * f + t) * OV, (2 * f + t + 1) * OV)
             cols = slice(t * 128, (t + 1) * 128)
-            ahead[at : at + OV, :] = held[f, CX - OV :, cols]
-            behind[at : at + OV, :] = held[f, :OV, cols]
+            odd[at, :], even[at, :] = to_pairs(
+                "gx", held[f, CX - OV :, cols], held[f, :OV, cols]
+            )
     for t in range(3):
-        at = 160 + t * K
+        at = slice(160 + t * K, 160 + (t + 1) * K)
         cols = slice(t * 128, (t + 1) * 128)
-        ahead[at : at + K, :] = tail[:, cols] * live
-        behind[at : at + K, :] = head[:, cols] * live
-
-
-def pack_columns(held, before, after, rows, odd, even):
+        odd[at, :], even[at, :] = to_pairs("gx", tail[:, cols], head[:, cols])
+
+
+def pack_columns(held, row_odd, row_even, rows, odd, even):
+    before, after = from_pairs("gx", row_odd[: 10 * OV, :], row_even[: 10 * OV, :])
     lanes = lanes_of((PX, 128))
     to_right = to_left = None
     for f in range(5):
@@ -253,13 +252,13 @@
             first = pltpu.roll(first, STRIP * f, 1)
         to_right = last if f == 0 else to_right + last
         to_left = first if f == 0 else to_left + first
-    odd[...], even[...] = to_pairs(to_right, to_left)
-
-
-def prepare(suby, live, rows, odd, even, basis, patch, coefs, solved, gather, tiles, flat):
+    odd[...], even[...] = to_pairs("gy", to_right, to_left)
+
+
+def prepare(suby, counts, rows, odd, even, basis, live, patch, coefs, solved, gather, tiles, flat):
     zero = jnp.zeros((PX, LW - CY), f32)
     lanes = lanes_of((PX, 128))
-    from_left, from_right = from_pairs(odd[...], even[...])
+    from_left, from_right = from_pairs("gy", odd[...], even[...])
     fields = []
     for f in range(5):
         middle = pltpu.roll(jnp.concatenate([rows[f], zero], axis=1), OV, 1)
@@ -291,6 +290,7 @@
     square = total(jnp.where(own, source * source, 0.0))
     local = relax(source[8:56], diagonal[8:56], [face[8:56] for face in faces])
     solved[...] = jnp.where(own_mask((48, LW), 8), local, 0.0)
+    live[...] = (rows_of((K, 128)) < counts[0, 0]).astype(f32)
     residual = restrict(basis, source, tiles, flat) * live[:, 0:1]
     row = to_row(residual)
     row = jnp.where(lanes_of((1, 128)) == SCALARS, square, row)
@@ -306,7 +306,7 @@
 
 
 def spread_first(
-    suby, live, rows, inverse, basis, solved, part, weights, scalars, coarse, tiles, flat
+    suby, live, rows, inverse, basis, solved, part, odd, even, weights, scalars, coarse, tiles, flat
 ):
     sums = unpacked(rows, coarse, suby)
     square = pick(sums, SCALARS)
@@ -318,36 +318,38 @@
     put(scalars, 1, square / (square + EPSILON))
     part[...] = prolong(basis, solution, tiles, flat)
     part[8:56, :] = part[8:56, :] + solved[...] * scale
-
-
-def fold_rows(part, before, after, folded, odd, even):
+    odd[...], even[...] = to_pairs("gx", part[PX // 2 :, :], part[: PX // 2, :])
+    odd[:, LIVE:] = live[:, : LW - LIVE]
+    even[:, LIVE:] = live[:, : LW - LIVE]
+
+
+def fold_rows(part, row_odd, row_even, folded, odd, even):
     height = folded.shape[0]
     first = (PX - height) // 2
-    half = height // 2
-    whole = part[first : first + height, :] + jnp.concatenate(
-        [before[PX // 2 - half :, :] if before.shape[0] > half else before[...],
-         after[:half, :] if after.shape[0] > half else after[...]],
-        axis=0,
-    )
+    before, after = from_pairs("gx", row_odd[...], row_even[...])
+    whole = part[first : first + height, :] + jnp.concatenate([before, after], axis=0)
+    whole = jnp.where(lanes_of(whole.shape) < PY, whole, 0.0)
     folded[...] = whole
     lanes = lanes_of((height, 128))
     moved = pltpu.roll(whole, LW - 255, 1)
     odd[...], even[...] = to_pairs(
-        jnp.where(lanes < 33, moved[:, :128], 0.0), jnp.where(lanes < 33, whole[:, :128], 0.0)
+        "gy",
+        jnp.where(lanes < 33, moved[:, :128], 0.0),
+        jnp.where(lanes < 33, whole[:, :128], 0.0),
     )
 
 
 def folded_columns(folded, odd, even):
     height = folded.shape[0]
     zero = jnp.zeros((height, 256), f32)
-    from_left, from_right = from_pairs(odd[...], even[...])
+    from_left, from_right = from_pairs("gy", odd[...], even[...])
     one = pltpu.roll(jnp.concatenate([from_left, zero], axis=1), LW - 1, 1)
     two = jnp.concatenate([zero, from_right], axis=1)
     return folded[...] + one + two
 
 
 def apply_first(
-    suby, live, folded, odd, even, coefs, patch, scalars, basis, before, after,
+    suby, live, folded, odd, even, coefs, patch, scalars, basis, row_odd, row_even, half_odd, half_even,
     direction, image, solved, gather, tiles, flat,
 ):
     field = folded_columns(folded, odd, even)
@@ -372,12 +374,18 @@
     for_next = for_before = jnp.zeros((K, 128), f32)
     for t in range(3):
         cols = slice(t * 128, (t + 1) * 128)
-        at = 160 + t * K
-        for_next = for_next + after[at : at + K, :] * fourth[0:1, cols]
-        for_before = for_before + before[at : at + K, :] * third[7:8, cols]
+        at = slice(160 + t * K, 160 + (t + 1) * K)
+        before, after = from_pairs("gx", row_odd[at, :], row_even[at, :])
+        for_next = for_next + after * fourth[0:1, cols]
+        for_before = for_before + before * third[7:8, cols]
+    before, after = from_pairs(
+        "gx", half_odd[:, LIVE : LIVE + 1], half_even[:, LIVE : LIVE + 1]
+    )
+    for_next = after * jnp.sum(for_next, axis=1, keepdims=True)
+    for_before = before * jnp.sum(for_before, axis=1, keepdims=True)
     row = to_row(residual)
-    row = row + pltpu.roll(to_row(jnp.sum(for_next, axis=1, keepdims=True)), 32, 1)
-    row = row + pltpu.roll(to_row(jnp.sum(for_before, axis=1, keepdims=True)), 64, 1)
+    row = row + pltpu.roll(to_row(for_next), 32, 1)
+    row = row + pltpu.roll(to_row(for_before), 64, 1)
     lanes = lanes_of((1, 128))
     row = jnp.where(lanes == SCALARS, cross, jnp.where(lanes == SCALARS + 1, square, row))
     gather[...] = jnp.broadcast_to(row, gather.shape)
@@ -385,7 +393,7 @@
 
 def spread_second(
     suby, live, rows, inverse, basis, solved_first, solved, weights, scalars_in,
-    part, scalars, coarse, tiles, flat,
+    part, odd, even, scalars, coarse, tiles, flat,
 ):
     sums = gathered(rows, coarse, suby)
     cross = pick(sums, SCALARS)
@@ -404,6 +412,7 @@
     part[...] = prolong(basis, solution, tiles, flat)
     local = (solved[...] - (cross / norm) * solved_first[...]) * scale
     part[8:56, :] = part[8:56, :] + local
+    odd[...], even[...] = to_pairs("gx", part[40:, :], part[:24, :])
 
 
 def apply_second(
@@ -475,12 +484,15 @@
 PARAMS = pltpu.CompilerParams(vmem_limit_bytes=24 * 1024 * 1024)
 
 
-def kernel(body, outs, scratch=()):
+def kernel(body, outs, scratch=(), first_smem=False):
     def call(*args):
+        specs = [VMEM] * len(args)
+        if first_smem:
+            specs[0] = pl.BlockSpec(memory_space=pltpu.SMEM)
         return pl.pallas_call(
             body,
             out_shape=outs,
-            in_specs=[VMEM] * len(args),
+            in_specs=specs,
             out_specs=[VMEM] * len(outs),
             scratch_shapes=list(scratch),
             compiler_params=PARAMS,
@@ -489,19 +501,12 @@
     return call
 
 
-def swap(axis, forward, backward):
+def swap(axis, odd, even):
     count = lax.axis_size(axis)
-    before = lax.ppermute(forward, axis, [(i, i + 1) for i in range(count - 1)])
-    after = lax.ppermute(backward, axis, [(i + 1, i) for i in range(count - 1)])
-    return before, after
-
-
-def swap_columns(odd, even):
-    count = lax.axis_size("gy")
-    inside = [(i, i ^ 1) for i in range(count)]
-    across = [(i, i + 1 if i % 2 else i - 1) for i in range(1, count - 1)]
-    even = lax.ppermute(even, "gy", inside)
-    odd = lax.ppermute(odd, "gy", across)
+    even = lax.ppermute(even, axis, [(i, i ^ 1) for i in range(count)])
+    odd = lax.ppermute(
+        odd, axis, [(i, i + 1 if i % 2 else i - 1) for i in range(1, count - 1)]
+    )
     return odd, even
 
 
@@ -530,61 +535,60 @@
         return run
 
     edge = pltpu.VMEM((K, 3 * 128), f32)
-    held, ahead, behind, live = pl.pallas_call(
+    held, odd, even = pl.pallas_call(
         pack_rows,
-        out_shape=[
-            shape_of(5, CX, CY), shape_of(256, 128), shape_of(256, 128), shape_of(K, 128)
-        ],
-        in_specs=[pl.BlockSpec(memory_space=pltpu.SMEM)]
-        + [pl.BlockSpec(memory_space=pltpu.HBM)] * 6,
-        out_specs=[VMEM] * 4,
-        scratch_shapes=[
-            edge, edge, pltpu.SemaphoreType.DMA((7,))
-        ],
+        out_shape=[shape_of(5, CX, CY), shape_of(256, 128), shape_of(256, 128)],
+        in_specs=[pl.BlockSpec(memory_space=pltpu.HBM)] * 6,
+        out_specs=[VMEM] * 3,
+        scratch_shapes=[edge, edge, pltpu.SemaphoreType.DMA((7,))],
         compiler_params=PARAMS,
-    )(counts, *[pltpu.with_memory_space_constraint(x, pltpu.HBM) for x in (*fields, basis)])
-    before, after = swap("gx", ahead, behind)
+    )(*[pltpu.with_memory_space_constraint(x, pltpu.HBM) for x in (*fields, basis)])
+    row_odd, row_even = swap("gx", odd, even)
     strip = shape_of(PX, 128)
     grown, odd, even = kernel(pack_columns, [shape_of(5, PX, CY), strip, strip])(
-        held, before, after
-    )
-    odd, even = swap_columns(odd, even)
-    patch, coefs, solved_one, row = kernel(
+        held, row_odd, row_even
+    )
+    odd, even = swap("gy", odd, even)
+    live, patch, coefs, solved_one, row = kernel(
         bind(prepare),
-        [patch_shape, shape_of(5, PX, LW), shape_of(48, LW), shape_of(suby, 128)],
+        [shape_of(K, 128), patch_shape, shape_of(5, PX, LW), shape_of(48, LW), shape_of(suby, 128)],
         [tiles, flat],
-    )(live, grown, odd, even, basis)
+        True,
+    )(counts, grown, odd, even, basis)
     (row,) = kernel(compact, [shape_of(devices // suby * slot_rows(suby), 128)])(
         everywhere(row, "gy")
     )
-    part, weights, scalars_one = kernel(
+    half = shape_of(PX // 2, LW)
+    part, odd, even, weights, scalars_one = kernel(
         bind(spread_first),
-        [patch_shape, shape_of(K, 128), shape_of(8, 128)],
+        [patch_shape, half, half, shape_of(K, 128), shape_of(8, 128)],
         [coarse, tiles, flat],
     )(live, everywhere(row, "gx"), coarse_inverse, basis, solved_one)
-    over, under = swap("gx", part[PX // 2 :], part[: PX // 2])
-    folded, odd, even = kernel(fold_rows, [patch_shape, strip, strip])(part, over, under)
-    odd, even = swap_columns(odd, even)
+    half_odd, half_even = swap("gx", odd, even)
+    folded, odd, even = kernel(fold_rows, [patch_shape, strip, strip])(part, half_odd, half_even)
+    odd, even = swap("gy", odd, even)
     direction_one, image_one, solved_two, row = kernel(
         bind(apply_first),
         [own_shape, own_shape, shape_of(48, LW), rows],
         [tiles, flat],
     )(
-        live, folded, odd, even, coefs, patch, scalars_one, basis, before, after
-    )
-    part, scalars_two = kernel(
+        live, folded, odd, even, coefs, patch, scalars_one, basis,
+        row_odd, row_even, half_odd, half_even,
+    )
+    half = shape_of(24, LW)
+    part, odd, even, scalars_two = kernel(
         bind(spread_second),
-        [patch_shape, shape_of(8, 128)],
+        [patch_shape, half, half, shape_of(8, 128)],
         [coarse, tiles, flat],
     )(
         live, everywhere(row), coarse_inverse, basis, solved_one, solved_two, weights, scalars_one
     )
-    over, under = swap("gx", part[40:], part[:24])
+    half_odd, half_even = swap("gx", odd, even)
     strip = shape_of(48, 128)
     folded, odd, even = kernel(fold_rows, [shape_of(48, LW), strip, strip])(
-        part, over, under
-    )
-    odd, even = swap_columns(odd, even)
+        part, half_odd, half_even
+    )
+    odd, even = swap("gy", odd, even)
     direction_two, image_two, row = kernel(
         apply_second, [own_shape, own_shape, shape_of(devices // suby, 128)]
     )(

time: 151 us -> 147 us (0.974)
  blocking collectives: 96.6 us -> 94.3 us
  waiting for transfers between devices: 9.75 us -> 7.62 us
    all_to_all x5, blocking collectives: 96.6 us -> 94.3 us  [everywhere(): return lax.all_to_all(slots, axes, 0, 0).reshape(rows.shape)]
    ppermute x12, waiting for transfers between devices: 9.75 us -> 7.62 us  [the longest x6 7.6 us: swap(): even = lax.ppermute(even, axis, [(i, i ^ 1) for i in range(count)])]
  transfers between devices with their start and end apart: 12 -> 12, of which waited for: 8 -> 6; matrix products, arithmetic and copies ran while one was open for 0% -> 0% of each run, Pallas kernels for 0% -> 0%
where the time goes in v5:
time: 147 us; the launch traced here: 146 us
  blocking collectives  94.3 us (64%)
  starting transfers between devices  36.2 us (25%)
  waiting for transfers between devices  7.62 us (5%)
  Pallas kernels  6.44 us (4%)
  between operations  1.49 us (1%)
    all_to_all x5, blocking collectives, everywhere(): return lax.all_to_all(slots, axes, 0, 0).reshape(rows.shape)  94.3 us
    ppermute x6, starting transfers between devices, swap(): even = lax.ppermute(even, axis, [(i, i ^ 1) for i in range(count)])  20.1 us
    ppermute x6, starting transfers between devices, swap(): lax.ppermute(odd, axis, [(i, i + 1 if i % 2 else i - 1) for i in range(1,...  16.2 us
    ppermute x6, waiting for transfers between devices, swap(): even = lax.ppermute(even, axis, [(i, i ^ 1) for i in range(count)])  7.6 us
    pallas_call x11, Pallas kernels, call(): pl.pallas_call(body, out_shape=outs, in_specs=specs, out_specs=[VMEM] * l...  5.29 us
  transfers between devices with their start and end apart: 12, of which 6 were waited for; matrix products, arithmetic and copies ran while one was open for 0% of the time, Pallas kernels for 0%

profile of v5, /device:TPU:1, one launch (start us, length us, event | category | flops | bytes accessed | tf_op | source)
XLA Modules:
  0.0 146.1 jit_solution(9028029941335032452)
XLA Ops:
  0.6 0.0 copy-start
  0.6 1.1 shard_map.95
  1.8 0.0 copy-start.1
  1.8 0.8 collective-permute-start
  2.6 6.6 %collective-permute-start.1 = (f32[256,128]{1,0:T(8,128)S(1)}, f32[256,128]{1,0:T(8,128)S(1)}, u32[]{:S(2)}, u32[]{:S(2)}) collective-permute-start(f32[256,128]{1,0:T(8,128)S(1)} %get-tuple-element.37), channel_id=1, source_target_pairs={{0,64},{64,0},{128,192},{192,128},{256,320},{320,256},{384,448},{4... | collective-permute-start | bytes 393224 | tf_op jit(solution)/shard_map/ppermute | solution.py:506
  9.2 0.0 collective-permute-done.row_odd.refs_8_
  9.2 2.3 %collective-permute-done.1.row_even.refs_9_ = f32[256,128]{1,0:T(8,128)S(1)} collective-permute-done((f32[256,128]{1,0:T(8,128)S(1)}, f32[256,128]{1,0:T(8,128)S(1)}, u32[]{:S(2)}, u32[]{:S(2)}) %collective-permute-start.1) | collective-permute-done | bytes 131104 | tf_op jit(solution)/shard_map/ppermute | solution.py:506
  11.5 0.1 shard_map.96
  11.7 5.1 %collective-permute-start.2 = (f32[64,128]{1,0:T(8,128)S(1)}, f32[64,128]{1,0:T(8,128)S(1)}, u32[]{:S(2)}, u32[]{:S(2)}) collective-permute-start(f32[64,128]{1,0:T(8,128)S(1)} %get-tuple-element.39), channel_id=1, source_target_pairs={{1,2},{2,1},{3,4},{4,3},{5,6},{6,5},{7,8},{8,7},{9,10},{10,9},{11,... | collective-permute-start | bytes 98312 | tf_op jit(solution)/shard_map/ppermute | solution.py:507
  16.8 2.3 %collective-permute-start.3 = (f32[64,128]{1,0:T(8,128)S(1)}, f32[64,128]{1,0:T(8,128)S(1)}, u32[]{:S(2)}, u32[]{:S(2)}) collective-permute-start(f32[64,128]{1,0:T(8,128)S(1)} %get-tuple-element.40), channel_id=1, source_target_pairs={{0,1},{1,0},{2,3},{3,2},{4,5},{5,4},{6,7},{7,6},{8,9},{9,8},{10,11... | collective-permute-start | bytes 98312 | tf_op jit(solution)/shard_map/ppermute | solution.py:506
  19.7 0.0 collective-permute-done.2.refs_2_
  19.8 0.2 collective-permute-done.3.refs_3_
  19.9 0.0 copy-done
  19.9 1.3 shard_map.97
  21.3 22.4 %all_to_all.25 = f32[64,1,128]{2,1,0:T(1,128)S(1)} all-to-all(f32[64,1,128]{2,1,0:T(1,128)S(1)} %bitcast.25), channel_id=1, replica_groups=mesh['gx'=8,'gy'=64] {'gy'}, dimensions={0} | all-to-all | bytes 65536 | tf_op jit(solution)/shard_map/all_to_all | solution.py:516
  43.7 0.1 shard_map.98
  43.8 13.4 %all_to_all.26 = f32[8,24,128]{2,1,0:T(8,128)S(1)} all-to-all(f32[8,24,128]{2,1,0:T(8,128)S(1)} %bitcast.19), channel_id=1, replica_groups=mesh['gx'=8,'gy'=64] {'gx'}, dimensions={0} | all-to-all | bytes 196608 | tf_op jit(solution)/shard_map/all_to_all | solution.py:516
  57.2 0.0 copy-done.1
  57.2 0.6 shard_map.99
  57.8 0.7 collective-permute-start.4
  58.4 3.5 %collective-permute-start.5 = (f32[32,384]{1,0:T(8,128)S(1)}, f32[32,384]{1,0:T(8,128)S(1)}, u32[]{:S(2)}, u32[]{:S(2)}) collective-permute-start(f32[32,384]{1,0:T(8,128)S(1)} %get-tuple-element.46), channel_id=1, source_target_pairs={{0,64},{64,0},{128,192},{192,128},{256,320},{320,256},{384,448},{4... | collective-permute-start | bytes 147464 | tf_op jit(solution)/shard_map/ppermute | solution.py:506
  62.0 0.0 collective-permute-done.4.row_odd.refs_10_
  62.0 1.5 collective-permute-done.5.row_even.refs_11_
  63.4 0.1 shard_map.100
  63.5 5.1 %collective-permute-start.6 = (f32[64,128]{1,0:T(8,128)S(1)}, f32[64,128]{1,0:T(8,128)S(1)}, u32[]{:S(2)}, u32[]{:S(2)}) collective-permute-start(f32[64,128]{1,0:T(8,128)S(1)} %get-tuple-element.48), channel_id=1, source_target_pairs={{1,2},{2,1},{3,4},{4,3},{5,6},{6,5},{7,8},{8,7},{9,10},{10,9},{11,... | collective-permute-start | bytes 98312 | tf_op jit(solution)/shard_map/ppermute | solution.py:507
  68.7 1.9 %collective-permute-start.7 = (f32[64,128]{1,0:T(8,128)S(1)}, f32[64,128]{1,0:T(8,128)S(1)}, u32[]{:S(2)}, u32[]{:S(2)}) collective-permute-start(f32[64,128]{1,0:T(8,128)S(1)} %get-tuple-element.49), channel_id=1, source_target_pairs={{0,1},{1,0},{2,3},{3,2},{4,5},{5,4},{6,7},{7,6},{8,9},{9,8},{10,11... | collective-permute-start | bytes 98312 | tf_op jit(solution)/shard_map/ppermute | solution.py:506
  70.6 0.0 collective-permute-done.6.refs_2_
  70.6 1.2 collective-permute-done.7.refs_3_
  71.8 1.1 shard_map.101
  72.9 29.1 %all_to_all.27 = f32[512,1,128]{2,1,0:T(1,128)S(1)} all-to-all(f32[512,1,128]{2,1,0:T(1,128)S(1)} %bitcast.21), channel_id=1, replica_groups=mesh['gx'=8,'gy'=64] {'gx','gy'}, dimensions={0} | all-to-all | bytes 524288 | tf_op jit(solution)/shard_map/all_to_all | solution.py:516
  102.0 0.7 shard_map.102
  102.7 0.7 collective-permute-start.8
  103.3 3.8 %collective-permute-start.9 = (f32[24,384]{1,0:T(8,128)S(1)}, f32[24,384]{1,0:T(8,128)S(1)}, u32[]{:S(2)}, u32[]{:S(2)}) collective-permute-start(f32[24,384]{1,0:T(8,128)S(1)} %get-tuple-element.58), channel_id=1, source_target_pairs={{0,64},{64,0},{128,192},{192,128},{256,320},{320,256},{384,448},{4... | collective-permute-start | bytes 110600 | tf_op jit(solution)/shard_map/ppermute | solution.py:506
  107.2 0.0 collective-permute-done.8.row_odd
  107.2 1.3 collective-permute-done.9.row_even
  108.5 0.1 shard_map.103
  108.6 3.8 %collective-permute-start.10 = (f32[48,128]{1,0:T(8,128)S(1)}, f32[48,128]{1,0:T(8,128)S(1)}, u32[]{:S(2)}, u32[]{:S(2)}) collective-permute-start(f32[48,128]{1,0:T(8,128)S(1)} %get-tuple-element.60), channel_id=1, source_target_pairs={{1,2},{2,1},{3,4},{4,3},{5,6},{6,5},{7,8},{8,7},{9,10},{10,9},{11,... | collective-permute-start | bytes 73736 | tf_op jit(solution)/shard_map/ppermute | solution.py:507
  112.4 1.9 %collective-permute-start.11 = (f32[48,128]{1,0:T(8,128)S(1)}, f32[48,128]{1,0:T(8,128)S(1)}, u32[]{:S(2)}, u32[]{:S(2)}) collective-permute-start(f32[48,128]{1,0:T(8,128)S(1)} %get-tuple-element.61), channel_id=1, source_target_pairs={{0,1},{1,0},{2,3},{3,2},{4,5},{5,4},{6,7},{7,6},{8,9},{9,8},{10,11... | collective-permute-start | bytes 73736 | tf_op jit(solution)/shard_map/ppermute | solution.py:506
  114.4 0.0 collective-permute-done.10.odd
  114.4 1.2 collective-permute-done.11.even
  115.5 0.3 shard_map.104
  115.8 11.5 %all_to_all.28 = f32[8,1,128]{2,1,0:T(1,128)S(1)} all-to-all(f32[8,1,128]{2,1,0:T(1,128)S(1)} %bitcast.27), channel_id=1, replica_groups=mesh['gx'=8,'gy'=64] {'gx'}, dimensions={0} | all-to-all | bytes 8192 | tf_op jit(solution)/shard_map/all_to_all | solution.py:516
  127.3 17.9 %all_to_all.29 = f32[64,1,128]{2,1,0:T(1,128)S(1)} all-to-all(f32[64,1,128]{2,1,0:T(1,128)S(1)} %bitcast.22), channel_id=1, replica_groups=mesh['gx'=8,'gy'=64] {'gy'}, dimensions={0} | all-to-all | bytes 65536 | tf_op jit(solution)/shard_map/all_to_all | solution.py:516
  145.2 0.9 shard_map.106
  (1 shorter events, 0.0 us)
Async XLA Ops:
  0.6 19.3 %copy-start = (f32[32,18432]{1,0:T(8,128)S(1)}, f32[32,18432]{1,0:T(8,128)}, u32[]{:S(2)}) copy-start(f32[32,18432]{1,0:T(8,128)} %refs_3_.3) | copy-start | bytes 7077892
  1.8 55.4 %copy-start.1 = (f32[32,16384]{1,0:T(8,128)S(1)}, f32[32,16384]{1,0:T(8,128)}, u32[]{:S(2)}) copy-start(f32[32,16384]{1,0:T(8,128)} %refs_2_.3) | copy-start | bytes 6291460
  1.8 7.4 %collective-permute-start = (f32[256,128]{1,0:T(8,128)S(1)}, f32[256,128]{1,0:T(8,128)S(1)}, u32[]{:S(2)}, u32[]{:S(2)}) collective-permute-start(f32[256,128]{1,0:T(8,128)S(1)} %get-tuple-element.36), channel_id=1, source_target_pairs={{64,128},{128,64},{192,256},{256,192},{320,384},{384,320},{65,129}... | collective-permute-start | bytes 393224 | tf_op jit(solution)/shard_map/ppermute | solution.py:507
  2.6 8.9 %collective-permute-start.1 = (f32[256,128]{1,0:T(8,128)S(1)}, f32[256,128]{1,0:T(8,128)S(1)}, u32[]{:S(2)}, u32[]{:S(2)}) collective-permute-start(f32[256,128]{1,0:T(8,128)S(1)} %get-tuple-element.37), channel_id=1, source_target_pairs={{0,64},{64,0},{128,192},{192,128},{256,320},{320,256},{384,448},{4... | collective-permute-start | bytes 393224 | tf_op jit(solution)/shard_map/ppermute | solution.py:506
  11.7 8.1 %collective-permute-start.2 = (f32[64,128]{1,0:T(8,128)S(1)}, f32[64,128]{1,0:T(8,128)S(1)}, u32[]{:S(2)}, u32[]{:S(2)}) collective-permute-start(f32[64,128]{1,0:T(8,128)S(1)} %get-tuple-element.39), channel_id=1, source_target_pairs={{1,2},{2,1},{3,4},{4,3},{5,6},{6,5},{7,8},{8,7},{9,10},{10,9},{11,... | collective-permute-start | bytes 98312 | tf_op jit(solution)/shard_map/ppermute | solution.py:507
  16.8 3.1 %collective-permute-start.3 = (f32[64,128]{1,0:T(8,128)S(1)}, f32[64,128]{1,0:T(8,128)S(1)}, u32[]{:S(2)}, u32[]{:S(2)}) collective-permute-start(f32[64,128]{1,0:T(8,128)S(1)} %get-tuple-element.40), channel_id=1, source_target_pairs={{0,1},{1,0},{2,3},{3,2},{4,5},{5,4},{6,7},{7,6},{8,9},{9,8},{10,11... | collective-permute-start | bytes 98312 | tf_op jit(solution)/shard_map/ppermute | solution.py:506
  57.8 4.2 %collective-permute-start.4 = (f32[32,384]{1,0:T(8,128)S(1)}, f32[32,384]{1,0:T(8,128)S(1)}, u32[]{:S(2)}, u32[]{:S(2)}) collective-permute-start(f32[32,384]{1,0:T(8,128)S(1)} %get-tuple-element.45), channel_id=1, source_target_pairs={{64,128},{128,64},{192,256},{256,192},{320,384},{384,320},{65,129}... | collective-permute-start | bytes 147464 | tf_op jit(solution)/shard_map/ppermute | solution.py:507
  58.4 5.0 %collective-permute-start.5 = (f32[32,384]{1,0:T(8,128)S(1)}, f32[32,384]{1,0:T(8,128)S(1)}, u32[]{:S(2)}, u32[]{:S(2)}) collective-permute-start(f32[32,384]{1,0:T(8,128)S(1)} %get-tuple-element.46), channel_id=1, source_target_pairs={{0,64},{64,0},{128,192},{192,128},{256,320},{320,256},{384,448},{4... | collective-permute-start | bytes 147464 | tf_op jit(solution)/shard_map/ppermute | solution.py:506
  63.5 7.1 %collective-permute-start.6 = (f32[64,128]{1,0:T(8,128)S(1)}, f32[64,128]{1,0:T(8,128)S(1)}, u32[]{:S(2)}, u32[]{:S(2)}) collective-permute-start(f32[64,128]{1,0:T(8,128)S(1)} %get-tuple-element.48), channel_id=1, source_target_pairs={{1,2},{2,1},{3,4},{4,3},{5,6},{6,5},{7,8},{8,7},{9,10},{10,9},{11,... | collective-permute-start | bytes 98312 | tf_op jit(solution)/shard_map/ppermute | solution.py:507
  68.7 3.1 %collective-permute-start.7 = (f32[64,128]{1,0:T(8,128)S(1)}, f32[64,128]{1,0:T(8,128)S(1)}, u32[]{:S(2)}, u32[]{:S(2)}) collective-permute-start(f32[64,128]{1,0:T(8,128)S(1)} %get-tuple-element.49), channel_id=1, source_target_pairs={{0,1},{1,0},{2,3},{3,2},{4,5},{5,4},{6,7},{7,6},{8,9},{9,8},{10,11... | collective-permute-start | bytes 98312 | tf_op jit(solution)/shard_map/ppermute | solution.py:506
  102.7 4.5 %collective-permute-start.8 = (f32[24,384]{1,0:T(8,128)S(1)}, f32[24,384]{1,0:T(8,128)S(1)}, u32[]{:S(2)}, u32[]{:S(2)}) collective-permute-start(f32[24,384]{1,0:T(8,128)S(1)} %get-tuple-element.57), channel_id=1, source_target_pairs={{64,128},{128,64},{192,256},{256,192},{320,384},{384,320},{65,129}... | collective-permute-start | bytes 110600 | tf_op jit(solution)/shard_map/ppermute | solution.py:507
  103.3 5.2 %collective-permute-start.9 = (f32[24,384]{1,0:T(8,128)S(1)}, f32[24,384]{1,0:T(8,128)S(1)}, u32[]{:S(2)}, u32[]{:S(2)}) collective-permute-start(f32[24,384]{1,0:T(8,128)S(1)} %get-tuple-element.58), channel_id=1, source_target_pairs={{0,64},{64,0},{128,192},{192,128},{256,320},{320,256},{384,448},{4... | collective-permute-start | bytes 110600 | tf_op jit(solution)/shard_map/ppermute | solution.py:506
  108.6 5.7 %collective-permute-start.10 = (f32[48,128]{1,0:T(8,128)S(1)}, f32[48,128]{1,0:T(8,128)S(1)}, u32[]{:S(2)}, u32[]{:S(2)}) collective-permute-start(f32[48,128]{1,0:T(8,128)S(1)} %get-tuple-element.60), channel_id=1, source_target_pairs={{1,2},{2,1},{3,4},{4,3},{5,6},{6,5},{7,8},{8,7},{9,10},{10,9},{11,... | collective-permute-start | bytes 73736 | tf_op jit(solution)/shard_map/ppermute | solution.py:507
  112.4 3.1 %collective-permute-start.11 = (f32[48,128]{1,0:T(8,128)S(1)}, f32[48,128]{1,0:T(8,128)S(1)}, u32[]{:S(2)}, u32[]{:S(2)}) collective-permute-start(f32[48,128]{1,0:T(8,128)S(1)} %get-tuple-element.61), channel_id=1, source_target_pairs={{0,1},{1,0},{2,3},{3,2},{4,5},{5,4},{6,7},{7,6},{8,9},{9,8},{10,11... | collective-permute-start | bytes 73736 | tf_op jit(solution)/shard_map/ppermute | solution.py:506

commit v6 on v5

--- a/solution.py
+++ b/solution.py
@@ -590,14 +590,14 @@
     )
     odd, even = swap("gy", odd, even)
     direction_two, image_two, row = kernel(
-        apply_second, [own_shape, own_shape, shape_of(devices // suby, 128)]
+        apply_second, [own_shape, own_shape, shape_of(suby, 128)]
     )(
         folded, odd, even, coefs, patch, image_one, scalars_two
     )
-    (row,) = kernel(add_rows, [shape_of(suby, 128)])(everywhere(row, "gx"))
+    (row,) = kernel(add_rows, [shape_of(devices // suby, 128)])(everywhere(row, "gy"))
     out = shape_of(CX, CY)
     answer, residual = kernel(finish, [out, out])(
-        everywhere(row, "gy"), patch, image_one, image_two, direction_one, direction_two, scalars_two
+        everywhere(row, "gx"), patch, image_one, image_two, direction_one, direction_two, scalars_two
     )
     return answer, residual
 

time: 147 us -> 145 us (0.986)
  no operation moved by 1% of the time
where the time goes in v6:
time: 145 us
  blocking collectives  92.9 us (64%)
  starting transfers between devices  36.2 us (25%)
  waiting for transfers between devices  7.62 us (5%)
  Pallas kernels  6.43 us (4%)
  between operations  1.49 us (1%)
    all_to_all x5, blocking collectives, everywhere(): return lax.all_to_all(slots, axes, 0, 0).reshape(rows.shape)  92.9 us
    ppermute x6, starting transfers between devices, swap(): even = lax.ppermute(even, axis, [(i, i ^ 1) for i in range(count)])  20.1 us
    ppermute x6, starting transfers between devices, swap(): lax.ppermute(odd, axis, [(i, i + 1 if i % 2 else i - 1) for i in range(1,...  16.2 us
    ppermute x6, waiting for transfers between devices, swap(): even = lax.ppermute(even, axis, [(i, i ^ 1) for i in range(count)])  7.6 us
    pallas_call x11, Pallas kernels, call(): pl.pallas_call(body, out_shape=outs, in_specs=specs, out_specs=[VMEM] * l...  5.29 us
  transfers between devices with their start and end apart: 12, of which 6 were waited for; matrix products, arithmetic and copies ran while one was open for 0% of the time, Pallas kernels for 0%

profile of v6, /device:TPU:1, one launch (start us, length us, event | category | flops | bytes accessed | tf_op | source)
XLA Modules:
  0.0 144.6 jit_solution(12202562837854647740)
XLA Ops:
  0.6 0.0 copy-start
  0.6 1.1 shard_map.95
  1.8 0.0 copy-start.1
  1.8 0.8 collective-permute-start
  2.6 6.6 %collective-permute-start.1 = (f32[256,128]{1,0:T(8,128)S(1)}, f32[256,128]{1,0:T(8,128)S(1)}, u32[]{:S(2)}, u32[]{:S(2)}) collective-permute-start(f32[256,128]{1,0:T(8,128)S(1)} %get-tuple-element.37), channel_id=1, source_target_pairs={{0,64},{64,0},{128,192},{192,128},{256,320},{320,256},{384,448},{4... | collective-permute-start | bytes 393224 | tf_op jit(solution)/shard_map/ppermute | solution.py:506
  9.2 0.0 collective-permute-done.row_odd.refs_8_
  9.2 2.3 %collective-permute-done.1.row_even.refs_9_ = f32[256,128]{1,0:T(8,128)S(1)} collective-permute-done((f32[256,128]{1,0:T(8,128)S(1)}, f32[256,128]{1,0:T(8,128)S(1)}, u32[]{:S(2)}, u32[]{:S(2)}) %collective-permute-start.1) | collective-permute-done | bytes 131104 | tf_op jit(solution)/shard_map/ppermute | solution.py:506
  11.5 0.1 shard_map.96
  11.7 5.1 %collective-permute-start.2 = (f32[64,128]{1,0:T(8,128)S(1)}, f32[64,128]{1,0:T(8,128)S(1)}, u32[]{:S(2)}, u32[]{:S(2)}) collective-permute-start(f32[64,128]{1,0:T(8,128)S(1)} %get-tuple-element.39), channel_id=1, source_target_pairs={{1,2},{2,1},{3,4},{4,3},{5,6},{6,5},{7,8},{8,7},{9,10},{10,9},{11,... | collective-permute-start | bytes 98312 | tf_op jit(solution)/shard_map/ppermute | solution.py:507
  16.8 2.3 %collective-permute-start.3 = (f32[64,128]{1,0:T(8,128)S(1)}, f32[64,128]{1,0:T(8,128)S(1)}, u32[]{:S(2)}, u32[]{:S(2)}) collective-permute-start(f32[64,128]{1,0:T(8,128)S(1)} %get-tuple-element.40), channel_id=1, source_target_pairs={{0,1},{1,0},{2,3},{3,2},{4,5},{5,4},{6,7},{7,6},{8,9},{9,8},{10,11... | collective-permute-start | bytes 98312 | tf_op jit(solution)/shard_map/ppermute | solution.py:506
  19.7 0.0 collective-permute-done.2.refs_2_
  19.8 0.2 collective-permute-done.3.refs_3_
  19.9 0.0 copy-done
  19.9 1.3 shard_map.97
  21.3 22.4 %all_to_all.25 = f32[64,1,128]{2,1,0:T(1,128)S(1)} all-to-all(f32[64,1,128]{2,1,0:T(1,128)S(1)} %bitcast.24), channel_id=1, replica_groups=mesh['gx'=8,'gy'=64] {'gy'}, dimensions={0} | all-to-all | bytes 65536 | tf_op jit(solution)/shard_map/all_to_all | solution.py:516
  43.7 0.1 shard_map.98
  43.8 13.4 %all_to_all.26 = f32[8,24,128]{2,1,0:T(8,128)S(1)} all-to-all(f32[8,24,128]{2,1,0:T(8,128)S(1)} %bitcast.19), channel_id=1, replica_groups=mesh['gx'=8,'gy'=64] {'gx'}, dimensions={0} | all-to-all | bytes 196608 | tf_op jit(solution)/shard_map/all_to_all | solution.py:516
  57.2 0.0 copy-done.1
  57.2 0.6 shard_map.99
  57.8 0.7 collective-permute-start.4
  58.4 3.5 %collective-permute-start.5 = (f32[32,384]{1,0:T(8,128)S(1)}, f32[32,384]{1,0:T(8,128)S(1)}, u32[]{:S(2)}, u32[]{:S(2)}) collective-permute-start(f32[32,384]{1,0:T(8,128)S(1)} %get-tuple-element.46), channel_id=1, source_target_pairs={{0,64},{64,0},{128,192},{192,128},{256,320},{320,256},{384,448},{4... | collective-permute-start | bytes 147464 | tf_op jit(solution)/shard_map/ppermute | solution.py:506
  62.0 0.0 collective-permute-done.4.row_odd.refs_10_
  62.0 1.5 %collective-permute-done.5.row_even.refs_11_ = f32[32,384]{1,0:T(8,128)S(1)} collective-permute-done((f32[32,384]{1,0:T(8,128)S(1)}, f32[32,384]{1,0:T(8,128)S(1)}, u32[]{:S(2)}, u32[]{:S(2)}) %collective-permute-start.5) | collective-permute-done | bytes 49184 | tf_op jit(solution)/shard_map/ppermute | solution.py:506
  63.4 0.1 shard_map.100
  63.5 5.1 %collective-permute-start.6 = (f32[64,128]{1,0:T(8,128)S(1)}, f32[64,128]{1,0:T(8,128)S(1)}, u32[]{:S(2)}, u32[]{:S(2)}) collective-permute-start(f32[64,128]{1,0:T(8,128)S(1)} %get-tuple-element.48), channel_id=1, source_target_pairs={{1,2},{2,1},{3,4},{4,3},{5,6},{6,5},{7,8},{8,7},{9,10},{10,9},{11,... | collective-permute-start | bytes 98312 | tf_op jit(solution)/shard_map/ppermute | solution.py:507
  68.7 1.9 %collective-permute-start.7 = (f32[64,128]{1,0:T(8,128)S(1)}, f32[64,128]{1,0:T(8,128)S(1)}, u32[]{:S(2)}, u32[]{:S(2)}) collective-permute-start(f32[64,128]{1,0:T(8,128)S(1)} %get-tuple-element.49), channel_id=1, source_target_pairs={{0,1},{1,0},{2,3},{3,2},{4,5},{5,4},{6,7},{7,6},{8,9},{9,8},{10,11... | collective-permute-start | bytes 98312 | tf_op jit(solution)/shard_map/ppermute | solution.py:506
  70.6 0.0 collective-permute-done.6.refs_2_
  70.6 1.2 collective-permute-done.7.refs_3_
  71.8 1.1 shard_map.101
  72.9 29.1 %all_to_all.27 = f32[512,1,128]{2,1,0:T(1,128)S(1)} all-to-all(f32[512,1,128]{2,1,0:T(1,128)S(1)} %bitcast.21), channel_id=1, replica_groups=mesh['gx'=8,'gy'=64] {'gx','gy'}, dimensions={0} | all-to-all | bytes 524288 | tf_op jit(solution)/shard_map/all_to_all | solution.py:516
  102.0 0.7 shard_map.102
  102.7 0.7 collective-permute-start.8
  103.3 3.8 %collective-permute-start.9 = (f32[24,384]{1,0:T(8,128)S(1)}, f32[24,384]{1,0:T(8,128)S(1)}, u32[]{:S(2)}, u32[]{:S(2)}) collective-permute-start(f32[24,384]{1,0:T(8,128)S(1)} %get-tuple-element.58), channel_id=1, source_target_pairs={{0,64},{64,0},{128,192},{192,128},{256,320},{320,256},{384,448},{4... | collective-permute-start | bytes 110600 | tf_op jit(solution)/shard_map/ppermute | solution.py:506
  107.2 0.0 collective-permute-done.8.row_odd
  107.2 1.3 collective-permute-done.9.row_even
  108.5 0.1 shard_map.103
  108.6 3.8 %collective-permute-start.10 = (f32[48,128]{1,0:T(8,128)S(1)}, f32[48,128]{1,0:T(8,128)S(1)}, u32[]{:S(2)}, u32[]{:S(2)}) collective-permute-start(f32[48,128]{1,0:T(8,128)S(1)} %get-tuple-element.60), channel_id=1, source_target_pairs={{1,2},{2,1},{3,4},{4,3},{5,6},{6,5},{7,8},{8,7},{9,10},{10,9},{11,... | collective-permute-start | bytes 73736 | tf_op jit(solution)/shard_map/ppermute | solution.py:507
  112.4 1.9 %collective-permute-start.11 = (f32[48,128]{1,0:T(8,128)S(1)}, f32[48,128]{1,0:T(8,128)S(1)}, u32[]{:S(2)}, u32[]{:S(2)}) collective-permute-start(f32[48,128]{1,0:T(8,128)S(1)} %get-tuple-element.61), channel_id=1, source_target_pairs={{0,1},{1,0},{2,3},{3,2},{4,5},{5,4},{6,7},{7,6},{8,9},{9,8},{10,11... | collective-permute-start | bytes 73736 | tf_op jit(solution)/shard_map/ppermute | solution.py:506
  114.4 0.0 collective-permute-done.10.odd
  114.4 1.2 collective-permute-done.11.even
  115.5 0.3 shard_map.104
  115.8 16.3 %all_to_all.28 = f32[64,1,128]{2,1,0:T(1,128)S(1)} all-to-all(f32[64,1,128]{2,1,0:T(1,128)S(1)} %bitcast.25), channel_id=1, replica_groups=mesh['gx'=8,'gy'=64] {'gy'}, dimensions={0} | all-to-all | bytes 65536 | tf_op jit(solution)/shard_map/all_to_all | solution.py:516
  132.1 11.6 %all_to_all.29 = f32[8,1,128]{2,1,0:T(1,128)S(1)} all-to-all(f32[8,1,128]{2,1,0:T(1,128)S(1)} %bitcast.27), channel_id=1, replica_groups=mesh['gx'=8,'gy'=64] {'gx'}, dimensions={0} | all-to-all | bytes 8192 | tf_op jit(solution)/shard_map/all_to_all | solution.py:516
  143.8 0.9 shard_map.106
  (1 shorter events, 0.0 us)
Async XLA Ops:
  0.6 19.3 %copy-start = (f32[32,18432]{1,0:T(8,128)S(1)}, f32[32,18432]{1,0:T(8,128)}, u32[]{:S(2)}) copy-start(f32[32,18432]{1,0:T(8,128)} %refs_3_.3) | copy-start | bytes 7077892
  1.8 55.4 %copy-start.1 = (f32[32,16384]{1,0:T(8,128)S(1)}, f32[32,16384]{1,0:T(8,128)}, u32[]{:S(2)}) copy-start(f32[32,16384]{1,0:T(8,128)} %refs_2_.3) | copy-start | bytes 6291460
  1.8 7.4 %collective-permute-start = (f32[256,128]{1,0:T(8,128)S(1)}, f32[256,128]{1,0:T(8,128)S(1)}, u32[]{:S(2)}, u32[]{:S(2)}) collective-permute-start(f32[256,128]{1,0:T(8,128)S(1)} %get-tuple-element.36), channel_id=1, source_target_pairs={{64,128},{128,64},{192,256},{256,192},{320,384},{384,320},{65,129}... | collective-permute-start | bytes 393224 | tf_op jit(solution)/shard_map/ppermute | solution.py:507
  2.6 8.9 %collective-permute-start.1 = (f32[256,128]{1,0:T(8,128)S(1)}, f32[256,128]{1,0:T(8,128)S(1)}, u32[]{:S(2)}, u32[]{:S(2)}) collective-permute-start(f32[256,128]{1,0:T(8,128)S(1)} %get-tuple-element.37), channel_id=1, source_target_pairs={{0,64},{64,0},{128,192},{192,128},{256,320},{320,256},{384,448},{4... | collective-permute-start | bytes 393224 | tf_op jit(solution)/shard_map/ppermute | solution.py:506
  11.7 8.1 %collective-permute-start.2 = (f32[64,128]{1,0:T(8,128)S(1)}, f32[64,128]{1,0:T(8,128)S(1)}, u32[]{:S(2)}, u32[]{:S(2)}) collective-permute-start(f32[64,128]{1,0:T(8,128)S(1)} %get-tuple-element.39), channel_id=1, source_target_pairs={{1,2},{2,1},{3,4},{4,3},{5,6},{6,5},{7,8},{8,7},{9,10},{10,9},{11,... | collective-permute-start | bytes 98312 | tf_op jit(solution)/shard_map/ppermute | solution.py:507
  16.8 3.1 %collective-permute-start.3 = (f32[64,128]{1,0:T(8,128)S(1)}, f32[64,128]{1,0:T(8,128)S(1)}, u32[]{:S(2)}, u32[]{:S(2)}) collective-permute-start(f32[64,128]{1,0:T(8,128)S(1)} %get-tuple-element.40), channel_id=1, source_target_pairs={{0,1},{1,0},{2,3},{3,2},{4,5},{5,4},{6,7},{7,6},{8,9},{9,8},{10,11... | collective-permute-start | bytes 98312 | tf_op jit(solution)/shard_map/ppermute | solution.py:506
  57.8 4.2 %collective-permute-start.4 = (f32[32,384]{1,0:T(8,128)S(1)}, f32[32,384]{1,0:T(8,128)S(1)}, u32[]{:S(2)}, u32[]{:S(2)}) collective-permute-start(f32[32,384]{1,0:T(8,128)S(1)} %get-tuple-element.45), channel_id=1, source_target_pairs={{64,128},{128,64},{192,256},{256,192},{320,384},{384,320},{65,129}... | collective-permute-start | bytes 147464 | tf_op jit(solution)/shard_map/ppermute | solution.py:507
  58.4 5.0 %collective-permute-start.5 = (f32[32,384]{1,0:T(8,128)S(1)}, f32[32,384]{1,0:T(8,128)S(1)}, u32[]{:S(2)}, u32[]{:S(2)}) collective-permute-start(f32[32,384]{1,0:T(8,128)S(1)} %get-tuple-element.46), channel_id=1, source_target_pairs={{0,64},{64,0},{128,192},{192,128},{256,320},{320,256},{384,448},{4... | collective-permute-start | bytes 147464 | tf_op jit(solution)/shard_map/ppermute | solution.py:506
  63.5 7.1 %collective-permute-start.6 = (f32[64,128]{1,0:T(8,128)S(1)}, f32[64,128]{1,0:T(8,128)S(1)}, u32[]{:S(2)}, u32[]{:S(2)}) collective-permute-start(f32[64,128]{1,0:T(8,128)S(1)} %get-tuple-element.48), channel_id=1, source_target_pairs={{1,2},{2,1},{3,4},{4,3},{5,6},{6,5},{7,8},{8,7},{9,10},{10,9},{11,... | collective-permute-start | bytes 98312 | tf_op jit(solution)/shard_map/ppermute | solution.py:507
  68.7 3.1 %collective-permute-start.7 = (f32[64,128]{1,0:T(8,128)S(1)}, f32[64,128]{1,0:T(8,128)S(1)}, u32[]{:S(2)}, u32[]{:S(2)}) collective-permute-start(f32[64,128]{1,0:T(8,128)S(1)} %get-tuple-element.49), channel_id=1, source_target_pairs={{0,1},{1,0},{2,3},{3,2},{4,5},{5,4},{6,7},{7,6},{8,9},{9,8},{10,11... | collective-permute-start | bytes 98312 | tf_op jit(solution)/shard_map/ppermute | solution.py:506
  102.7 4.5 %collective-permute-start.8 = (f32[24,384]{1,0:T(8,128)S(1)}, f32[24,384]{1,0:T(8,128)S(1)}, u32[]{:S(2)}, u32[]{:S(2)}) collective-permute-start(f32[24,384]{1,0:T(8,128)S(1)} %get-tuple-element.57), channel_id=1, source_target_pairs={{64,128},{128,64},{192,256},{256,192},{320,384},{384,320},{65,129}... | collective-permute-start | bytes 110600 | tf_op jit(solution)/shard_map/ppermute | solution.py:507
  103.3 5.2 %collective-permute-start.9 = (f32[24,384]{1,0:T(8,128)S(1)}, f32[24,384]{1,0:T(8,128)S(1)}, u32[]{:S(2)}, u32[]{:S(2)}) collective-permute-start(f32[24,384]{1,0:T(8,128)S(1)} %get-tuple-element.58), channel_id=1, source_target_pairs={{0,64},{64,0},{128,192},{192,128},{256,320},{320,256},{384,448},{4... | collective-permute-start | bytes 110600 | tf_op jit(solution)/shard_map/ppermute | solution.py:506
  108.6 5.7 %collective-permute-start.10 = (f32[48,128]{1,0:T(8,128)S(1)}, f32[48,128]{1,0:T(8,128)S(1)}, u32[]{:S(2)}, u32[]{:S(2)}) collective-permute-start(f32[48,128]{1,0:T(8,128)S(1)} %get-tuple-element.60), channel_id=1, source_target_pairs={{1,2},{2,1},{3,4},{4,3},{5,6},{6,5},{7,8},{8,7},{9,10},{10,9},{11,... | collective-permute-start | bytes 73736 | tf_op jit(solution)/shard_map/ppermute | solution.py:507
  112.4 3.1 %collective-permute-start.11 = (f32[48,128]{1,0:T(8,128)S(1)}, f32[48,128]{1,0:T(8,128)S(1)}, u32[]{:S(2)}, u32[]{:S(2)}) collective-permute-start(f32[48,128]{1,0:T(8,128)S(1)} %get-tuple-element.61), channel_id=1, source_target_pairs={{0,1},{1,0},{2,3},{3,2},{4,5},{5,4},{6,7},{7,6},{8,9},{9,8},{10,11... | collective-permute-start | bytes 73736 | tf_op jit(solution)/shard_map/ppermute | solution.py:506

commit v7 on v6

--- a/solution.py
+++ b/solution.py
@@ -173,7 +173,7 @@
 
 
 def pick(row, lane):
-    return jnp.sum(jnp.where(lanes_of(row.shape) == lane, row, 0.0), axis=1, keepdims=True)
+    return row[:, lane : lane + 1]
 
 
 def coarse_solve(inverse, coarse):
@@ -263,12 +263,11 @@
     for f in range(5):
         middle = pltpu.roll(jnp.concatenate([rows[f], zero], axis=1), OV, 1)
         band = (lanes >= STRIP * f) & (lanes < STRIP * f + 17)
-        wide = jnp.zeros((PX, LW - 128), f32)
-        one = jnp.concatenate([jnp.where(band, from_left, 0.0), wide], axis=1)
-        two = jnp.concatenate([jnp.where(band, from_right, 0.0), wide], axis=1)
-        one = pltpu.roll(one, LW - 1 - STRIP * f, 1)
-        two = pltpu.roll(two, OV + CY - STRIP * f, 1)
-        fields.append(middle + one + two)
+        one = pltpu.roll(jnp.where(band, from_left, 0.0), 127 - STRIP * f, 1)
+        two = pltpu.roll(jnp.where(band, from_right, 0.0), (128 + OV - STRIP * f) % 128, 1)
+        one, end = jnp.where(lanes < OV, one, 0.0), jnp.where(lanes == 127, one, 0.0)
+        sides = jnp.concatenate([one, jnp.zeros((PX, 128), f32), two + end], axis=1)
+        fields.append(middle + sides)
     source, potential, along, across, recombination = fields
     weight = jnp.sqrt(along * up(along))
     rise = 0.5 * (up(potential) - potential)
@@ -331,21 +330,22 @@
     whole = jnp.where(lanes_of(whole.shape) < PY, whole, 0.0)
     folded[...] = whole
     lanes = lanes_of((height, 128))
-    moved = pltpu.roll(whole, LW - 255, 1)
+    moved = pltpu.roll(jnp.where(lanes == 127, whole[:, 128:256], whole[:, 256:]), 1, 1)
     odd[...], even[...] = to_pairs(
         "gy",
-        jnp.where(lanes < 33, moved[:, :128], 0.0),
+        jnp.where(lanes < 33, moved, 0.0),
         jnp.where(lanes < 33, whole[:, :128], 0.0),
     )
 
 
 def folded_columns(folded, odd, even):
     height = folded.shape[0]
-    zero = jnp.zeros((height, 256), f32)
     from_left, from_right = from_pairs("gy", odd[...], even[...])
-    one = pltpu.roll(jnp.concatenate([from_left, zero], axis=1), LW - 1, 1)
-    two = jnp.concatenate([zero, from_right], axis=1)
-    return folded[...] + one + two
+    lanes = lanes_of((height, 128))
+    one = pltpu.roll(from_left, 127, 1)
+    one, end = jnp.where(lanes < 32, one, 0.0), jnp.where(lanes == 127, one, 0.0)
+    sides = jnp.concatenate([one, jnp.zeros((height, 128), f32), from_right + end], axis=1)
+    return folded[...] + sides
 
 
 def apply_first(
@@ -409,6 +409,10 @@
     put(scalars, 1, unit)
     put(scalars, 2, cross)
     put(scalars, 3, second)
+    radius = 1.0 / jnp.sqrt(cross * cross + second * second)
+    put(scalars, 4, radius)
+    put(scalars, 5, 1.0 / norm)
+    put(scalars, 6, scale)
     part[...] = prolong(basis, solution, tiles, flat)
     local = (solved[...] - (cross / norm) * solved_first[...]) * scale
     part[8:56, :] = part[8:56, :] + local
@@ -424,8 +428,8 @@
     direction[...] = field[8 : 8 + CX]
     vector = jnp.where(own, vector[8 : 8 + CX], 0.0)
     third[...] = vector
-    first = jnp.where(own, patch[OV : OV + CX] * (1.0 / got(scalars, 0)), 0.0)
-    second = (image[...] - got(scalars, 2) * first) * (1.0 / got(scalars, 3))
+    first = jnp.where(own, patch[OV : OV + CX] * got(scalars, 5), 0.0)
+    second = (image[...] - got(scalars, 2) * first) * got(scalars, 6)
     second = jnp.where(own, second, 0.0)
     lanes = lanes_of((1, 128))
     row = jnp.zeros((1, 128), f32)
@@ -452,26 +456,24 @@
     unit = got(scalars, 1)
     first_first = got(scalars, 2)
     second_first = got(scalars, 3)
+    inverse_radius = got(scalars, 4)
+    cosine = first_first * inverse_radius
+    sine = second_first * inverse_radius
     rest = square - first_second * first_second * (2.0 - unit)
     rest = rest - second_second * second_second * (2.0 - unit_two)
     rest = rest + 2.0 * first_second * second_second * cross
-    third_second = jnp.sqrt(jnp.maximum(rest, 0.0) + EPSILON)
-    radius = jnp.sqrt(first_first * first_first + second_first * second_first)
-    cosine = first_first / radius
-    sine = second_first / radius
+    third_square = jnp.maximum(rest, 0.0) + EPSILON
     upper_right = cosine * first_second + sine * second_second
     lower_right = cosine * second_second - sine * first_second
-    radius_two = jnp.sqrt(lower_right * lower_right + third_second * third_second)
-    weight_two = lower_right / radius_two * (-sine * source_norm) / radius_two
-    weight_one = (cosine * source_norm - upper_right * weight_two) / radius
+    weight_two = lower_right * (-sine * source_norm) / (lower_right * lower_right + third_square)
+    weight_one = (cosine * source_norm - upper_right * weight_two) * inverse_radius
     remainder_one = source_norm - first_first * weight_one - first_second * weight_two
     remainder_two = -second_first * weight_one - second_second * weight_two
-    remainder_three = -third_second * weight_two
-    first = patch[OV : OV + CX] * (1.0 / source_norm)
-    second = (image[...] - first_first * first) * (1.0 / second_first)
-    third = (third_image[...] - first_second * first - second_second * second) * (1.0 / third_second)
+    first = patch[OV : OV + CX] * got(scalars, 5)
+    second = (image[...] - first_first * first) * got(scalars, 6)
+    third = third_image[...] - first_second * first - second_second * second
     found = weight_one * direction_one[...] + weight_two * direction_two[...]
-    left_over = remainder_one * first + remainder_two * second + remainder_three * third
+    left_over = remainder_one * first + remainder_two * second - weight_two * third
     solution[...] = pltpu.roll(found, LW - OV, 1)[:, :CY]
     residual[...] = pltpu.roll(left_over, LW - OV, 1)[:, :CY]
 

time: 145 us -> 146 us (level)
  no operation moved by 1% of the time
where the time goes in v7:
time: 146 us; the launch traced here: 145 us
  blocking collectives  92.9 us (64%)
  starting transfers between devices  36.2 us (25%)
  waiting for transfers between devices  7.62 us (5%)
  Pallas kernels  6.74 us (5%)
  between operations  1.48 us (1%)
    all_to_all x5, blocking collectives, everywhere(): return lax.all_to_all(slots, axes, 0, 0).reshape(rows.shape)  92.9 us
    ppermute x6, starting transfers between devices, swap(): even = lax.ppermute(even, axis, [(i, i ^ 1) for i in range(count)])  20.1 us
    ppermute x6, starting transfers between devices, swap(): lax.ppermute(odd, axis, [(i, i + 1 if i % 2 else i - 1) for i in range(1,...  16.1 us
    ppermute x6, waiting for transfers between devices, swap(): even = lax.ppermute(even, axis, [(i, i ^ 1) for i in range(count)])  7.6 us
    pallas_call x11, Pallas kernels, call(): pl.pallas_call(body, out_shape=outs, in_specs=specs, out_specs=[VMEM] * l...  5.6 us
  transfers between devices with their start and end apart: 12, of which 6 were waited for; matrix products, arithmetic and copies ran while one was open for 0% of the time, Pallas kernels for 0%

profile of v7, /device:TPU:1, one launch (start us, length us, event | category | flops | bytes accessed | tf_op | source)
XLA Modules:
  0.0 144.9 jit_solution(1803967036049195176)
XLA Ops:
  0.6 0.0 copy-start
  0.6 1.1 shard_map.95
  1.8 0.0 copy-start.1
  1.8 0.8 collective-permute-start
  2.6 6.6 %collective-permute-start.1 = (f32[256,128]{1,0:T(8,128)S(1)}, f32[256,128]{1,0:T(8,128)S(1)}, u32[]{:S(2)}, u32[]{:S(2)}) collective-permute-start(f32[256,128]{1,0:T(8,128)S(1)} %get-tuple-element.37), channel_id=1, source_target_pairs={{0,64},{64,0},{128,192},{192,128},{256,320},{320,256},{384,448},{4... | collective-permute-start | bytes 393224 | tf_op jit(solution)/shard_map/ppermute | solution.py:508
  9.2 0.0 collective-permute-done.row_odd.refs_8_
  9.2 2.3 %collective-permute-done.1.row_even.refs_9_ = f32[256,128]{1,0:T(8,128)S(1)} collective-permute-done((f32[256,128]{1,0:T(8,128)S(1)}, f32[256,128]{1,0:T(8,128)S(1)}, u32[]{:S(2)}, u32[]{:S(2)}) %collective-permute-start.1) | collective-permute-done | bytes 131104 | tf_op jit(solution)/shard_map/ppermute | solution.py:508
  11.5 0.1 shard_map.96
  11.7 5.1 %collective-permute-start.2 = (f32[64,128]{1,0:T(8,128)S(1)}, f32[64,128]{1,0:T(8,128)S(1)}, u32[]{:S(2)}, u32[]{:S(2)}) collective-permute-start(f32[64,128]{1,0:T(8,128)S(1)} %get-tuple-element.39), channel_id=1, source_target_pairs={{1,2},{2,1},{3,4},{4,3},{5,6},{6,5},{7,8},{8,7},{9,10},{10,9},{11,... | collective-permute-start | bytes 98312 | tf_op jit(solution)/shard_map/ppermute | solution.py:509
  16.8 2.3 %collective-permute-start.3 = (f32[64,128]{1,0:T(8,128)S(1)}, f32[64,128]{1,0:T(8,128)S(1)}, u32[]{:S(2)}, u32[]{:S(2)}) collective-permute-start(f32[64,128]{1,0:T(8,128)S(1)} %get-tuple-element.40), channel_id=1, source_target_pairs={{0,1},{1,0},{2,3},{3,2},{4,5},{5,4},{6,7},{7,6},{8,9},{9,8},{10,11... | collective-permute-start | bytes 98312 | tf_op jit(solution)/shard_map/ppermute | solution.py:508
  19.7 0.0 collective-permute-done.2.refs_2_
  19.8 0.2 collective-permute-done.3.refs_3_
  19.9 0.0 copy-done
  19.9 1.3 shard_map.97
  21.2 22.4 %all_to_all.25 = f32[64,1,128]{2,1,0:T(1,128)S(1)} all-to-all(f32[64,1,128]{2,1,0:T(1,128)S(1)} %bitcast.24), channel_id=1, replica_groups=mesh['gx'=8,'gy'=64] {'gy'}, dimensions={0} | all-to-all | bytes 65536 | tf_op jit(solution)/shard_map/all_to_all | solution.py:518
  43.7 0.1 shard_map.98
  43.8 13.4 %all_to_all.26 = f32[8,24,128]{2,1,0:T(8,128)S(1)} all-to-all(f32[8,24,128]{2,1,0:T(8,128)S(1)} %bitcast.19), channel_id=1, replica_groups=mesh['gx'=8,'gy'=64] {'gx'}, dimensions={0} | all-to-all | bytes 196608 | tf_op jit(solution)/shard_map/all_to_all | solution.py:518
  57.1 0.0 copy-done.1
  57.1 0.7 shard_map.99
  57.8 0.7 collective-permute-start.4
  58.5 3.5 %collective-permute-start.5 = (f32[32,384]{1,0:T(8,128)S(1)}, f32[32,384]{1,0:T(8,128)S(1)}, u32[]{:S(2)}, u32[]{:S(2)}) collective-permute-start(f32[32,384]{1,0:T(8,128)S(1)} %get-tuple-element.46), channel_id=1, source_target_pairs={{0,64},{64,0},{128,192},{192,128},{256,320},{320,256},{384,448},{4... | collective-permute-start | bytes 147464 | tf_op jit(solution)/shard_map/ppermute | solution.py:508
  62.0 0.0 collective-permute-done.4.row_odd.refs_10_
  62.0 1.5 %collective-permute-done.5.row_even.refs_11_ = f32[32,384]{1,0:T(8,128)S(1)} collective-permute-done((f32[32,384]{1,0:T(8,128)S(1)}, f32[32,384]{1,0:T(8,128)S(1)}, u32[]{:S(2)}, u32[]{:S(2)}) %collective-permute-start.5) | collective-permute-done | bytes 49184 | tf_op jit(solution)/shard_map/ppermute | solution.py:508
  63.5 0.1 shard_map.100
  63.6 5.1 %collective-permute-start.6 = (f32[64,128]{1,0:T(8,128)S(1)}, f32[64,128]{1,0:T(8,128)S(1)}, u32[]{:S(2)}, u32[]{:S(2)}) collective-permute-start(f32[64,128]{1,0:T(8,128)S(1)} %get-tuple-element.48), channel_id=1, source_target_pairs={{1,2},{2,1},{3,4},{4,3},{5,6},{6,5},{7,8},{8,7},{9,10},{10,9},{11,... | collective-permute-start | bytes 98312 | tf_op jit(solution)/shard_map/ppermute | solution.py:509
  68.7 1.9 %collective-permute-start.7 = (f32[64,128]{1,0:T(8,128)S(1)}, f32[64,128]{1,0:T(8,128)S(1)}, u32[]{:S(2)}, u32[]{:S(2)}) collective-permute-start(f32[64,128]{1,0:T(8,128)S(1)} %get-tuple-element.49), channel_id=1, source_target_pairs={{0,1},{1,0},{2,3},{3,2},{4,5},{5,4},{6,7},{7,6},{8,9},{9,8},{10,11... | collective-permute-start | bytes 98312 | tf_op jit(solution)/shard_map/ppermute | solution.py:508
  70.6 0.0 collective-permute-done.6.refs_2_
  70.6 1.2 collective-permute-done.7.refs_3_
  71.8 1.1 shard_map.101
  72.9 29.1 %all_to_all.27 = f32[512,1,128]{2,1,0:T(1,128)S(1)} all-to-all(f32[512,1,128]{2,1,0:T(1,128)S(1)} %bitcast.21), channel_id=1, replica_groups=mesh['gx'=8,'gy'=64] {'gx','gy'}, dimensions={0} | all-to-all | bytes 524288 | tf_op jit(solution)/shard_map/all_to_all | solution.py:518
  102.0 0.7 shard_map.102
  102.7 0.7 collective-permute-start.8
  103.4 3.8 %collective-permute-start.9 = (f32[24,384]{1,0:T(8,128)S(1)}, f32[24,384]{1,0:T(8,128)S(1)}, u32[]{:S(2)}, u32[]{:S(2)}) collective-permute-start(f32[24,384]{1,0:T(8,128)S(1)} %get-tuple-element.58), channel_id=1, source_target_pairs={{0,64},{64,0},{128,192},{192,128},{256,320},{320,256},{384,448},{4... | collective-permute-start | bytes 110600 | tf_op jit(solution)/shard_map/ppermute | solution.py:508
  107.3 0.0 collective-permute-done.8.row_odd
  107.3 1.3 collective-permute-done.9.row_even
  108.6 0.1 shard_map.103
  108.7 3.8 %collective-permute-start.10 = (f32[48,128]{1,0:T(8,128)S(1)}, f32[48,128]{1,0:T(8,128)S(1)}, u32[]{:S(2)}, u32[]{:S(2)}) collective-permute-start(f32[48,128]{1,0:T(8,128)S(1)} %get-tuple-element.60), channel_id=1, source_target_pairs={{1,2},{2,1},{3,4},{4,3},{5,6},{6,5},{7,8},{8,7},{9,10},{10,9},{11,... | collective-permute-start | bytes 73736 | tf_op jit(solution)/shard_map/ppermute | solution.py:509
  112.5 1.9 %collective-permute-start.11 = (f32[48,128]{1,0:T(8,128)S(1)}, f32[48,128]{1,0:T(8,128)S(1)}, u32[]{:S(2)}, u32[]{:S(2)}) collective-permute-start(f32[48,128]{1,0:T(8,128)S(1)} %get-tuple-element.61), channel_id=1, source_target_pairs={{0,1},{1,0},{2,3},{3,2},{4,5},{5,4},{6,7},{7,6},{8,9},{9,8},{10,11... | collective-permute-start | bytes 73736 | tf_op jit(solution)/shard_map/ppermute | solution.py:508
  114.4 0.0 collective-permute-done.10.odd
  114.4 1.2 collective-permute-done.11.even
  115.6 0.3 shard_map.104
  115.8 16.3 %all_to_all.28 = f32[64,1,128]{2,1,0:T(1,128)S(1)} all-to-all(f32[64,1,128]{2,1,0:T(1,128)S(1)} %bitcast.25), channel_id=1, replica_groups=mesh['gx'=8,'gy'=64] {'gy'}, dimensions={0} | all-to-all | bytes 65536 | tf_op jit(solution)/shard_map/all_to_all | solution.py:518
  132.2 11.6 %all_to_all.29 = f32[8,1,128]{2,1,0:T(1,128)S(1)} all-to-all(f32[8,1,128]{2,1,0:T(1,128)S(1)} %bitcast.27), channel_id=1, replica_groups=mesh['gx'=8,'gy'=64] {'gx'}, dimensions={0} | all-to-all | bytes 8192 | tf_op jit(solution)/shard_map/all_to_all | solution.py:518
  143.8 1.1 shard_map.106
  (1 shorter events, 0.0 us)
Async XLA Ops:
  0.6 19.3 %copy-start = (f32[32,18432]{1,0:T(8,128)S(1)}, f32[32,18432]{1,0:T(8,128)}, u32[]{:S(2)}) copy-start(f32[32,18432]{1,0:T(8,128)} %refs_3_.3) | copy-start | bytes 7077892
  1.8 55.4 %copy-start.1 = (f32[32,16384]{1,0:T(8,128)S(1)}, f32[32,16384]{1,0:T(8,128)}, u32[]{:S(2)}) copy-start(f32[32,16384]{1,0:T(8,128)} %refs_2_.3) | copy-start | bytes 6291460
  1.8 7.4 %collective-permute-start = (f32[256,128]{1,0:T(8,128)S(1)}, f32[256,128]{1,0:T(8,128)S(1)}, u32[]{:S(2)}, u32[]{:S(2)}) collective-permute-start(f32[256,128]{1,0:T(8,128)S(1)} %get-tuple-element.36), channel_id=1, source_target_pairs={{64,128},{128,64},{192,256},{256,192},{320,384},{384,320},{65,129}... | collective-permute-start | bytes 393224 | tf_op jit(solution)/shard_map/ppermute | solution.py:509
  2.6 8.9 %collective-permute-start.1 = (f32[256,128]{1,0:T(8,128)S(1)}, f32[256,128]{1,0:T(8,128)S(1)}, u32[]{:S(2)}, u32[]{:S(2)}) collective-permute-start(f32[256,128]{1,0:T(8,128)S(1)} %get-tuple-element.37), channel_id=1, source_target_pairs={{0,64},{64,0},{128,192},{192,128},{256,320},{320,256},{384,448},{4... | collective-permute-start | bytes 393224 | tf_op jit(solution)/shard_map/ppermute | solution.py:508
  11.7 8.1 %collective-permute-start.2 = (f32[64,128]{1,0:T(8,128)S(1)}, f32[64,128]{1,0:T(8,128)S(1)}, u32[]{:S(2)}, u32[]{:S(2)}) collective-permute-start(f32[64,128]{1,0:T(8,128)S(1)} %get-tuple-element.39), channel_id=1, source_target_pairs={{1,2},{2,1},{3,4},{4,3},{5,6},{6,5},{7,8},{8,7},{9,10},{10,9},{11,... | collective-permute-start | bytes 98312 | tf_op jit(solution)/shard_map/ppermute | solution.py:509
  16.8 3.1 %collective-permute-start.3 = (f32[64,128]{1,0:T(8,128)S(1)}, f32[64,128]{1,0:T(8,128)S(1)}, u32[]{:S(2)}, u32[]{:S(2)}) collective-permute-start(f32[64,128]{1,0:T(8,128)S(1)} %get-tuple-element.40), channel_id=1, source_target_pairs={{0,1},{1,0},{2,3},{3,2},{4,5},{5,4},{6,7},{7,6},{8,9},{9,8},{10,11... | collective-permute-start | bytes 98312 | tf_op jit(solution)/shard_map/ppermute | solution.py:508
  57.8 4.2 %collective-permute-start.4 = (f32[32,384]{1,0:T(8,128)S(1)}, f32[32,384]{1,0:T(8,128)S(1)}, u32[]{:S(2)}, u32[]{:S(2)}) collective-permute-start(f32[32,384]{1,0:T(8,128)S(1)} %get-tuple-element.45), channel_id=1, source_target_pairs={{64,128},{128,64},{192,256},{256,192},{320,384},{384,320},{65,129}... | collective-permute-start | bytes 147464 | tf_op jit(solution)/shard_map/ppermute | solution.py:509
  58.5 5.0 %collective-permute-start.5 = (f32[32,384]{1,0:T(8,128)S(1)}, f32[32,384]{1,0:T(8,128)S(1)}, u32[]{:S(2)}, u32[]{:S(2)}) collective-permute-start(f32[32,384]{1,0:T(8,128)S(1)} %get-tuple-element.46), channel_id=1, source_target_pairs={{0,64},{64,0},{128,192},{192,128},{256,320},{320,256},{384,448},{4... | collective-permute-start | bytes 147464 | tf_op jit(solution)/shard_map/ppermute | solution.py:508
  63.6 7.1 %collective-permute-start.6 = (f32[64,128]{1,0:T(8,128)S(1)}, f32[64,128]{1,0:T(8,128)S(1)}, u32[]{:S(2)}, u32[]{:S(2)}) collective-permute-start(f32[64,128]{1,0:T(8,128)S(1)} %get-tuple-element.48), channel_id=1, source_target_pairs={{1,2},{2,1},{3,4},{4,3},{5,6},{6,5},{7,8},{8,7},{9,10},{10,9},{11,... | collective-permute-start | bytes 98312 | tf_op jit(solution)/shard_map/ppermute | solution.py:509
  68.7 3.1 %collective-permute-start.7 = (f32[64,128]{1,0:T(8,128)S(1)}, f32[64,128]{1,0:T(8,128)S(1)}, u32[]{:S(2)}, u32[]{:S(2)}) collective-permute-start(f32[64,128]{1,0:T(8,128)S(1)} %get-tuple-element.49), channel_id=1, source_target_pairs={{0,1},{1,0},{2,3},{3,2},{4,5},{5,4},{6,7},{7,6},{8,9},{9,8},{10,11... | collective-permute-start | bytes 98312 | tf_op jit(solution)/shard_map/ppermute | solution.py:508
  102.7 4.5 %collective-permute-start.8 = (f32[24,384]{1,0:T(8,128)S(1)}, f32[24,384]{1,0:T(8,128)S(1)}, u32[]{:S(2)}, u32[]{:S(2)}) collective-permute-start(f32[24,384]{1,0:T(8,128)S(1)} %get-tuple-element.57), channel_id=1, source_target_pairs={{64,128},{128,64},{192,256},{256,192},{320,384},{384,320},{65,129}... | collective-permute-start | bytes 110600 | tf_op jit(solution)/shard_map/ppermute | solution.py:509
  103.4 5.2 %collective-permute-start.9 = (f32[24,384]{1,0:T(8,128)S(1)}, f32[24,384]{1,0:T(8,128)S(1)}, u32[]{:S(2)}, u32[]{:S(2)}) collective-permute-start(f32[24,384]{1,0:T(8,128)S(1)} %get-tuple-element.58), channel_id=1, source_target_pairs={{0,64},{64,0},{128,192},{192,128},{256,320},{320,256},{384,448},{4... | collective-permute-start | bytes 110600 | tf_op jit(solution)/shard_map/ppermute | solution.py:508
  108.7 5.7 %collective-permute-start.10 = (f32[48,128]{1,0:T(8,128)S(1)}, f32[48,128]{1,0:T(8,128)S(1)}, u32[]{:S(2)}, u32[]{:S(2)}) collective-permute-start(f32[48,128]{1,0:T(8,128)S(1)} %get-tuple-element.60), channel_id=1, source_target_pairs={{1,2},{2,1},{3,4},{4,3},{5,6},{6,5},{7,8},{8,7},{9,10},{10,9},{11,... | collective-permute-start | bytes 73736 | tf_op jit(solution)/shard_map/ppermute | solution.py:509
  112.5 3.1 %collective-permute-start.11 = (f32[48,128]{1,0:T(8,128)S(1)}, f32[48,128]{1,0:T(8,128)S(1)}, u32[]{:S(2)}, u32[]{:S(2)}) collective-permute-start(f32[48,128]{1,0:T(8,128)S(1)} %get-tuple-element.61), channel_id=1, source_target_pairs={{0,1},{1,0},{2,3},{3,2},{4,5},{5,4},{6,7},{7,6},{8,9},{9,8},{10,11... | collective-permute-start | bytes 73736 | tf_op jit(solution)/shard_map/ppermute | solution.py:508

commit v8 on v7

--- a/solution.py
+++ b/solution.py
@@ -173,7 +173,7 @@
 
 
 def pick(row, lane):
-    return row[:, lane : lane + 1]
+    return jnp.sum(jnp.where(lanes_of(row.shape) == lane, row, 0.0), axis=1, keepdims=True)
 
 
 def coarse_solve(inverse, coarse):

time: 146 us -> 145 us (level)
  no operation moved by 1% of the time
where the time goes in v8:
time: 145 us
  blocking collectives  92.9 us (64%)
  starting transfers between devices  36.2 us (25%)
  waiting for transfers between devices  7.62 us (5%)
  Pallas kernels  6.4 us (4%)
  between operations  1.48 us (1%)
    all_to_all x5, blocking collectives, everywhere(): return lax.all_to_all(slots, axes, 0, 0).reshape(rows.shape)  92.9 us
    ppermute x6, starting transfers between devices, swap(): even = lax.ppermute(even, axis, [(i, i ^ 1) for i in range(count)])  20.1 us
    ppermute x6, starting transfers between devices, swap(): lax.ppermute(odd, axis, [(i, i + 1 if i % 2 else i - 1) for i in range(1,...  16.1 us
    ppermute x6, waiting for transfers between devices, swap(): even = lax.ppermute(even, axis, [(i, i ^ 1) for i in range(count)])  7.6 us
    pallas_call x11, Pallas kernels, call(): pl.pallas_call(body, out_shape=outs, in_specs=specs, out_specs=[VMEM] * l...  5.26 us
  transfers between devices with their start and end apart: 12, of which 6 were waited for; matrix products, arithmetic and copies ran while one was open for 0% of the time, Pallas kernels for 0%

profile of v8, /device:TPU:1, one launch (start us, length us, event | category | flops | bytes accessed | tf_op | source)
XLA Modules:
  0.0 144.6 jit_solution(2915572729364790008)
XLA Ops:
  0.6 0.0 copy-start
  0.6 1.1 shard_map.95
  1.8 0.0 copy-start.1
  1.8 0.8 collective-permute-start
  2.6 6.6 %collective-permute-start.1 = (f32[256,128]{1,0:T(8,128)S(1)}, f32[256,128]{1,0:T(8,128)S(1)}, u32[]{:S(2)}, u32[]{:S(2)}) collective-permute-start(f32[256,128]{1,0:T(8,128)S(1)} %get-tuple-element.37), channel_id=1, source_target_pairs={{0,64},{64,0},{128,192},{192,128},{256,320},{320,256},{384,448},{4... | collective-permute-start | bytes 393224 | tf_op jit(solution)/shard_map/ppermute | solution.py:508
  9.2 0.0 collective-permute-done.row_odd.refs_8_
  9.2 2.3 %collective-permute-done.1.row_even.refs_9_ = f32[256,128]{1,0:T(8,128)S(1)} collective-permute-done((f32[256,128]{1,0:T(8,128)S(1)}, f32[256,128]{1,0:T(8,128)S(1)}, u32[]{:S(2)}, u32[]{:S(2)}) %collective-permute-start.1) | collective-permute-done | bytes 131104 | tf_op jit(solution)/shard_map/ppermute | solution.py:508
  11.5 0.1 shard_map.96
  11.7 5.1 %collective-permute-start.2 = (f32[64,128]{1,0:T(8,128)S(1)}, f32[64,128]{1,0:T(8,128)S(1)}, u32[]{:S(2)}, u32[]{:S(2)}) collective-permute-start(f32[64,128]{1,0:T(8,128)S(1)} %get-tuple-element.39), channel_id=1, source_target_pairs={{1,2},{2,1},{3,4},{4,3},{5,6},{6,5},{7,8},{8,7},{9,10},{10,9},{11,... | collective-permute-start | bytes 98312 | tf_op jit(solution)/shard_map/ppermute | solution.py:509
  16.8 2.3 %collective-permute-start.3 = (f32[64,128]{1,0:T(8,128)S(1)}, f32[64,128]{1,0:T(8,128)S(1)}, u32[]{:S(2)}, u32[]{:S(2)}) collective-permute-start(f32[64,128]{1,0:T(8,128)S(1)} %get-tuple-element.40), channel_id=1, source_target_pairs={{0,1},{1,0},{2,3},{3,2},{4,5},{5,4},{6,7},{7,6},{8,9},{9,8},{10,11... | collective-permute-start | bytes 98312 | tf_op jit(solution)/shard_map/ppermute | solution.py:508
  19.7 0.0 collective-permute-done.2.refs_2_
  19.8 0.2 collective-permute-done.3.refs_3_
  19.9 0.0 copy-done
  19.9 1.3 shard_map.97
  21.2 22.4 %all_to_all.25 = f32[64,1,128]{2,1,0:T(1,128)S(1)} all-to-all(f32[64,1,128]{2,1,0:T(1,128)S(1)} %bitcast.24), channel_id=1, replica_groups=mesh['gx'=8,'gy'=64] {'gy'}, dimensions={0} | all-to-all | bytes 65536 | tf_op jit(solution)/shard_map/all_to_all | solution.py:518
  43.7 0.1 shard_map.98
  43.8 13.4 %all_to_all.26 = f32[8,24,128]{2,1,0:T(8,128)S(1)} all-to-all(f32[8,24,128]{2,1,0:T(8,128)S(1)} %bitcast.19), channel_id=1, replica_groups=mesh['gx'=8,'gy'=64] {'gx'}, dimensions={0} | all-to-all | bytes 196608 | tf_op jit(solution)/shard_map/all_to_all | solution.py:518
  57.1 0.0 copy-done.1
  57.1 0.6 shard_map.99
  57.7 0.7 collective-permute-start.4
  58.4 3.5 %collective-permute-start.5 = (f32[32,384]{1,0:T(8,128)S(1)}, f32[32,384]{1,0:T(8,128)S(1)}, u32[]{:S(2)}, u32[]{:S(2)}) collective-permute-start(f32[32,384]{1,0:T(8,128)S(1)} %get-tuple-element.46), channel_id=1, source_target_pairs={{0,64},{64,0},{128,192},{192,128},{256,320},{320,256},{384,448},{4... | collective-permute-start | bytes 147464 | tf_op jit(solution)/shard_map/ppermute | solution.py:508
  62.0 0.0 collective-permute-done.4.row_odd.refs_10_
  62.0 1.5 %collective-permute-done.5.row_even.refs_11_ = f32[32,384]{1,0:T(8,128)S(1)} collective-permute-done((f32[32,384]{1,0:T(8,128)S(1)}, f32[32,384]{1,0:T(8,128)S(1)}, u32[]{:S(2)}, u32[]{:S(2)}) %collective-permute-start.5) | collective-permute-done | bytes 49184 | tf_op jit(solution)/shard_map/ppermute | solution.py:508
  63.4 0.1 shard_map.100
  63.5 5.1 %collective-permute-start.6 = (f32[64,128]{1,0:T(8,128)S(1)}, f32[64,128]{1,0:T(8,128)S(1)}, u32[]{:S(2)}, u32[]{:S(2)}) collective-permute-start(f32[64,128]{1,0:T(8,128)S(1)} %get-tuple-element.48), channel_id=1, source_target_pairs={{1,2},{2,1},{3,4},{4,3},{5,6},{6,5},{7,8},{8,7},{9,10},{10,9},{11,... | collective-permute-start | bytes 98312 | tf_op jit(solution)/shard_map/ppermute | solution.py:509
  68.6 1.9 %collective-permute-start.7 = (f32[64,128]{1,0:T(8,128)S(1)}, f32[64,128]{1,0:T(8,128)S(1)}, u32[]{:S(2)}, u32[]{:S(2)}) collective-permute-start(f32[64,128]{1,0:T(8,128)S(1)} %get-tuple-element.49), channel_id=1, source_target_pairs={{0,1},{1,0},{2,3},{3,2},{4,5},{5,4},{6,7},{7,6},{8,9},{9,8},{10,11... | collective-permute-start | bytes 98312 | tf_op jit(solution)/shard_map/ppermute | solution.py:508
  70.6 0.0 collective-permute-done.6.refs_2_
  70.6 1.2 collective-permute-done.7.refs_3_
  71.7 1.1 shard_map.101
  72.9 29.1 %all_to_all.27 = f32[512,1,128]{2,1,0:T(1,128)S(1)} all-to-all(f32[512,1,128]{2,1,0:T(1,128)S(1)} %bitcast.21), channel_id=1, replica_groups=mesh['gx'=8,'gy'=64] {'gx','gy'}, dimensions={0} | all-to-all | bytes 524288 | tf_op jit(solution)/shard_map/all_to_all | solution.py:518
  102.0 0.7 shard_map.102
  102.6 0.7 collective-permute-start.8
  103.3 3.8 %collective-permute-start.9 = (f32[24,384]{1,0:T(8,128)S(1)}, f32[24,384]{1,0:T(8,128)S(1)}, u32[]{:S(2)}, u32[]{:S(2)}) collective-permute-start(f32[24,384]{1,0:T(8,128)S(1)} %get-tuple-element.58), channel_id=1, source_target_pairs={{0,64},{64,0},{128,192},{192,128},{256,320},{320,256},{384,448},{4... | collective-permute-start | bytes 110600 | tf_op jit(solution)/shard_map/ppermute | solution.py:508
  107.2 0.0 collective-permute-done.8.row_odd
  107.2 1.3 collective-permute-done.9.row_even
  108.5 0.1 shard_map.103
  108.6 3.8 %collective-permute-start.10 = (f32[48,128]{1,0:T(8,128)S(1)}, f32[48,128]{1,0:T(8,128)S(1)}, u32[]{:S(2)}, u32[]{:S(2)}) collective-permute-start(f32[48,128]{1,0:T(8,128)S(1)} %get-tuple-element.60), channel_id=1, source_target_pairs={{1,2},{2,1},{3,4},{4,3},{5,6},{6,5},{7,8},{8,7},{9,10},{10,9},{11,... | collective-permute-start | bytes 73736 | tf_op jit(solution)/shard_map/ppermute | solution.py:509
  112.4 1.9 %collective-permute-start.11 = (f32[48,128]{1,0:T(8,128)S(1)}, f32[48,128]{1,0:T(8,128)S(1)}, u32[]{:S(2)}, u32[]{:S(2)}) collective-permute-start(f32[48,128]{1,0:T(8,128)S(1)} %get-tuple-element.61), channel_id=1, source_target_pairs={{0,1},{1,0},{2,3},{3,2},{4,5},{5,4},{6,7},{7,6},{8,9},{9,8},{10,11... | collective-permute-start | bytes 73736 | tf_op jit(solution)/shard_map/ppermute | solution.py:508
  114.3 0.0 collective-permute-done.10.odd
  114.3 1.2 collective-permute-done.11.even
  115.5 0.3 shard_map.104
  115.7 16.3 %all_to_all.28 = f32[64,1,128]{2,1,0:T(1,128)S(1)} all-to-all(f32[64,1,128]{2,1,0:T(1,128)S(1)} %bitcast.25), channel_id=1, replica_groups=mesh['gx'=8,'gy'=64] {'gy'}, dimensions={0} | all-to-all | bytes 65536 | tf_op jit(solution)/shard_map/all_to_all | solution.py:518
  132.1 11.6 %all_to_all.29 = f32[8,1,128]{2,1,0:T(1,128)S(1)} all-to-all(f32[8,1,128]{2,1,0:T(1,128)S(1)} %bitcast.27), channel_id=1, replica_groups=mesh['gx'=8,'gy'=64] {'gx'}, dimensions={0} | all-to-all | bytes 8192 | tf_op jit(solution)/shard_map/all_to_all | solution.py:518
  143.7 0.8 shard_map.106
  (1 shorter events, 0.0 us)
Async XLA Ops:
  0.6 19.3 %copy-start = (f32[32,18432]{1,0:T(8,128)S(1)}, f32[32,18432]{1,0:T(8,128)}, u32[]{:S(2)}) copy-start(f32[32,18432]{1,0:T(8,128)} %refs_3_.3) | copy-start | bytes 7077892
  1.8 55.4 %copy-start.1 = (f32[32,16384]{1,0:T(8,128)S(1)}, f32[32,16384]{1,0:T(8,128)}, u32[]{:S(2)}) copy-start(f32[32,16384]{1,0:T(8,128)} %refs_2_.3) | copy-start | bytes 6291460
  1.8 7.4 %collective-permute-start = (f32[256,128]{1,0:T(8,128)S(1)}, f32[256,128]{1,0:T(8,128)S(1)}, u32[]{:S(2)}, u32[]{:S(2)}) collective-permute-start(f32[256,128]{1,0:T(8,128)S(1)} %get-tuple-element.36), channel_id=1, source_target_pairs={{64,128},{128,64},{192,256},{256,192},{320,384},{384,320},{65,129}... | collective-permute-start | bytes 393224 | tf_op jit(solution)/shard_map/ppermute | solution.py:509
  2.6 8.9 %collective-permute-start.1 = (f32[256,128]{1,0:T(8,128)S(1)}, f32[256,128]{1,0:T(8,128)S(1)}, u32[]{:S(2)}, u32[]{:S(2)}) collective-permute-start(f32[256,128]{1,0:T(8,128)S(1)} %get-tuple-element.37), channel_id=1, source_target_pairs={{0,64},{64,0},{128,192},{192,128},{256,320},{320,256},{384,448},{4... | collective-permute-start | bytes 393224 | tf_op jit(solution)/shard_map/ppermute | solution.py:508
  11.7 8.1 %collective-permute-start.2 = (f32[64,128]{1,0:T(8,128)S(1)}, f32[64,128]{1,0:T(8,128)S(1)}, u32[]{:S(2)}, u32[]{:S(2)}) collective-permute-start(f32[64,128]{1,0:T(8,128)S(1)} %get-tuple-element.39), channel_id=1, source_target_pairs={{1,2},{2,1},{3,4},{4,3},{5,6},{6,5},{7,8},{8,7},{9,10},{10,9},{11,... | collective-permute-start | bytes 98312 | tf_op jit(solution)/shard_map/ppermute | solution.py:509
  16.8 3.1 %collective-permute-start.3 = (f32[64,128]{1,0:T(8,128)S(1)}, f32[64,128]{1,0:T(8,128)S(1)}, u32[]{:S(2)}, u32[]{:S(2)}) collective-permute-start(f32[64,128]{1,0:T(8,128)S(1)} %get-tuple-element.40), channel_id=1, source_target_pairs={{0,1},{1,0},{2,3},{3,2},{4,5},{5,4},{6,7},{7,6},{8,9},{9,8},{10,11... | collective-permute-start | bytes 98312 | tf_op jit(solution)/shard_map/ppermute | solution.py:508
  57.7 4.2 %collective-permute-start.4 = (f32[32,384]{1,0:T(8,128)S(1)}, f32[32,384]{1,0:T(8,128)S(1)}, u32[]{:S(2)}, u32[]{:S(2)}) collective-permute-start(f32[32,384]{1,0:T(8,128)S(1)} %get-tuple-element.45), channel_id=1, source_target_pairs={{64,128},{128,64},{192,256},{256,192},{320,384},{384,320},{65,129}... | collective-permute-start | bytes 147464 | tf_op jit(solution)/shard_map/ppermute | solution.py:509
  58.4 5.0 %collective-permute-start.5 = (f32[32,384]{1,0:T(8,128)S(1)}, f32[32,384]{1,0:T(8,128)S(1)}, u32[]{:S(2)}, u32[]{:S(2)}) collective-permute-start(f32[32,384]{1,0:T(8,128)S(1)} %get-tuple-element.46), channel_id=1, source_target_pairs={{0,64},{64,0},{128,192},{192,128},{256,320},{320,256},{384,448},{4... | collective-permute-start | bytes 147464 | tf_op jit(solution)/shard_map/ppermute | solution.py:508
  63.5 7.1 %collective-permute-start.6 = (f32[64,128]{1,0:T(8,128)S(1)}, f32[64,128]{1,0:T(8,128)S(1)}, u32[]{:S(2)}, u32[]{:S(2)}) collective-permute-start(f32[64,128]{1,0:T(8,128)S(1)} %get-tuple-element.48), channel_id=1, source_target_pairs={{1,2},{2,1},{3,4},{4,3},{5,6},{6,5},{7,8},{8,7},{9,10},{10,9},{11,... | collective-permute-start | bytes 98312 | tf_op jit(solution)/shard_map/ppermute | solution.py:509
  68.6 3.1 %collective-permute-start.7 = (f32[64,128]{1,0:T(8,128)S(1)}, f32[64,128]{1,0:T(8,128)S(1)}, u32[]{:S(2)}, u32[]{:S(2)}) collective-permute-start(f32[64,128]{1,0:T(8,128)S(1)} %get-tuple-element.49), channel_id=1, source_target_pairs={{0,1},{1,0},{2,3},{3,2},{4,5},{5,4},{6,7},{7,6},{8,9},{9,8},{10,11... | collective-permute-start | bytes 98312 | tf_op jit(solution)/shard_map/ppermute | solution.py:508
  102.6 4.5 %collective-permute-start.8 = (f32[24,384]{1,0:T(8,128)S(1)}, f32[24,384]{1,0:T(8,128)S(1)}, u32[]{:S(2)}, u32[]{:S(2)}) collective-permute-start(f32[24,384]{1,0:T(8,128)S(1)} %get-tuple-element.57), channel_id=1, source_target_pairs={{64,128},{128,64},{192,256},{256,192},{320,384},{384,320},{65,129}... | collective-permute-start | bytes 110600 | tf_op jit(solution)/shard_map/ppermute | solution.py:509
  103.3 5.2 %collective-permute-start.9 = (f32[24,384]{1,0:T(8,128)S(1)}, f32[24,384]{1,0:T(8,128)S(1)}, u32[]{:S(2)}, u32[]{:S(2)}) collective-permute-start(f32[24,384]{1,0:T(8,128)S(1)} %get-tuple-element.58), channel_id=1, source_target_pairs={{0,64},{64,0},{128,192},{192,128},{256,320},{320,256},{384,448},{4... | collective-permute-start | bytes 110600 | tf_op jit(solution)/shard_map/ppermute | solution.py:508
  108.6 5.7 %collective-permute-start.10 = (f32[48,128]{1,0:T(8,128)S(1)}, f32[48,128]{1,0:T(8,128)S(1)}, u32[]{:S(2)}, u32[]{:S(2)}) collective-permute-start(f32[48,128]{1,0:T(8,128)S(1)} %get-tuple-element.60), channel_id=1, source_target_pairs={{1,2},{2,1},{3,4},{4,3},{5,6},{6,5},{7,8},{8,7},{9,10},{10,9},{11,... | collective-permute-start | bytes 73736 | tf_op jit(solution)/shard_map/ppermute | solution.py:509
  112.4 3.1 %collective-permute-start.11 = (f32[48,128]{1,0:T(8,128)S(1)}, f32[48,128]{1,0:T(8,128)S(1)}, u32[]{:S(2)}, u32[]{:S(2)}) collective-permute-start(f32[48,128]{1,0:T(8,128)S(1)} %get-tuple-element.61), channel_id=1, source_target_pairs={{0,1},{1,0},{2,3},{3,2},{4,5},{5,4},{6,7},{7,6},{8,9},{9,8},{10,11... | collective-permute-start | bytes 73736 | tf_op jit(solution)/shard_map/ppermute | solution.py:508
